TPU v7x, 256 devices: a whole 4x4x8 slice. The times are simulated.
256 devices in a mesh: dp: 32 (over y, x, core), tensor: 8 (over z).
Axes of the slice: x: 4, y: 4, z: 8, core: 2. Of those that a mesh axis runs over, the one named last changes fastest.
Arguments:
- tokens: bfloat16 [8192, 4096], P(('dp', 'tensor')), may hold values from -6 to 6
- grad_out: bfloat16 [8192, 16384], P('dp', 'tensor'), may hold values from -0.0625 to 0.0625
- owner: int32 [8, 128], P('tensor'), may hold values from 0 to 31, as said below
- left_factor: float32 [8, 160, 256, 256], P('tensor', 'dp'), may hold values from -0.15 to 2, as said below
- right_factor: float32 [8, 160, 256, 256], P('tensor', 'dp'), may hold values from -0.15 to 2, as said below
- left_basis: bfloat16 [8, 160, 256, 256], P('tensor', 'dp'), may hold values from -0.375 to 0.375
- right_basis: bfloat16 [8, 160, 256, 256], P('tensor', 'dp'), may hold values from -0.375 to 0.375
- first_moment: bfloat16 [8, 160, 256, 256], P('tensor', 'dp'), may hold values from -0.29882812 to 0.29882812
- second_moment: bfloat16 [8, 160, 256, 256], P('tensor', 'dp'), may hold values from 0.0049743652 to 0.049804688
Outputs:
- update: bfloat16 [8, 128, 256, 256], P('tensor', 'dp')
- left_factor_new: float32 [8, 160, 256, 256], P('tensor', 'dp')
- right_factor_new: float32 [8, 160, 256, 256], P('tensor', 'dp')
- first_moment_new: bfloat16 [8, 160, 256, 256], P('tensor', 'dp')
- second_moment_new: bfloat16 [8, 160, 256, 256], P('tensor', 'dp')
Inputs may be any that keep to these rules, and one draw needn't show every extreme that they name: For every t, each owner holds between 3 and 5 blocks, some owner exactly 5; among the blocks k with one value of k // 4, no owner holds more than 1, and some owner exactly 1. `left_factor`: each block is symmetric. `right_factor`: each block is symmetric.
All inputs are finite; a program needn't handle non-finite values.
Results may differ from a plain program's by a relative error of at most 0.035.
Values may be sent and summed in bfloat16 or wider, within the bound.
No kernel may reach another device: no remote copies, remote signals or barrier semaphores. Data moves between devices by JAX's collectives and lax.ppermute only.
A program may use at most 192 MiB of HBM per device.

v0:
```python
import jax
import jax.numpy as jnp
from jax import lax
from jax.sharding import PartitionSpec as P

BLOCK = 256
D = 4096


factor_decay = 0.9
first_decay = 0.95
second_decay = 0.95
epsilon_value = 1e-08


def rank_tables(owner_row, dp_count, home_count):
    columns = jnp.arange(dp_count, dtype=jnp.int32)
    onehot = (owner_row[:, None] == columns[None, :]).astype(jnp.int32)
    rank = jnp.sum((jnp.cumsum(onehot, axis=0) - onehot) * onehot, axis=1)
    per_home = onehot.reshape(dp_count, home_count, dp_count)
    within = jnp.sum((jnp.cumsum(per_home, axis=1) - per_home) * per_home, axis=2)
    return (rank, within.reshape(-1))


def flatten(array):
    return array.reshape(array.shape[0], -1)


def select_rows(selector, array, shape):
    moved = jnp.dot(selector, flatten(array), preferred_element_type=jnp.float32)
    return moved.astype(jnp.bfloat16).reshape(shape)


def local(
    tokens,
    grad_out,
    owner,
    left_factor,
    right_factor,
    left_basis,
    right_basis,
    first_moment,
    second_moment,
):
    dp_count = lax.axis_size("dp")
    my_index = lax.axis_index("dp")
    block_count = owner.shape[1]
    home_count = block_count // dp_count
    slot_count = left_factor.shape[1]
    pair_count = (slot_count + dp_count - 1) // dp_count
    buffer_count = dp_count * pair_count
    row_blocks = D // BLOCK
    owner_row = owner[0]
    rank, within = rank_tables(owner_row, dp_count, home_count)
    block_ids = jnp.arange(block_count, dtype=jnp.int32)
    arrival = block_ids // home_count * pair_count + within
    slot_ids = jnp.arange(slot_count, dtype=jnp.int32)
    mine = (owner_row == my_index)[None, :]
    holds = ((rank[None, :] == slot_ids[:, None]) & mine).astype(jnp.int32)
    live = jnp.sum(holds, axis=1) > 0
    slot_arrival = jnp.sum(holds * arrival[None, :], axis=1)
    buffer_ids = jnp.arange(buffer_count, dtype=jnp.int32)
    owner_pick = ((slot_arrival[:, None] == buffer_ids[None, :]) & live[:, None]).astype(
        jnp.bfloat16
    )
    home_owner = lax.dynamic_slice_in_dim(owner_row, my_index * home_count, home_count)
    home_within = lax.dynamic_slice_in_dim(within, my_index * home_count, home_count)
    departure = home_owner * pair_count + home_within
    home_pick = (buffer_ids[:, None] == departure[None, :]).astype(jnp.bfloat16)
    whole_x = lax.all_gather(tokens, "tensor", axis=0, tiled=True)
    contract = (((0,), (0,)), ((), ()))
    block_shape = (slot_count, BLOCK, BLOCK)
    columns_taken = home_count * lax.axis_size("dp") // row_blocks
    product = lax.dot_general(whole_x, grad_out, contract, preferred_element_type=jnp.float32)
    product = product.reshape(row_blocks, BLOCK, columns_taken, BLOCK).transpose(2, 0, 1, 3)
    home_grad = lax.psum_scatter(
        product.reshape(home_count * lax.axis_size("dp"), BLOCK, BLOCK).astype(jnp.bfloat16),
        "dp",
        scatter_dimension=0,
        tiled=True,
    )
    outgoing = select_rows(home_pick, home_grad, (dp_count, pair_count, BLOCK, BLOCK))
    arrived = lax.all_to_all(outgoing, "dp", split_axis=0, concat_axis=0, tiled=True)
    slot_grad = select_rows(owner_pick, arrived.reshape(buffer_count, BLOCK, BLOCK), block_shape)
    live_mask = live[:, None, None]
    left_old = left_factor[0]
    right_old = right_factor[0]
    basis_left = left_basis[0]
    basis_right = right_basis[0]
    gram_left = jnp.einsum("sik,sjk->sij", slot_grad, slot_grad, preferred_element_type=jnp.float32)
    gram_right = jnp.einsum(
        "ski,skj->sij", slot_grad, slot_grad, preferred_element_type=jnp.float32
    )
    left_new = jnp.where(
        live_mask, factor_decay * left_old + (1.0 - factor_decay) / BLOCK * gram_left, left_old
    )
    right_new = jnp.where(
        live_mask, factor_decay * right_old + (1.0 - factor_decay) / BLOCK * gram_right, right_old
    )
    halfway = jnp.einsum(
        "ski,skj->sij", basis_left, slot_grad, preferred_element_type=jnp.float32
    ).astype(jnp.bfloat16)
    rotated = jnp.einsum("sik,skj->sij", halfway, basis_right, preferred_element_type=jnp.float32)
    first_new = first_decay * first_moment[0].astype(jnp.float32) + (1.0 - first_decay) * rotated
    second_new = (
        second_decay * second_moment[0].astype(jnp.float32)
        + (1.0 - second_decay) * rotated * rotated
    )
    ratio = (first_new / (jnp.sqrt(second_new) + epsilon_value)).astype(jnp.bfloat16)
    turned = jnp.einsum(
        "sik,skj->sij", basis_left, ratio, preferred_element_type=jnp.float32
    ).astype(jnp.bfloat16)
    update = jnp.einsum(
        "sik,sjk->sij", turned, basis_right, preferred_element_type=jnp.float32
    ).astype(jnp.bfloat16)
    backward = select_rows(owner_pick.T, update, (dp_count, pair_count, BLOCK, BLOCK))
    returned = lax.all_to_all(backward, "dp", split_axis=0, concat_axis=0, tiled=True)
    home_update = select_rows(
        home_pick.T, returned.reshape(buffer_count, BLOCK, BLOCK), (1, home_count, BLOCK, BLOCK)
    )
    first_out = jnp.where(live_mask, first_new.astype(jnp.bfloat16), first_moment[0])
    second_out = jnp.where(live_mask, second_new.astype(jnp.bfloat16), second_moment[0])
    return (home_update, left_new[None], right_new[None], first_out[None], second_out[None])


def solution(mesh):
    placed = (
        P(("dp", "tensor"), None),
        P("dp", "tensor"),
        P("tensor", None),
        P("tensor", "dp", None, None),
        P("tensor", "dp", None, None),
        P("tensor", "dp", None, None),
        P("tensor", "dp", None, None),
        P("tensor", "dp", None, None),
        P("tensor", "dp", None, None),
    )
    return jax.shard_map(
        local,
        mesh=mesh,
        in_specs=placed,
        out_specs=(
            P("tensor", "dp", None, None),
            P("tensor", "dp", None, None),
            P("tensor", "dp", None, None),
            P("tensor", "dp", None, None),
            P("tensor", "dp", None, None),
        ),
        check_vma=False,
    )
```

profile of v0, /device:TPU:97, one launch (start us, length us, event | category | flops | bytes accessed | tf_op | source)
XLA Modules:
  0.0 352.7 jit_solution(16497659386238510013)
XLA Ops:
  7.2 0.0 copy-start
  7.2 0.0 all-gather.2.cloned.1.call-start
  7.2 0.7 all-gather.2.cloned.1.call-update
  7.9 0.0 reduce-scatter.2.cloned.1.call-start
  8.0 39.7 %all-gather.2.cloned.1.call-done = bf16[256,4096]{1,0:T(8,128)(2,1)} async-done(((bf16[32,4096]{1,0:T(8,128)(2,1)}), bf16[256,4096]{1,0:T(8,128)(2,1)}) %all-gather.2.cloned.1.call-update) | async-done | bytes 2097168 | tf_op jit(solution)/shard_map/all_gather | solution.py:70
  47.7 0.0 copy-done
  47.7 9.8 %convolution_convert_fusion.4 = bf16[4096,2048]{1,0:T(8,128)(2,1)} fusion(bf16[256,4096]{1,0:T(8,128)(2,1)} %all-gather.2.cloned.1.call-done, bf16[256,2048]{1,0:T(8,128)(2,1)S(1)} %copy-done), kind=kOutput, calls=%fused_computation.4 | convolution fusion | flops 4303355904 | bytes 19922944 | tf_op jit(solution)/shard_map/dot_general | solution.py:74
  57.5 10.8 %copy.40 = bf16[512,8,8,256]{3,2,1,0:T(8,128)(2,1)S(1)} copy(bf16[512,8,8,256]{3,1,2,0:T(8,128)(2,1)} %bitcast.94) | data formatting | bytes 33554432
  68.3 9.7 %copy.27 = bf16[16,256,8,256]{3,1,0,2:T(8,128)(2,1)} copy(bf16[16,256,8,256]{3,2,1,0:T(8,128)(2,1)S(1)} %bitcast.96) | data formatting | bytes 33554432 | tf_op jit(solution)/shard_map/convert_element_type | solution.py:77
  78.0 0.0 copy-start.6
  78.0 0.0 reduce-scatter.2.cloned.1.call-update
  78.0 0.5 broadcast.99
  78.5 0.1 copy-done.6
  78.7 0.7 reduce.3
  79.3 0.1 eq.71
  79.4 0.1 copy.25
  79.5 0.3 fusion.50
  79.8 0.1 copy.26
  79.9 0.1 reshape.73
  80.0 0.1 bitcast_add_fusion
  80.1 123.2 %reduce-scatter.2.cloned.1.call-done = bf16[4,256,256]{2,1,0:T(8,128)(2,1)} async-done(((bf16[128,256,256]{2,1,0:T(8,128)(2,1)}), bf16[4,256,256]{2,1,0:T(8,128)(2,1)}) %reduce-scatter.2.cloned.1.call-update) | async-done | bytes 524304 | tf_op jit(solution)/shard_map/reduce_scatter | solution.py:76
  203.3 1.4 copy.41
  204.7 1.2 convolution_convert_fusion.1
  205.9 3.0 copy.42
  208.9 7.1 %all-to-all-start = ((bf16[32,1,256,256]{3,2,1,0:T(8,128)(2,1)}), bf16[32,1,256,256]{3,2,1,0:T(8,128)(2,1)}, u32[]{:S(2)}, u32[]{:S(2)}) async-start(bf16[32,1,256,256]{3,2,1,0:T(8,128)(2,1)} %bitcast.97), calls=%async_computation.1 | async-start | bytes 8388608 | tf_op jit(solution)/shard_map/all_to_all | solution.py:83
  216.0 0.1 fusion.30
  216.1 0.2 reduce_window_sum.23
  216.3 0.2 select_reduce_fusion
  216.5 0.1 convert_reduce_fusion
  216.6 49.5 %all-to-all-done = bf16[32,1,256,256]{3,2,1,0:T(8,128)(2,1)} async-done(((bf16[32,1,256,256]{3,2,1,0:T(8,128)(2,1)}), bf16[32,1,256,256]{3,2,1,0:T(8,128)(2,1)}, u32[]{:S(2)}, u32[]{:S(2)}) %all-to-all-start) | async-done | bytes 4194336 | tf_op jit(solution)/shard_map/all_to_all | solution.py:83
  266.2 4.6 %copy.43 = bf16[4,8,256,256]{3,1,2,0:T(8,128)(2,1)S(1)} copy(bf16[4,8,256,256]{3,2,1,0:T(8,128)(2,1)} %bitcast.28) | data formatting | bytes 8388608
  270.8 0.0 copy-start.3
  270.8 0.7 convolution_convert_fusion.2
  271.5 0.4 copy-done.3
  271.9 1.7 fusion.8
  273.6 2.9 fusion.7
  276.5 0.4 copy.45
  276.9 1.4 convolution_convert_fusion
  278.3 3.0 copy.46
  281.3 8.1 %all-to-all-start.1 = ((bf16[32,1,256,256]{3,2,1,0:T(8,128)(2,1)}), bf16[32,1,256,256]{3,2,1,0:T(8,128)(2,1)}, u32[]{:S(2)}, u32[]{:S(2)}) async-start(bf16[32,1,256,256]{3,2,1,0:T(8,128)(2,1)} %bitcast.98), calls=%async_computation.2 | async-start | bytes 8388608 | tf_op jit(solution)/shard_map/all_to_all | solution.py:117
  289.4 0.0 copy-start.2
  289.4 3.0 fusion.2
  292.3 0.0 copy-done.2
  292.4 0.0 copy-start.4
  292.4 0.0 copy-start.5
  292.4 1.5 fusion.5
  293.9 0.0 copy-done.4
  293.9 0.0 copy-done.5
  293.9 1.6 fusion.14
  295.5 44.1 %all-to-all-done.1 = bf16[32,1,256,256]{3,2,1,0:T(8,128)(2,1)} async-done(((bf16[32,1,256,256]{3,2,1,0:T(8,128)(2,1)}), bf16[32,1,256,256]{3,2,1,0:T(8,128)(2,1)}, u32[]{:S(2)}, u32[]{:S(2)}) %all-to-all-start.1) | async-done | bytes 4194336 | tf_op jit(solution)/shard_map/all_to_all | solution.py:117
  339.6 4.6 %copy.47 = bf16[4,8,256,256]{3,1,2,0:T(8,128)(2,1)S(1)} copy(bf16[4,8,256,256]{3,2,1,0:T(8,128)(2,1)} %bitcast.39) | data formatting | bytes 8388608
  344.2 0.0 copy-start.1
  344.2 0.7 convolution_convert_fusion.3
  344.9 0.9 copy.63
  345.8 0.0 copy-done.1
  (3 shorter events, 0.0 us)
Async XLA Ops:
  7.2 40.5 %copy-start = (bf16[256,2048]{1,0:T(8,128)(2,1)S(1)}, bf16[256,2048]{1,0:T(8,128)(2,1)}, u32[]{:S(2)}) copy-start(bf16[256,2048]{1,0:T(8,128)(2,1)} %param.10) | copy-start | bytes 3145732
  7.2 40.5 %all-gather.2.cloned.1.call-start = ((), (), s32[]{:S(2)}) async-start(), calls=%async_computation.3 | async-start | bytes 2359296 | tf_op jit(solution)/shard_map/all_gather | solution.py:70
  7.9 195.3 %reduce-scatter.2.cloned.1.call-start = ((), (), s32[]{:S(2)}) async-start(), calls=%async_computation.4 | async-start | bytes 17301504 | tf_op jit(solution)/shard_map/reduce_scatter | solution.py:76
  78.0 0.7 copy-start.6
  208.9 57.3 %all-to-all-start = ((bf16[32,1,256,256]{3,2,1,0:T(8,128)(2,1)}), bf16[32,1,256,256]{3,2,1,0:T(8,128)(2,1)}, u32[]{:S(2)}, u32[]{:S(2)}) async-start(bf16[32,1,256,256]{3,2,1,0:T(8,128)(2,1)} %bitcast.97), calls=%async_computation.1 | async-start | bytes 8388608 | tf_op jit(solution)/shard_map/all_to_all | solution.py:83
  270.8 1.1 copy-start.3
  281.3 58.3 %all-to-all-start.1 = ((bf16[32,1,256,256]{3,2,1,0:T(8,128)(2,1)}), bf16[32,1,256,256]{3,2,1,0:T(8,128)(2,1)}, u32[]{:S(2)}, u32[]{:S(2)}) async-start(bf16[32,1,256,256]{3,2,1,0:T(8,128)(2,1)} %bitcast.98), calls=%async_computation.2 | async-start | bytes 8388608 | tf_op jit(solution)/shard_map/all_to_all | solution.py:117
  289.4 3.0 copy-start.2
  292.4 1.5 copy-start.4
  292.4 1.5 copy-start.5
  344.2 1.6 copy-start.1
Sparse Core Ops, SparseCore 0:
  9.8 37.8 all-gather.1
  78.1 125.0 reduce-scatter.1
where the time goes:
time: 357 us; the launch traced here: 353 us
  waiting for transfers between devices  257 us (72%)
  local copies, waits for them, and re-layouts  39.7 us (11%)
  matrix products  23 us (6%)
  starting transfers between devices  15.3 us (4%)
  between operations  14.2 us (4%)
    reduce_scatter x1, waiting for transfers between devices, local(): lax.psum_scatter(product.reshape(home_count * lax.axis_size('dp'), BLOCK,...  123 us
    all_to_all x1, waiting for transfers between devices, local(): lax.all_to_all(outgoing, 'dp', split_axis=0, concat_axis=0, tiled=True)  49.5 us
    all_to_all x1, waiting for transfers between devices, local(): lax.all_to_all(backward, 'dp', split_axis=0, concat_axis=0, tiled=True)  44.1 us
    all_gather x1, waiting for transfers between devices, local(): whole_x = lax.all_gather(tokens, 'tensor', axis=0, tiled=True)  39.7 us
    unnamed x23, local copies, waits for them, and re-layouts  29.6 us
    dot_general x1, matrix products, local(): lax.dot_general(whole_x, grad_out, contract, preferred_element_type=jnp.f...  9.77 us
    convert_element_type x1, local copies, waits for them, and re-layouts, local(): product.reshape(home_count * lax.axis_size('dp'), BLOCK, BLOCK)  9.73 us
    all_to_all x1, starting transfers between devices, local(): lax.all_to_all(backward, 'dp', split_axis=0, concat_axis=0, tiled=True)  8.07 us
  transfers between devices with their start and end apart: 4, of which 4 were waited for; matrix products, arithmetic and copies ran while one was open for 2% of the time, Pallas kernels for 0%

commit v1 on v0

v1 whole, which is shorter than its diff:
```python
import functools

import jax
import jax.numpy as jnp
from jax import lax
from jax.experimental import pallas as pl
from jax.experimental.pallas import tpu as pltpu
from jax.sharding import Mesh
from jax.sharding import PartitionSpec as P

BLOCK = 256
TILE_ROWS = 16
TILE_COLS = 128
Y, X, CORE = 4, 4, 2
N_DP = Y * X * CORE
N_TENSOR = 8
ROW = X * CORE
SLOTS = 5
HOME = 4
NBLK = 128
ROW_BLOCKS = 16
COL_BLOCKS = 8
LOCAL_ROWS = ROW_BLOCKS // ROW
LOCAL_BLOCKS = LOCAL_ROWS * COL_BLOCKS
TOK_SUB = 32
DP = ("y", "x", "core")
ROW_AXES = ("x", "core")

factor_decay = 0.9
first_decay = 0.95
second_decay = 0.95
epsilon_value = 1e-08

PARAMS = pltpu.CompilerParams(vmem_limit_bytes=40 * 1024 * 1024)


def tile_of(m):
    return (
        slice(TILE_ROWS * (m // 2), TILE_ROWS * (m // 2 + 1)),
        slice(TILE_COLS * (m % 2), TILE_COLS * (m % 2 + 1)),
    )


def gradient_kernel(order, *refs):
    whole, halves, grads, out = refs[:7], refs[7:9], refs[9], refs[10]
    total = None
    for j in range(N_TENSOR):
        if j < 7:
            left = whole[j][...]
        else:
            left = jnp.concatenate([halves[0][...], halves[1][...]], axis=1)
        right = grads[:, order[j]].reshape(ROW * TOK_SUB, BLOCK)
        term = jnp.dot(left, right, preferred_element_type=jnp.float32)
        total = term if total is None else total + term
    result = total.astype(jnp.bfloat16)
    for rr in range(LOCAL_ROWS):
        block = result[rr * BLOCK : (rr + 1) * BLOCK]
        for m in range(N_DP):
            rows, cols = tile_of(m)
            out[m, rr] = block[rows, cols]


def gradient_tiles(order, whole, halves, grads):
    resident = lambda a: pl.BlockSpec(a.shape, lambda c, order: (0, 0))
    return pl.pallas_call(
        gradient_kernel,
        grid_spec=pltpu.PrefetchScalarGridSpec(
            num_scalar_prefetch=1,
            grid=(COL_BLOCKS,),
            in_specs=[resident(a) for a in (*whole, *halves)]
            + [
                pl.BlockSpec(
                    (ROW, N_TENSOR, TOK_SUB, BLOCK), lambda c, order: (0, 0, 0, c)
                )
            ],
            out_specs=pl.BlockSpec(
                (N_DP, LOCAL_ROWS, TILE_ROWS, TILE_COLS), lambda c, order: (0, c, 0, 0)
            ),
        ),
        out_shape=jax.ShapeDtypeStruct(
            (N_DP, LOCAL_BLOCKS, TILE_ROWS, TILE_COLS), jnp.bfloat16
        ),
        compiler_params=PARAMS,
        name="gradient_tiles",
    )(order, *whole, *halves, grads)


def to_slots_kernel(slot, parts, out):
    out[...] = jnp.zeros_like(out)

    def body(k, carry):
        c, r = k // ROW_BLOCKS, k % ROW_BLOCKS
        source, place = r // LOCAL_ROWS, c * LOCAL_ROWS + r % LOCAL_ROWS
        total = parts[source, place].astype(jnp.float32)
        for y in range(1, Y):
            total = total + parts[y * ROW + source, place].astype(jnp.float32)
        out[slot[k]] = total.astype(jnp.bfloat16)
        return carry

    lax.fori_loop(0, NBLK, body, 0, unroll=4)


def to_slots(slot, parts):
    return pl.pallas_call(
        to_slots_kernel,
        grid_spec=pltpu.PrefetchScalarGridSpec(
            num_scalar_prefetch=1,
            grid=(1,),
            in_specs=[pl.BlockSpec(parts.shape, lambda i, slot: (0, 0, 0, 0))],
            out_specs=pl.BlockSpec(
                (N_DP * SLOTS, TILE_ROWS, TILE_COLS), lambda i, slot: (0, 0, 0)
            ),
        ),
        out_shape=jax.ShapeDtypeStruct((N_DP * SLOTS, TILE_ROWS, TILE_COLS), jnp.bfloat16),
        compiler_params=PARAMS,
        name="to_slots",
    )(slot, parts)


def from_slots_kernel(slot, tiles, out):
    def body(k, carry):
        out[k] = tiles[slot[k]]
        return carry

    lax.fori_loop(0, NBLK, body, 0, unroll=8)


def from_slots(slot, tiles):
    return pl.pallas_call(
        from_slots_kernel,
        grid_spec=pltpu.PrefetchScalarGridSpec(
            num_scalar_prefetch=1,
            grid=(1,),
            in_specs=[pl.BlockSpec(tiles.shape, lambda i, slot: (0, 0, 0))],
            out_specs=pl.BlockSpec((NBLK, TILE_ROWS, TILE_COLS), lambda i, slot: (0, 0, 0)),
        ),
        out_shape=jax.ShapeDtypeStruct((NBLK, TILE_ROWS, TILE_COLS), jnp.bfloat16),
        compiler_params=PARAMS,
        name="from_slots",
    )(slot, tiles)


def assemble_kernel(tiles, out):
    for h in range(HOME):
        for m in range(N_DP):
            rows, cols = tile_of(m)
            out[0, h, rows, cols] = tiles[m, h]


def assemble(tiles):
    return pl.pallas_call(
        assemble_kernel,
        out_shape=jax.ShapeDtypeStruct((1, HOME, BLOCK, BLOCK), jnp.bfloat16),
        compiler_params=PARAMS,
        name="assemble",
    )(tiles)


def dot(a, b, ca, cb):
    return lax.dot_general(a, b, (((ca,), (cb,)), ((), ())), preferred_element_type=jnp.float32)


def soap_kernel(
    live, tiles, left, right, basis_left, basis_right, first, second,
    update, left_new, right_new, first_new, second_new, gradient,
):
    alive = live[pl.program_id(0)] > 0
    for m in range(N_DP):
        rows, cols = tile_of(m)
        gradient[rows, cols] = tiles[m, 0]
    grad = gradient[...]
    ql, qr = basis_left[0, 0], basis_right[0, 0]
    halfway = dot(ql, grad, 0, 0).astype(jnp.bfloat16)
    rotated = dot(halfway, qr, 1, 0)
    first_old, second_old = first[0, 0], second[0, 0]
    first_float = first_decay * first_old.astype(jnp.float32) + (1.0 - first_decay) * rotated
    second_float = (
        second_decay * second_old.astype(jnp.float32)
        + (1.0 - second_decay) * rotated * rotated
    )
    ratio = (first_float / (jnp.sqrt(second_float) + epsilon_value)).astype(jnp.bfloat16)
    turned = dot(ql, ratio, 1, 0).astype(jnp.bfloat16)
    result = dot(turned, qr, 1, 1).astype(jnp.bfloat16)
    for m in range(N_DP):
        rows, cols = tile_of(m)
        update[m, 0] = result[rows, cols]
    first_new[0, 0] = jnp.where(alive, first_float.astype(jnp.bfloat16), first_old)
    second_new[0, 0] = jnp.where(alive, second_float.astype(jnp.bfloat16), second_old)
    scale = (1.0 - factor_decay) / BLOCK
    left_old, right_old = left[0, 0], right[0, 0]
    left_new[0, 0] = jnp.where(
        alive, factor_decay * left_old + scale * dot(grad, grad, 1, 1), left_old
    )
    right_new[0, 0] = jnp.where(
        alive, factor_decay * right_old + scale * dot(grad, grad, 0, 0), right_old
    )


def soap(live, tiles, left, right, basis_left, basis_right, first, second):
    state = pl.BlockSpec((1, 1, BLOCK, BLOCK), lambda s, live: (0, s, 0, 0))
    pieces = pl.BlockSpec((N_DP, 1, TILE_ROWS, TILE_COLS), lambda s, live: (0, s, 0, 0))
    like = lambda a: jax.ShapeDtypeStruct(a.shape, a.dtype)
    return pl.pallas_call(
        soap_kernel,
        grid_spec=pltpu.PrefetchScalarGridSpec(
            num_scalar_prefetch=1,
            grid=(SLOTS,),
            in_specs=[pieces] + [state] * 6,
            out_specs=[pieces] + [state] * 4,
            scratch_shapes=[pltpu.VMEM((BLOCK, BLOCK), jnp.bfloat16)],
        ),
        out_shape=[like(tiles), like(left), like(right), like(first), like(second)],
        compiler_params=PARAMS,
        name="soap",
    )(live, tiles, left, right, basis_left, basis_right, first, second)


def spread(array, axes):
    return lax.all_to_all(array, axes, split_axis=0, concat_axis=0, tiled=True)


def ring_tokens(mine):
    up = [(i, (i + 1) % N_TENSOR) for i in range(N_TENSOR)]
    down = [(i, (i - 1) % N_TENSOR) for i in range(N_TENSOR)]
    from_below, from_above = mine, mine
    whole = [mine]
    for _ in range(N_TENSOR // 2 - 1):
        from_below = lax.ppermute(from_below, "z", up)
        from_above = lax.ppermute(from_above, "z", down)
        whole += [from_below, from_above]
    half = mine.shape[1] // 2
    halves = [
        lax.ppermute(from_below[:, :half], "z", up),
        lax.ppermute(from_above[:, half:], "z", down),
    ]
    place = lax.axis_index("z")
    steps = jnp.array([0, -1, 1, -2, 2, -3, 3, 4], jnp.int32)
    order = (place + steps + N_TENSOR) % N_TENSOR
    return order, whole, halves


def local(
    tokens, grad_out, owner, left_factor, right_factor,
    left_basis, right_basis, first_moment, second_moment,
):
    owner_row = owner[0]
    block_ids = jnp.arange(NBLK, dtype=jnp.int32)
    same = owner_row[:, None] == owner_row[None, :]
    before = block_ids[None, :] < block_ids[:, None]
    rank = jnp.sum((same & before).astype(jnp.int32), axis=1)
    slot = owner_row * SLOTS + rank
    held = jnp.sum((owner_row == lax.axis_index(DP)).astype(jnp.int32))
    live = (jnp.arange(SLOTS, dtype=jnp.int32) < held).astype(jnp.int32)

    grads = lax.all_gather(grad_out, ROW_AXES, axis=0, tiled=True)
    grads = grads.reshape(ROW, N_TENSOR, TOK_SUB, grad_out.shape[1])
    width = tokens.shape[1] // ROW
    cut = tokens.reshape(TOK_SUB, ROW, width).transpose(1, 0, 2)
    mine = spread(cut, ROW_AXES).transpose(2, 0, 1).reshape(width, ROW * TOK_SUB)
    order, whole, halves = ring_tokens(mine)
    partial = gradient_tiles(order, whole, halves, grads)
    tiles = to_slots(slot, spread(partial, DP))
    tiles = tiles.reshape(N_DP, SLOTS, TILE_ROWS, TILE_COLS)
    update, left_new, right_new, first_new, second_new = soap(
        live, spread(tiles, DP), left_factor, right_factor,
        left_basis, right_basis, first_moment, second_moment,
    )
    back = spread(update, DP).reshape(N_DP * SLOTS, TILE_ROWS, TILE_COLS)
    picked = from_slots(slot, back).reshape(N_DP, HOME, TILE_ROWS, TILE_COLS)
    home_update = assemble(spread(picked, DP))
    return (home_update, left_new, right_new, first_new, second_new)


def solution(mesh):
    split = Mesh(mesh.devices.reshape(Y, X, CORE, N_TENSOR), ("y", "x", "core", "z"))
    state = P("z", DP, None, None)
    return jax.shard_map(
        local,
        mesh=split,
        in_specs=(P((*DP, "z"), None), P(DP, "z"), P("z", None)) + (state,) * 6,
        out_specs=(state,) * 5,
        check_vma=False,
    )
```

time: 357 us -> 186 us (0.52)
  waiting for transfers between devices: 257 us -> 70.4 us
  blocking collectives: 0 us -> 42.8 us
  local copies, waits for them, and re-layouts: 39.7 us -> 9.02 us
  matrix products: 23 us -> 0 us
  Pallas kernels: 0 us -> 19.3 us
  starting transfers between devices: 15.3 us -> 25.8 us
    reduce_scatter x1 -> x0, waiting for transfers between devices: 123 us -> none  [local(): lax.psum_scatter(product.reshape(home_count * lax.axis_size('dp'), BLOCK,...]
    all_to_all x2, waiting for transfers between devices: 93.6 us -> 39.4 us  [spread(): return lax.all_to_all(array, axes, split_axis=0, concat_axis=0, tiled=True)]
    all_to_all x0 -> x3, blocking collectives: none -> 42.8 us  [spread(): return lax.all_to_all(array, axes, split_axis=0, concat_axis=0, tiled=True)]
    all_gather x1, waiting for transfers between devices: 39.7 us -> 13.5 us  [local(): grads = lax.all_gather(grad_out, ROW_AXES, axis=0, tiled=True)]
    dot_general x9 -> x0, matrix products: 23 us -> none  [the longest x1 9.77 us: local(): lax.dot_general(whole_x, grad_out, contract, preferred_element_type=jnp.f...]
    unnamed x23 -> x19, local copies, waits for them, and re-layouts: 29.6 us -> 8.79 us
    pallas_call x0 -> x5, Pallas kernels: none -> 19.3 us  [the longest x1 8.39 us: gradient_tiles(): pl.pallas_call(gradient_kernel, grid_spec=pltpu.PrefetchScalarGridSpec(nu...]
    ppermute x0 -> x8, waiting for transfers between devices: none -> 16.9 us  [the longest x3 11.5 us: ring_tokens(): from_below = lax.ppermute(from_below, 'z', up)]
  transfers between devices with their start and end apart: 4 -> 11, of which waited for: 4 -> 8; matrix products, arithmetic and copies ran while one was open for 2% -> 2% of each run, Pallas kernels for 0% -> 0%
where the time goes in v1:
time: 186 us; the launch traced here: 183 us
  waiting for transfers between devices  70.4 us (38%)
  blocking collectives  42.8 us (23%)
  starting transfers between devices  25.8 us (14%)
  Pallas kernels  19.3 us (10%)
  between operations  14.2 us (8%)
  local copies, waits for them, and re-layouts  9.02 us (5%)
    all_to_all x3, blocking collectives, spread(): return lax.all_to_all(array, axes, split_axis=0, concat_axis=0, tiled=True)  42.8 us
    all_to_all x2, waiting for transfers between devices, spread(): return lax.all_to_all(array, axes, split_axis=0, concat_axis=0, tiled=True)  39.4 us
    all_gather x1, waiting for transfers between devices, local(): grads = lax.all_gather(grad_out, ROW_AXES, axis=0, tiled=True)  13.5 us
    all_to_all x2, starting transfers between devices, spread(): return lax.all_to_all(array, axes, split_axis=0, concat_axis=0, tiled=True)  12.2 us
    ppermute x3, waiting for transfers between devices, ring_tokens(): from_below = lax.ppermute(from_below, 'z', up)  11.5 us
    ppermute x3, starting transfers between devices, ring_tokens(): from_below = lax.ppermute(from_below, 'z', up)  9.85 us
    unnamed x19, local copies, waits for them, and re-layouts  8.79 us
    pallas_call x1, Pallas kernels, gradient_tiles(): pl.pallas_call(gradient_kernel, grid_spec=pltpu.PrefetchScalarGridSpec(nu...  8.39 us
  transfers between devices with their start and end apart: 11, of which 8 were waited for; matrix products, arithmetic and copies ran while one was open for 2% of the time, Pallas kernels for 0%

profile of v1, /device:TPU:97, one launch (start us, length us, event | category | flops | bytes accessed | tf_op | source)
XLA Modules:
  0.0 183.0 jit_solution(5246338303600340566)
XLA Ops:
  7.2 0.0 all-gather.2.cloned.1.call-start
  7.2 0.7 all-gather.2.cloned.1.call-update
  7.9 0.0 copy-start.8
  7.9 1.0 copy.31
  9.0 0.1 copy.27
  9.0 11.3 %all_to_all.25 = bf16[8,32,512]{2,1,0:T(8,128)(2,1)S(1)} all-to-all(bf16[8,32,512]{2,1,0:T(8,128)(2,1)S(1)} %copy.27), channel_id=1, replica_groups=mesh['y'=4,'x'=4,'core'=2,'z'=8] {'x','core'}, dimensions={0} | all-to-all | bytes 524288 | tf_op jit(solution)/shard_map/all_to_all | solution.py:219
  20.3 0.1 copy.30.refs_0_
  20.5 2.9 %collective-permute-start = (bf16[512,256]{1,0:T(8,128)(2,1)S(1)}, bf16[512,256]{1,0:T(8,128)(2,1)S(1)}, u32[]{:S(2)}, u32[]{:S(2)}) collective-permute-start(bf16[512,256]{1,0:T(8,128)(2,1)S(1)} %copy.30.refs_0_), channel_id=1, source_target_pairs={{0,1},{1,2},{2,3},{3,4},{4,5},{5,6},{6,7},{7,0},{8,9},{9,10},{10,1... | collective-permute-start | bytes 786440 | tf_op jit(solution)/shard_map/ppermute | solution.py:228
  23.4 0.0 collective-permute-start.1
  23.4 4.6 %collective-permute-done.refs_1_ = bf16[512,256]{1,0:T(8,128)(2,1)S(1)} collective-permute-done((bf16[512,256]{1,0:T(8,128)(2,1)S(1)}, bf16[512,256]{1,0:T(8,128)(2,1)S(1)}, u32[]{:S(2)}, u32[]{:S(2)}) %collective-permute-start) | collective-permute-done | bytes 262176 | tf_op jit(solution)/shard_map/ppermute | solution.py:228
  27.9 3.4 %collective-permute-start.2 = (bf16[512,256]{1,0:T(8,128)(2,1)S(1)}, bf16[512,256]{1,0:T(8,128)(2,1)S(1)}, u32[]{:S(2)}, u32[]{:S(2)}) collective-permute-start(bf16[512,256]{1,0:T(8,128)(2,1)S(1)} %collective-permute-done.refs_1_), channel_id=1, source_target_pairs={{0,1},{1,2},{2,3},{3,4},{4,5},{5,6},{6,7},{7,0},{8,9},{9,10},{10,1... | collective-permute-start | bytes 786440 | tf_op jit(solution)/shard_map/ppermute | solution.py:228
  31.3 0.0 collective-permute-done.1.refs_2_
  31.3 0.0 collective-permute-start.3
  31.4 3.6 %collective-permute-done.2.refs_3_ = bf16[512,256]{1,0:T(8,128)(2,1)S(1)} collective-permute-done((bf16[512,256]{1,0:T(8,128)(2,1)S(1)}, bf16[512,256]{1,0:T(8,128)(2,1)S(1)}, u32[]{:S(2)}, u32[]{:S(2)}) %collective-permute-start.2) | collective-permute-done | bytes 262176 | tf_op jit(solution)/shard_map/ppermute | solution.py:228
  35.0 3.5 %collective-permute-start.4 = (bf16[512,256]{1,0:T(8,128)(2,1)S(1)}, bf16[512,256]{1,0:T(8,128)(2,1)S(1)}, u32[]{:S(2)}, u32[]{:S(2)}) collective-permute-start(bf16[512,256]{1,0:T(8,128)(2,1)S(1)} %collective-permute-done.2.refs_3_), channel_id=1, source_target_pairs={{0,1},{1,2},{2,3},{3,4},{4,5},{5,6},{6,7},{7,0},{8,9},{9,10},{10,1... | collective-permute-start | bytes 786440 | tf_op jit(solution)/shard_map/ppermute | solution.py:228
  38.5 0.0 collective-permute-done.3.refs_4_
  38.5 0.0 collective-permute-start.5
  38.5 3.3 %collective-permute-done.4.refs_5_ = bf16[512,256]{1,0:T(8,128)(2,1)S(1)} collective-permute-done((bf16[512,256]{1,0:T(8,128)(2,1)S(1)}, bf16[512,256]{1,0:T(8,128)(2,1)S(1)}, u32[]{:S(2)}, u32[]{:S(2)}) %collective-permute-start.4) | collective-permute-done | bytes 262176 | tf_op jit(solution)/shard_map/ppermute | solution.py:228
  41.8 3.6 %collective-permute-start.6 = (bf16[512,128]{1,0:T(8,128)(2,1)S(1)}, bf16[512,128]{1,0:T(8,128)(2,1)S(1)}, u32[]{:S(2)}, u32[]{:S(2)}) collective-permute-start(bf16[512,128]{1,0:T(8,128)(2,1)S(1)} %slice.8), channel_id=1, source_target_pairs={{0,1},{1,2},{2,3},{3,4},{4,5},{5,6},{6,7},{7,0},{8,9},{9,10},{10,1... | collective-permute-start | bytes 393224 | tf_op jit(solution)/shard_map/ppermute | solution.py:233
  45.4 0.0 collective-permute-done.5.refs_6_
  45.4 0.1 collective-permute-start.7
  45.5 0.0 copy-done.8
  45.6 1.8 collective-permute-done.6.refs_7_
  47.4 3.6 %collective-permute-done.7.refs_8_ = bf16[512,128]{1,0:T(8,128)(2,1)S(1)} collective-permute-done((bf16[512,128]{1,0:T(8,128)(2,1)S(1)}, bf16[512,128]{1,0:T(8,128)(2,1)S(1)}, u32[]{:S(2)}, u32[]{:S(2)}) %collective-permute-start.7) | collective-permute-done | bytes 131104 | tf_op jit(solution)/shard_map/ppermute | solution.py:234
  50.9 13.5 %all-gather.2.cloned.1.call-done = bf16[2048,2048]{1,0:T(8,128)(2,1)} async-done(((bf16[256,2048]{1,0:T(8,128)(2,1)}), bf16[2048,2048]{1,0:T(8,128)(2,1)}) %all-gather.2.cloned.1.call-update) | async-done | bytes 8388624 | tf_op jit(solution)/shard_map/all_gather | solution.py:255
  64.4 0.0 copy-start
  64.4 3.4 %copy-done = bf16[2048,2048]{1,0:T(8,128)(2,1)S(1)} copy-done((bf16[2048,2048]{1,0:T(8,128)(2,1)S(1)}, bf16[2048,2048]{1,0:T(8,128)(2,1)}, u32[]{:S(2)}) %copy-start) | copy-done | bytes 8388632
  67.8 8.4 %gradient_tiles.1 = bf16[32,16,16,128]{3,2,1,0:T(8,128)(2,1)} custom-call(s32[8]{0:T(128)S(1)} %and_select_fusion.order, bf16[512,256]{1,0:T(8,128)(2,1)S(1)} %copy.30.refs_0_, bf16[512,256]{1,0:T(8,128)(2,1)S(1)} %collective-permute-done.refs_1_, bf16[512,256]{1,0:T(8,128)(2,1)S(1)} %collective-permute-done.1.refs_2_, ...), custom_call_target="tpu_custom_call" | custom-call | tf_op jit(solution)/shard_map/gradient_tiles/pallas_call | solution.py:65
  76.2 0.0 copy-start.7
  76.2 6.2 %all-to-all-start.1 = ((bf16[32,16,16,128]{3,2,1,0:T(8,128)(2,1)}), bf16[32,16,16,128]{3,2,1,0:T(8,128)(2,1)S(1)}, u32[]{:S(2)}, u32[]{:S(2)}) async-start(bf16[32,16,16,128]{3,2,1,0:T(8,128)(2,1)} %gradient_tiles.1), calls=%async_computation.1 | async-start | bytes 4194304 | tf_op jit(solution)/shard_map/all_to_all | solution.py:219
  82.4 0.0 copy-done.7
  82.4 0.2 convert_reduce_fusion
  82.6 0.6 fusion.1
  83.2 27.0 %all-to-all-done.1.parts = bf16[32,16,16,128]{3,2,1,0:T(8,128)(2,1)S(1)} async-done(((bf16[32,16,16,128]{3,2,1,0:T(8,128)(2,1)}), bf16[32,16,16,128]{3,2,1,0:T(8,128)(2,1)S(1)}, u32[]{:S(2)}, u32[]{:S(2)}) %all-to-all-start.1) | async-done | bytes 2097184 | tf_op jit(solution)/shard_map/all_to_all | solution.py:219
  110.2 0.0 copy-start.2
  110.2 3.3 %to_slots.1 = bf16[160,16,128]{2,1,0:T(8,128)(2,1)} custom-call(s32[128]{0:T(128)S(1)} %get-tuple-element.16.slot, bf16[32,16,16,128]{3,2,1,0:T(8,128)(2,1)S(1)} %all-to-all-done.1.parts), custom_call_target="tpu_custom_call" | custom-call | tf_op jit(solution)/shard_map/to_slots/pallas_call | solution.py:104
  113.6 0.0 copy-start.1
  113.6 6.1 %all-to-all-start.2 = ((bf16[32,5,16,128]{3,2,1,0:T(8,128)(2,1)}), bf16[32,5,16,128]{3,2,1,0:T(8,128)(2,1)S(1)}, u32[]{:S(2)}, u32[]{:S(2)}) async-start(bf16[32,5,16,128]{3,2,1,0:T(8,128)(2,1)} %bitcast.5), calls=%async_computation.2 | async-start | bytes 1310720 | tf_op jit(solution)/shard_map/all_to_all | solution.py:219
  119.7 0.7 compare_convert_fusion.live
  120.3 12.4 %all-to-all-done.2.tiles = bf16[32,5,16,128]{3,2,1,0:T(8,128)(2,1)S(1)} async-done(((bf16[32,5,16,128]{3,2,1,0:T(8,128)(2,1)}), bf16[32,5,16,128]{3,2,1,0:T(8,128)(2,1)S(1)}, u32[]{:S(2)}, u32[]{:S(2)}) %all-to-all-start.2) | async-done | bytes 655392 | tf_op jit(solution)/shard_map/all_to_all | solution.py:219
  132.7 0.0 copy-done.2
  132.7 0.0 copy-done.1
  132.7 0.0 copy-start.3
  132.7 1.1 copy-done.3
  133.8 0.0 copy-start.4
  133.8 1.1 copy-done.4
  134.9 0.0 copy-start.5
  134.9 1.1 copy-done.5
  135.9 0.0 copy-start.6
  135.9 1.1 copy-done.6
  137.0 5.9 %soap.1 = (bf16[32,5,16,128]{3,2,1,0:T(8,128)(2,1)S(1)}, f32[1,5,256,256]{3,2,1,0:T(8,128)}, f32[1,5,256,256]{3,2,1,0:T(8,128)}, bf16[1,5,256,256]{3,2,1,0:T(8,128)(2,1)}, bf16[1,5,256,256]{3,2,1,0:T(8,128)(2,1)}) custom-call(s32[5]{0:T(128)S(1)} %compare_convert_fusion.live, bf16[32,5,16,128]{3,2,1,0:T(8,128)(2,1)S(1)} %all-to-all-done.2.tiles, ...), custom_call_target="tpu_custom_call" | custom-call | tf_op jit(solution)/shard_map/soap/pallas_call | solution.py:203
  143.0 16.4 %all_to_all.26 = bf16[32,5,16,128]{3,2,1,0:T(8,128)(2,1)S(1)} all-to-all(bf16[32,5,16,128]{3,2,1,0:T(8,128)(2,1)S(1)} %get-tuple-element.10), channel_id=1, replica_groups=mesh['y'=4,'x'=4,'core'=2,'z'=8] {'y','x','core'}, dimensions={0} | all-to-all | bytes 1310720 | tf_op jit(solution)/shard_map/all_to_all | solution.py:219
  159.4 0.8 from_slots.1
  160.2 15.1 %all_to_all.27.tiles = bf16[32,4,16,128]{3,2,1,0:T(8,128)(2,1)S(1)} all-to-all(bf16[32,4,16,128]{3,2,1,0:T(8,128)(2,1)S(1)} %bitcast.16), channel_id=1, replica_groups=mesh['y'=4,'x'=4,'core'=2,'z'=8] {'y','x','core'}, dimensions={0} | all-to-all | bytes 1048576 | tf_op jit(solution)/shard_map/all_to_all | solution.py:219
  175.3 0.9 assemble.1
  (3 shorter events, 0.0 us)
Async XLA Ops:
  7.2 57.3 %all-gather.2.cloned.1.call-start = ((), (), s32[]{:S(2)}) async-start(), calls=%async_computation.5 | async-start | bytes 9437184 | tf_op jit(solution)/shard_map/all_gather | solution.py:255
  7.9 37.6 %copy-start.8 = (s32[8]{0:T(128)S(1)}, s32[8]{0:T(128)}, u32[]{:S(2)}) copy-start(s32[8]{0:T(128)} %constant.41.clone) | copy-start | bytes 100
  20.5 7.5 %collective-permute-start = (bf16[512,256]{1,0:T(8,128)(2,1)S(1)}, bf16[512,256]{1,0:T(8,128)(2,1)S(1)}, u32[]{:S(2)}, u32[]{:S(2)}) collective-permute-start(bf16[512,256]{1,0:T(8,128)(2,1)S(1)} %copy.30.refs_0_), channel_id=1, source_target_pairs={{0,1},{1,2},{2,3},{3,4},{4,5},{5,6},{6,7},{7,0},{8,9},{9,10},{10,1... | collective-permute-start | bytes 786440 | tf_op jit(solution)/shard_map/ppermute | solution.py:228
  23.4 8.0 %collective-permute-start.1 = (bf16[512,256]{1,0:T(8,128)(2,1)S(1)}, bf16[512,256]{1,0:T(8,128)(2,1)S(1)}, u32[]{:S(2)}, u32[]{:S(2)}) collective-permute-start(bf16[512,256]{1,0:T(8,128)(2,1)S(1)} %copy.30.refs_0_), channel_id=1, source_target_pairs={{0,7},{1,0},{2,1},{3,2},{4,3},{5,4},{6,5},{7,6},{8,15},{9,8},{10,9... | collective-permute-start | bytes 786440 | tf_op jit(solution)/shard_map/ppermute | solution.py:229
  27.9 7.0 %collective-permute-start.2 = (bf16[512,256]{1,0:T(8,128)(2,1)S(1)}, bf16[512,256]{1,0:T(8,128)(2,1)S(1)}, u32[]{:S(2)}, u32[]{:S(2)}) collective-permute-start(bf16[512,256]{1,0:T(8,128)(2,1)S(1)} %collective-permute-done.refs_1_), channel_id=1, source_target_pairs={{0,1},{1,2},{2,3},{3,4},{4,5},{5,6},{6,7},{7,0},{8,9},{9,10},{10,1... | collective-permute-start | bytes 786440 | tf_op jit(solution)/shard_map/ppermute | solution.py:228
  31.3 7.2 %collective-permute-start.3 = (bf16[512,256]{1,0:T(8,128)(2,1)S(1)}, bf16[512,256]{1,0:T(8,128)(2,1)S(1)}, u32[]{:S(2)}, u32[]{:S(2)}) collective-permute-start(bf16[512,256]{1,0:T(8,128)(2,1)S(1)} %collective-permute-done.1.refs_2_), channel_id=1, source_target_pairs={{0,7},{1,0},{2,1},{3,2},{4,3},{5,4},{6,5},{7,6},{8,15},{9,8},{10,9... | collective-permute-start | bytes 786440 | tf_op jit(solution)/shard_map/ppermute | solution.py:229
  35.0 6.8 %collective-permute-start.4 = (bf16[512,256]{1,0:T(8,128)(2,1)S(1)}, bf16[512,256]{1,0:T(8,128)(2,1)S(1)}, u32[]{:S(2)}, u32[]{:S(2)}) collective-permute-start(bf16[512,256]{1,0:T(8,128)(2,1)S(1)} %collective-permute-done.2.refs_3_), channel_id=1, source_target_pairs={{0,1},{1,2},{2,3},{3,4},{4,5},{5,6},{6,7},{7,0},{8,9},{9,10},{10,1... | collective-permute-start | bytes 786440 | tf_op jit(solution)/shard_map/ppermute | solution.py:228
  38.5 6.9 %collective-permute-start.5 = (bf16[512,256]{1,0:T(8,128)(2,1)S(1)}, bf16[512,256]{1,0:T(8,128)(2,1)S(1)}, u32[]{:S(2)}, u32[]{:S(2)}) collective-permute-start(bf16[512,256]{1,0:T(8,128)(2,1)S(1)} %collective-permute-done.3.refs_4_), channel_id=1, source_target_pairs={{0,7},{1,0},{2,1},{3,2},{4,3},{5,4},{6,5},{7,6},{8,15},{9,8},{10,9... | collective-permute-start | bytes 786440 | tf_op jit(solution)/shard_map/ppermute | solution.py:229
  41.8 5.5 %collective-permute-start.6 = (bf16[512,128]{1,0:T(8,128)(2,1)S(1)}, bf16[512,128]{1,0:T(8,128)(2,1)S(1)}, u32[]{:S(2)}, u32[]{:S(2)}) collective-permute-start(bf16[512,128]{1,0:T(8,128)(2,1)S(1)} %slice.8), channel_id=1, source_target_pairs={{0,1},{1,2},{2,3},{3,4},{4,5},{5,6},{6,7},{7,0},{8,9},{9,10},{10,1... | collective-permute-start | bytes 393224 | tf_op jit(solution)/shard_map/ppermute | solution.py:233
  45.4 5.5 %collective-permute-start.7 = (bf16[512,128]{1,0:T(8,128)(2,1)S(1)}, bf16[512,128]{1,0:T(8,128)(2,1)S(1)}, u32[]{:S(2)}, u32[]{:S(2)}) collective-permute-start(bf16[512,128]{1,0:T(8,128)(2,1)S(1)} %slice.9), channel_id=1, source_target_pairs={{0,7},{1,0},{2,1},{3,2},{4,3},{5,4},{6,5},{7,6},{8,15},{9,8},{10,9... | collective-permute-start | bytes 393224 | tf_op jit(solution)/shard_map/ppermute | solution.py:234
  64.4 3.4 %copy-start = (bf16[2048,2048]{1,0:T(8,128)(2,1)S(1)}, bf16[2048,2048]{1,0:T(8,128)(2,1)}, u32[]{:S(2)}) copy-start(bf16[2048,2048]{1,0:T(8,128)(2,1)} %all-gather.2.cloned.1.call-done) | copy-start | bytes 25165828
  76.2 6.2 %copy-start.7 = (s32[1,128]{1,0:T(1,128)S(1)}, s32[1,128]{1,0:T(1,128)}, u32[]{:S(2)}) copy-start(s32[1,128]{1,0:T(1,128)} %param.12) | copy-start | bytes 1540
  76.2 34.0 %all-to-all-start.1 = ((bf16[32,16,16,128]{3,2,1,0:T(8,128)(2,1)}), bf16[32,16,16,128]{3,2,1,0:T(8,128)(2,1)S(1)}, u32[]{:S(2)}, u32[]{:S(2)}) async-start(bf16[32,16,16,128]{3,2,1,0:T(8,128)(2,1)} %gradient_tiles.1), calls=%async_computation.1 | async-start | bytes 4194304 | tf_op jit(solution)/shard_map/all_to_all | solution.py:219
  110.2 22.4 %copy-start.2 = (f32[1,5,256,256]{3,2,1,0:T(8,128)S(1)}, f32[1,5,256,256]{3,2,1,0:T(8,128)}, u32[]{:S(2)}) copy-start(f32[1,5,256,256]{3,2,1,0:T(8,128)} %right.1) | copy-start | bytes 3932164
  113.6 19.1 %copy-start.1 = (f32[1,5,256,256]{3,2,1,0:T(8,128)S(1)}, f32[1,5,256,256]{3,2,1,0:T(8,128)}, u32[]{:S(2)}) copy-start(f32[1,5,256,256]{3,2,1,0:T(8,128)} %left.1) | copy-start | bytes 3932164
  113.6 19.1 %all-to-all-start.2 = ((bf16[32,5,16,128]{3,2,1,0:T(8,128)(2,1)}), bf16[32,5,16,128]{3,2,1,0:T(8,128)(2,1)S(1)}, u32[]{:S(2)}, u32[]{:S(2)}) async-start(bf16[32,5,16,128]{3,2,1,0:T(8,128)(2,1)} %bitcast.5), calls=%async_computation.2 | async-start | bytes 1310720 | tf_op jit(solution)/shard_map/all_to_all | solution.py:219
  132.7 1.1 copy-start.3
  133.8 1.1 copy-start.4
  134.9 1.1 copy-start.5
  135.9 1.1 copy-start.6
Sparse Core Ops, SparseCore 0:
  9.9 54.5 all-gather.1

commit v2 on v1

v2 whole, which is shorter than its diff:
```python
import jax
import jax.numpy as jnp
from jax import lax
from jax.experimental import pallas as pl
from jax.experimental.pallas import tpu as pltpu
from jax.sharding import Mesh
from jax.sharding import PartitionSpec as P

BLOCK = 256
TILE_ROWS = 16
TILE_COLS = 128
Y, X, CORE = 4, 4, 2
N_DP = Y * X * CORE
N_TENSOR = 8
ROW = X * CORE
STRIP = BLOCK // ROW
SLOTS = 5
HOME = 4
NBLK = 128
ROW_BLOCKS = 16
COL_BLOCKS = 8
TOK_SUB = 32
LOCAL_ROWS = ROW_BLOCKS * STRIP
DP = ("y", "x", "core")
CHIP_ROWS = LOCAL_ROWS * CORE
SHARD_K = X * TOK_SUB
WIDE = 2
CHUNK_K = NBLK // 2

factor_decay = 0.9
first_decay = 0.95
second_decay = 0.95
epsilon_value = 1e-08

MIB = 1024 * 1024
SMEM = pl.BlockSpec(memory_space=pltpu.SMEM)
VMEM = pl.BlockSpec(memory_space=pltpu.VMEM)


def params(mib):
    return pltpu.CompilerParams(vmem_limit_bytes=mib * MIB)


def tile_of(m):
    y, strip = m // ROW, m % ROW
    top, side = STRIP * strip + TILE_ROWS * (y // 2), TILE_COLS * (y % 2)
    return slice(top, top + TILE_ROWS), slice(side, side + TILE_COLS)


def cut_kernel(core, tokens, out):
    def strips_from(first):
        for chip in range(X):
            for i in range(CORE):
                start = STRIP * (chip * CORE + (first + i) % CORE)
                out[chip, :, i * LOCAL_ROWS : (i + 1) * LOCAL_ROWS] = jnp.concatenate(
                    [
                        tokens[:, r * BLOCK + start : r * BLOCK + start + STRIP]
                        for r in range(ROW_BLOCKS)
                    ],
                    axis=1,
                )

    for first in range(CORE):
        pl.when(core[0] == first)(lambda: strips_from(first))


def cut_tokens(core, tokens):
    return pl.pallas_call(
        cut_kernel,
        in_specs=[SMEM, VMEM],
        out_shape=jax.ShapeDtypeStruct((X, TOK_SUB, CHIP_ROWS), jnp.bfloat16),
        compiler_params=params(32),
        name="cut_tokens",
    )(core, tokens)


def turn_kernel(source, pieces, out):
    joined = jnp.concatenate([pieces[source[i]] for i in range(X)], axis=0)
    out[...] = joined.T


def turn(source, pieces):
    return pl.pallas_call(
        turn_kernel,
        in_specs=[SMEM, VMEM],
        out_shape=jax.ShapeDtypeStruct((CHIP_ROWS, SHARD_K), jnp.bfloat16),
        compiler_params=params(32),
        name="turn",
    )(source, pieces)


def gradient_kernel(place, *refs):
    whole, halves, sources = refs[:7], refs[7:9], refs[9:13]
    outs, (left, right) = refs[13:15], refs[15:]

    @pl.when(pl.program_id(0) == 0)
    def join_tokens():
        for j in range(7):
            left[:, j * SHARD_K : (j + 1) * SHARD_K] = whole[j][...]
        left[:LOCAL_ROWS, 7 * SHARD_K :] = halves[0][...]
        left[LOCAL_ROWS:, 7 * SHARD_K :] = halves[1][...]

    for j in range(N_TENSOR):
        for i in range(X):
            top = j * SHARD_K + i * TOK_SUB
            right[top : top + TOK_SUB] = sources[i][place[j]]
    for column in range(WIDE):
        blocks = slice(column * ROW_BLOCKS, (column + 1) * ROW_BLOCKS)
        result = jnp.dot(
            left[...], right[:, column * BLOCK : (column + 1) * BLOCK],
            preferred_element_type=jnp.float32,
        ).astype(jnp.bfloat16)
        for out, part in zip(outs, (result[:LOCAL_ROWS], result[LOCAL_ROWS:])):
            out[blocks] = part.reshape(ROW_BLOCKS, STRIP, BLOCK)


def gradient_strips(chunk, place, lefts, near, far):
    resident = lambda a: pl.BlockSpec(a.shape, lambda c, place: (0, 0))
    steps = COL_BLOCKS // 2 // WIDE
    shape = (N_TENSOR, TOK_SUB, WIDE * BLOCK)
    near_spec = pl.BlockSpec(shape, lambda c, place: (0, 0, steps * chunk + c))
    far_spec = pl.BlockSpec(shape, lambda c, place: (0, 0, c))
    strips = pl.BlockSpec((WIDE * ROW_BLOCKS, STRIP, BLOCK), lambda c, place: (c, 0, 0))
    return pl.pallas_call(
        gradient_kernel,
        grid_spec=pltpu.PrefetchScalarGridSpec(
            num_scalar_prefetch=1,
            grid=(steps,),
            in_specs=[resident(a) for a in lefts] + [near_spec] * 3 + [far_spec],
            out_specs=[strips] * CORE,
            scratch_shapes=[
                pltpu.VMEM((CHIP_ROWS, N_TENSOR * SHARD_K), jnp.bfloat16),
                pltpu.VMEM((N_TENSOR * SHARD_K, WIDE * BLOCK), jnp.bfloat16),
            ],
        ),
        out_shape=[jax.ShapeDtypeStruct((CHUNK_K, STRIP, BLOCK), jnp.bfloat16)] * CORE,
        compiler_params=params(60),
        cost_estimate=pl.CostEstimate(
            flops=2 * CHIP_ROWS * N_TENSOR * SHARD_K * 4 * BLOCK,
            bytes_accessed=8 * MIB, transcendentals=0,
        ),
        name="gradient_strips",
    )(place, *lefts, *near, far)


def to_slots_kernel(slot, *refs):
    out = refs[-1]
    out[...] = jnp.zeros_like(out)
    for chunk in range(2):
        one, two = refs[2 * chunk : 2 * chunk + 2]

        def body(k, carry):
            total = one[k].astype(jnp.float32) + two[k].astype(jnp.float32)
            out[slot[chunk * CHUNK_K + k]] = total.astype(jnp.bfloat16)
            return carry

        lax.fori_loop(0, CHUNK_K, body, 0, unroll=8)


def to_slots(slot, parts):
    return pl.pallas_call(
        to_slots_kernel,
        in_specs=[SMEM] + [VMEM] * len(parts),
        out_shape=jax.ShapeDtypeStruct((N_DP * SLOTS, STRIP, BLOCK), jnp.bfloat16),
        compiler_params=params(32),
        name="to_slots",
    )(slot, *parts)


def from_slots_kernel(slot, tiles, out):
    def body(k, carry):
        out[k] = tiles[slot[k]]
        return carry

    lax.fori_loop(0, NBLK, body, 0, unroll=8)


def from_slots(slot, tiles):
    return pl.pallas_call(
        from_slots_kernel,
        in_specs=[SMEM, VMEM],
        out_shape=jax.ShapeDtypeStruct((NBLK, TILE_ROWS, TILE_COLS), jnp.bfloat16),
        compiler_params=params(32),
        name="from_slots",
    )(slot, tiles)


def assemble_kernel(tiles, out):
    for h in range(HOME):
        for m in range(N_DP):
            rows, cols = tile_of(m)
            out[0, h, rows, cols] = tiles[m, h]


def assemble(tiles):
    return pl.pallas_call(
        assemble_kernel,
        out_shape=jax.ShapeDtypeStruct((1, HOME, BLOCK, BLOCK), jnp.bfloat16),
        compiler_params=params(32),
        name="assemble",
    )(tiles)


def dot(a, b, ca, cb):
    return lax.dot_general(a, b, (((ca,), (cb,)), ((), ())), preferred_element_type=jnp.float32)


def update_kernel(
    live, strips, basis_left, basis_right, first, second,
    update, grads, first_new, second_new,
):
    for s in range(SLOTS):
        for strip in range(ROW):
            total = strips[strip, s].astype(jnp.float32)
            for y in range(1, Y):
                total = total + strips[y * ROW + strip, s].astype(jnp.float32)
            grads[s, strip * STRIP : (strip + 1) * STRIP] = total.astype(jnp.bfloat16)
        grad = grads[s]
        ql, qr = basis_left[0, s], basis_right[0, s]
        halfway = dot(ql, grad, 0, 0).astype(jnp.bfloat16)
        rotated = dot(halfway, qr, 1, 0)
        first_old, second_old = first[0, s], second[0, s]
        first_float = first_decay * first_old.astype(jnp.float32) + (1.0 - first_decay) * rotated
        second_float = (
            second_decay * second_old.astype(jnp.float32)
            + (1.0 - second_decay) * rotated * rotated
        )
        ratio = (first_float / (jnp.sqrt(second_float) + epsilon_value)).astype(jnp.bfloat16)
        turned = dot(ql, ratio, 1, 0).astype(jnp.bfloat16)
        result = dot(turned, qr, 1, 1).astype(jnp.bfloat16)
        for m in range(N_DP):
            rows, cols = tile_of(m)
            update[m, s] = result[rows, cols]
        alive = live[s] > 0
        first_new[0, s] = jnp.where(alive, first_float.astype(jnp.bfloat16), first_old)
        second_new[0, s] = jnp.where(alive, second_float.astype(jnp.bfloat16), second_old)


def update_blocks(live, strips, basis_left, basis_right, first, second):
    like = lambda a: jax.ShapeDtypeStruct(a.shape, a.dtype)
    return pl.pallas_call(
        update_kernel,
        in_specs=[SMEM] + [VMEM] * 5,
        out_shape=[
            jax.ShapeDtypeStruct((N_DP, SLOTS, TILE_ROWS, TILE_COLS), jnp.bfloat16),
            jax.ShapeDtypeStruct((SLOTS, BLOCK, BLOCK), jnp.bfloat16),
            like(first),
            like(second),
        ],
        compiler_params=params(60),
        name="update",
    )(live, strips, basis_left, basis_right, first, second)


def factor_kernel(live, grads, left, right, left_new, right_new):
    alive = live[pl.program_id(0)] > 0
    grad = grads[0]
    scale = (1.0 - factor_decay) / BLOCK
    left_old, right_old = left[0, 0], right[0, 0]
    left_new[0, 0] = jnp.where(
        alive, factor_decay * left_old + scale * dot(grad, grad, 1, 1), left_old
    )
    right_new[0, 0] = jnp.where(
        alive, factor_decay * right_old + scale * dot(grad, grad, 0, 0), right_old
    )


def update_factors(live, grads, left, right):
    state = pl.BlockSpec((1, 1, BLOCK, BLOCK), lambda s, live: (0, s, 0, 0))
    return pl.pallas_call(
        factor_kernel,
        grid_spec=pltpu.PrefetchScalarGridSpec(
            num_scalar_prefetch=1,
            grid=(SLOTS,),
            in_specs=[pl.BlockSpec((1, BLOCK, BLOCK), lambda s, live: (s, 0, 0))] + [state] * 2,
            out_specs=[state] * 2,
        ),
        out_shape=[jax.ShapeDtypeStruct(a.shape, a.dtype) for a in (left, right)],
        compiler_params=params(60),
        cost_estimate=pl.CostEstimate(
            flops=4 * SLOTS * BLOCK**3, bytes_accessed=6 * MIB, transcendentals=0
        ),
        name="factors",
    )(live, grads, left, right)


def spread(array, axes):
    return lax.all_to_all(array, axes, split_axis=0, concat_axis=0, tiled=True)


def ring(size, step):
    return [(i, (i + step) % size) for i in range(size)]


def gather_row(tokens, grads, source, core):
    up, down = ring(N_TENSOR, 1), ring(N_TENSOR, -1)
    ahead, back = ring(X, 1), ring(X, -1)

    pieces, grads = lax.optimization_barrier((spread(cut_tokens(core, tokens), "x"), grads))
    behind, before = lax.ppermute(grads, "x", ahead), lax.ppermute(grads, "x", back)
    mine = turn(source, pieces)
    below, above = lax.ppermute(mine, "z", up), lax.ppermute(mine, "z", down)
    whole = [mine, below, above]
    below, above = lax.ppermute(below, "z", up), lax.ppermute(above, "z", down)
    whole += [below, above]
    behind, before, below, above = lax.optimization_barrier((behind, before, below, above))
    half = grads.shape[-1] // 2
    far = [
        lax.ppermute(behind[..., :half], "x", ahead),
        lax.ppermute(before[..., half:], "x", back),
    ]
    below, above = lax.ppermute(below, "z", up), lax.ppermute(above, "z", down)
    whole += [below, above]
    halves = [
        lax.ppermute(below[:LOCAL_ROWS], "z", up),
        lax.ppermute(above[LOCAL_ROWS:], "z", down),
    ]
    return whole + halves, [grads, behind, before], far


def local(
    tokens, grad_out, owner, left_factor, right_factor,
    left_basis, right_basis, first_moment, second_moment,
):
    owner_row = owner[0]
    block_ids = jnp.arange(NBLK, dtype=jnp.int32)
    same = owner_row[:, None] == owner_row[None, :]
    before = block_ids[None, :] < block_ids[:, None]
    rank = jnp.sum((same & before).astype(jnp.int32), axis=1)
    slot = owner_row * SLOTS + rank
    held = jnp.sum((owner_row == lax.axis_index(DP)).astype(jnp.int32))
    live = (jnp.arange(SLOTS, dtype=jnp.int32) < held).astype(jnp.int32)

    steps = jnp.array([0, -1, 1, -2, 2, -3, 3, 4], jnp.int32)
    place = (lax.axis_index("z") + steps + N_TENSOR) % N_TENSOR
    along = jnp.array([0, -1, 1, 2], jnp.int32)
    source = (lax.axis_index("x") + along + X) % X
    core = lax.axis_index("core").astype(jnp.int32).reshape(1)
    grads = grad_out.reshape(N_TENSOR, TOK_SUB, grad_out.shape[1])
    lefts, near, far = gather_row(tokens, grads, source, core)
    parts = []
    for chunk in range(2):
        mine, other = gradient_strips(chunk, place, lefts, near, far[chunk])
        parts += [mine, lax.ppermute(other, "core", ring(CORE, 1))]
    strips = to_slots(slot, parts).reshape(N_DP, SLOTS, STRIP, BLOCK)
    update, grad_blocks, first_new, second_new = update_blocks(
        live, spread(strips, DP), left_basis, right_basis, first_moment, second_moment
    )
    left_new, right_new = update_factors(live, grad_blocks, left_factor, right_factor)
    back = spread(update, DP).reshape(N_DP * SLOTS, TILE_ROWS, TILE_COLS)
    picked = from_slots(slot, back).reshape(N_DP, HOME, TILE_ROWS, TILE_COLS)
    home_update = assemble(spread(picked, DP))
    return (home_update, left_new, right_new, first_new, second_new)


def solution(mesh):
    split = Mesh(mesh.devices.reshape(Y, X, CORE, N_TENSOR), ("y", "x", "core", "z"))
    state = P("z", DP, None, None)
    return jax.shard_map(
        local,
        mesh=split,
        in_specs=(P((*DP, "z"), None), P(DP, "z"), P("z", None)) + (state,) * 6,
        out_specs=(state,) * 5,
        check_vma=False,
    )
```

time: 186 us -> 165 us (0.89); the launches traced: 183 us -> 164 us
  blocking collectives: 42.8 us -> 28.7 us
  between operations: 14.2 us -> 0.83 us
  Pallas kernels: 19.3 us -> 31.6 us
  waiting for transfers between devices: 70.4 us -> 58.4 us
  starting transfers between devices: 25.8 us -> 36.2 us
  local copies, waits for them, and re-layouts: 9.02 us -> 5.49 us
    all_to_all x3 -> x2, blocking collectives: 42.8 us -> 28.7 us  [spread(): return lax.all_to_all(array, axes, split_axis=0, concat_axis=0, tiled=True)]
    all_gather x1 -> x0, waiting for transfers between devices: 13.5 us -> none  [local(): grads = lax.all_gather(grad_out, ROW_AXES, axis=0, tiled=True)]
    pallas_call x4 -> x8, Pallas kernels: 18.4 us -> 30.7 us  [the longest x2 13.2 us: gradient_strips(): pl.pallas_call(gradient_kernel, grid_spec=pltpu.PrefetchScalarGridSpec(nu...]
    ppermute x8 -> x14, starting transfers between devices: 13.5 us -> 23.2 us  [the longest x2 6.23 us: gather_row(): lax.ppermute(below, 'z', up)]
    unnamed x19 -> x28, local copies, waits for them, and re-layouts: 8.79 us -> 4.35 us
    ppermute x8 -> x14, waiting for transfers between devices: 16.9 us -> 20.5 us  [the longest x1 3.74 us: gather_row(): lax.ppermute(above[LOCAL_ROWS:], 'z', down)]
  transfers between devices with their start and end apart: 11 -> 16, of which waited for: 8 -> 10; matrix products, arithmetic and copies ran while one was open for 2% -> 3% of each run, Pallas kernels for 0% -> 12%
where the time goes in v2:
time: 165 us; the launch traced here: 164 us
  waiting for transfers between devices  58.4 us (35%)
  starting transfers between devices  36.2 us (22%)
  Pallas kernels  31.6 us (19%)
  blocking collectives  28.7 us (17%)
  local copies, waits for them, and re-layouts  5.49 us (3%)
  other arithmetic  3.28 us (2%)
    all_to_all x2, waiting for transfers between devices, spread(): return lax.all_to_all(array, axes, split_axis=0, concat_axis=0, tiled=True)  37.9 us
    all_to_all x2, blocking collectives, spread(): return lax.all_to_all(array, axes, split_axis=0, concat_axis=0, tiled=True)  28.7 us
    pallas_call x2, Pallas kernels, gradient_strips(): pl.pallas_call(gradient_kernel, grid_spec=pltpu.PrefetchScalarGridSpec(nu...  13.2 us
    all_to_all x2, starting transfers between devices, spread(): return lax.all_to_all(array, axes, split_axis=0, concat_axis=0, tiled=True)  13 us
    ppermute x2, starting transfers between devices, gather_row(): lax.ppermute(below, 'z', up)  6.23 us
    pallas_call x1, Pallas kernels, update_blocks(): pl.pallas_call(update_kernel, in_specs=[SMEM] + [VMEM] * 5, out_shape=[ja...  6.18 us
    pallas_call x1, Pallas kernels, update_factors(): pl.pallas_call(factor_kernel, grid_spec=pltpu.PrefetchScalarGridSpec(num_...  6.13 us
    ppermute x2, starting transfers between devices, local(): parts += [mine, lax.ppermute(other, 'core', ring(CORE, 1))]  5.53 us
  transfers between devices with their start and end apart: 16, of which 10 were waited for; matrix products, arithmetic and copies ran while one was open for 3% of the time, Pallas kernels for 12%

profile of v2, /device:TPU:97, one launch (start us, length us, event | category | flops | bytes accessed | tf_op | source)
XLA Modules:
  0.0 164.5 jit_solution(11072516377446625760)
XLA Ops:
  0.6 0.0 copy-start.2
  0.6 0.9 copy-done.2
  1.6 0.3 cut_tokens.1
  1.9 9.4 %all_to_all.20.pieces = bf16[4,32,1024]{2,1,0:T(8,128)(2,1)S(1)} all-to-all(bf16[4,32,1024]{2,1,0:T(8,128)(2,1)S(1)} %cut_tokens.1), channel_id=1, replica_groups=mesh['y'=4,'x'=4,'core'=2,'z'=8] {'x'}, dimensions={0} | all-to-all | bytes 524288 | tf_op jit(solution)/shard_map/all_to_all | solution.py:288
  11.2 0.4 collective-permute-start.4
  11.6 2.3 %collective-permute-start.5 = (bf16[8,32,2048]{2,1,0:T(8,128)(2,1)}, bf16[8,32,2048]{2,1,0:T(8,128)(2,1)}, u32[]{:S(2)}, u32[]{:S(2)}) collective-permute-start(bf16[8,32,2048]{2,1,0:T(8,128)(2,1)} %bitcast.11), channel_id=1, source_target_pairs={{0,48},{16,0},{32,16},{48,32},{1,49},{17,1},{33,17},{49,33},{2,50}... | collective-permute-start | bytes 3145736 | tf_op jit(solution)/shard_map/ppermute | solution.py:300
  13.9 0.7 and_select_fusion.source
  14.6 0.7 turn.1.refs_0_
  15.2 0.0 copy-start.3
  15.3 0.0 copy-start.13
  15.3 2.9 %collective-permute-start = (bf16[1024,128]{1,0:T(8,128)(2,1)S(1)}, bf16[1024,128]{1,0:T(8,128)(2,1)S(1)}, u32[]{:S(2)}, u32[]{:S(2)}) collective-permute-start(bf16[1024,128]{1,0:T(8,128)(2,1)S(1)} %turn.1.refs_0_), channel_id=1, source_target_pairs={{0,1},{1,2},{2,3},{3,4},{4,5},{5,6},{6,7},{7,0},{8,9},{9,10},{10,1... | collective-permute-start | bytes 786440 | tf_op jit(solution)/shard_map/ppermute | solution.py:302
  18.2 0.0 collective-permute-start.1
  18.2 3.3 %collective-permute-done.refs_1_ = bf16[1024,128]{1,0:T(8,128)(2,1)S(1)} collective-permute-done((bf16[1024,128]{1,0:T(8,128)(2,1)S(1)}, bf16[1024,128]{1,0:T(8,128)(2,1)S(1)}, u32[]{:S(2)}, u32[]{:S(2)}) %collective-permute-start) | collective-permute-done | bytes 262176 | tf_op jit(solution)/shard_map/ppermute | solution.py:302
  21.5 3.4 %collective-permute-start.2 = (bf16[1024,128]{1,0:T(8,128)(2,1)S(1)}, bf16[1024,128]{1,0:T(8,128)(2,1)}, u32[]{:S(2)}, u32[]{:S(2)}) collective-permute-start(bf16[1024,128]{1,0:T(8,128)(2,1)S(1)} %collective-permute-done.refs_1_), channel_id=1, source_target_pairs={{0,1},{1,2},{2,3},{3,4},{4,5},{5,6},{6,7},{7,0},{8,9},{9,10},{10,1... | collective-permute-start | bytes 786440 | tf_op jit(solution)/shard_map/ppermute | solution.py:304
  24.9 0.0 collective-permute-done.1.refs_2_
  24.9 0.0 collective-permute-start.3
  24.9 3.3 %collective-permute-done.2.refs_3_ = bf16[1024,128]{1,0:T(8,128)(2,1)} collective-permute-done((bf16[1024,128]{1,0:T(8,128)(2,1)S(1)}, bf16[1024,128]{1,0:T(8,128)(2,1)}, u32[]{:S(2)}, u32[]{:S(2)}) %collective-permute-start.2) | collective-permute-done | bytes 262176 | tf_op jit(solution)/shard_map/ppermute | solution.py:304
  28.2 3.4 %collective-permute-done.3.refs_4_ = bf16[1024,128]{1,0:T(8,128)(2,1)} collective-permute-done((bf16[1024,128]{1,0:T(8,128)(2,1)S(1)}, bf16[1024,128]{1,0:T(8,128)(2,1)}, u32[]{:S(2)}, u32[]{:S(2)}) %collective-permute-start.3) | collective-permute-done | bytes 262176 | tf_op jit(solution)/shard_map/ppermute | solution.py:304
  31.7 3.7 %collective-permute-done.4.refs_10_ = bf16[8,32,2048]{2,1,0:T(8,128)(2,1)S(1)} collective-permute-done((bf16[8,32,2048]{2,1,0:T(8,128)(2,1)}, bf16[8,32,2048]{2,1,0:T(8,128)(2,1)S(1)}, u32[]{:S(2)}, u32[]{:S(2)}) %collective-permute-start.4) | collective-permute-done | bytes 1048608 | tf_op jit(solution)/shard_map/ppermute | solution.py:300
  35.3 0.0 collective-permute-done.5.refs_11_
  35.4 0.1 collective-permute-start.10
  35.5 2.8 %collective-permute-start.6 = (bf16[1024,128]{1,0:T(8,128)(2,1)}, bf16[1024,128]{1,0:T(8,128)(2,1)S(1)}, u32[]{:S(2)}, u32[]{:S(2)}) collective-permute-start(bf16[1024,128]{1,0:T(8,128)(2,1)} %collective-permute-done.2.refs_3_), channel_id=1, source_target_pairs={{0,1},{1,2},{2,3},{3,4},{4,5},{5,6},{6,7},{7,0},{8,9},{9,10},{10,1... | collective-permute-start | bytes 786440 | tf_op jit(solution)/shard_map/ppermute | solution.py:312
  38.3 0.0 collective-permute-start.7
  38.3 1.1 slice.15
  39.4 2.7 %collective-permute-start.12 = (bf16[8,32,1024]{2,1,0:T(8,128)(2,1)S(1)}, bf16[8,32,1024]{2,1,0:T(8,128)(2,1)}, u32[]{:S(2)}, u32[]{:S(2)}) collective-permute-start(bf16[8,32,1024]{2,1,0:T(8,128)(2,1)S(1)} %slice.15), channel_id=1, source_target_pairs={{0,48},{16,0},{32,16},{48,32},{1,49},{17,1},{33,17},{49,33},{2,50}... | collective-permute-start | bytes 1572872 | tf_op jit(solution)/shard_map/ppermute | solution.py:310
  42.0 0.0 copy-done.10
  42.0 0.0 collective-permute-done.6.refs_5_
  42.1 3.0 %collective-permute-start.8 = (bf16[512,128]{1,0:T(8,128)(2,1)S(1)}, bf16[512,128]{1,0:T(8,128)(2,1)S(1)}, u32[]{:S(2)}, u32[]{:S(2)}) collective-permute-start(bf16[512,128]{1,0:T(8,128)(2,1)S(1)} %slice.16), channel_id=1, source_target_pairs={{0,1},{1,2},{2,3},{3,4},{4,5},{5,6},{6,7},{7,0},{8,9},{9,10},{10,1... | collective-permute-start | bytes 393224 | tf_op jit(solution)/shard_map/ppermute | solution.py:315
  45.0 0.3 collective-permute-done.7.refs_6_
  45.4 0.0 copy-done.3
  45.4 0.0 copy-done.9
  45.4 0.1 collective-permute-start.9
  45.5 0.6 and_select_fusion.1.place
  46.1 0.9 collective-permute-done.8.refs_7_
  47.0 3.7 %collective-permute-done.9.refs_8_ = bf16[512,128]{1,0:T(8,128)(2,1)S(1)} collective-permute-done((bf16[512,128]{1,0:T(8,128)(2,1)S(1)}, bf16[512,128]{1,0:T(8,128)(2,1)S(1)}, u32[]{:S(2)}, u32[]{:S(2)}) %collective-permute-start.9) | collective-permute-done | bytes 131104 | tf_op jit(solution)/shard_map/ppermute | solution.py:316
  50.7 0.0 collective-permute-done.10.refs_12_
  50.7 0.0 copy-done.6
  50.7 0.0 copy-done.7
  50.7 0.0 copy-done.11
  50.7 0.6 copy-done.12
  51.4 6.6 %gradient_strips.2 = (bf16[64,32,256]{2,1,0:T(8,128)(2,1)}, bf16[64,32,256]{2,1,0:T(8,128)(2,1)}) custom-call(s32[8]{0:T(128)} %and_select_fusion.1.place, bf16[1024,128]{1,0:T(8,128)(2,1)} %copy-done.3, bf16[1024,128]{1,0:T(8,128)(2,1)} %copy-done.9, bf16[1024,128]{1,0:T(8,128)(2,1)} %copy-done.10, bf16[1024,128]{1,0:T(8,128)(2,1)} %collective-permute-done.2.refs_3_, ...), custom_call_target="tpu_custom_call" | custom-call | flops 2147483648 | bytes 8388608 | tf_op jit(solution)/shard_map/gradient_strips/pallas_call | solution.py:124
  58.0 0.0 copy-start
  58.0 5.3 %collective-permute-start.11 = (bf16[64,32,256]{2,1,0:T(8,128)(2,1)}, bf16[64,32,256]{2,1,0:T(8,128)(2,1)S(1)}, u32[]{:S(2)}, u32[]{:S(2)}) collective-permute-start(bf16[64,32,256]{2,1,0:T(8,128)(2,1)} %get-tuple-element.28), channel_id=1, source_target_pairs={{0,8},{8,0},{1,9},{9,1},{2,10},{10,2},{3,11},{11,3},{4,12},{12,4},... | collective-permute-start | bytes 3145736 | tf_op jit(solution)/shard_map/ppermute | solution.py:344
  63.3 0.0 collective-permute-done.12.refs_12_
  63.3 6.6 %gradient_strips.3 = (bf16[64,32,256]{2,1,0:T(8,128)(2,1)}, bf16[64,32,256]{2,1,0:T(8,128)(2,1)}) custom-call(s32[8]{0:T(128)} %and_select_fusion.1.place, bf16[1024,128]{1,0:T(8,128)(2,1)} %copy-done.3, bf16[1024,128]{1,0:T(8,128)(2,1)} %copy-done.9, bf16[1024,128]{1,0:T(8,128)(2,1)} %copy-done.10, bf16[1024,128]{1,0:T(8,128)(2,1)} %collective-permute-done.2.refs_3_, ...), custom_call_target="tpu_custom_call" | custom-call | flops 2147483648 | bytes 8388608 | tf_op jit(solution)/shard_map/gradient_strips/pallas_call | solution.py:124
  69.9 0.2 collective-permute-start.13
  70.1 0.2 convert_reduce_fusion
  70.3 0.6 fusion.1
  70.9 0.0 collective-permute-done.11.refs_1_
  70.9 1.9 %collective-permute-done.13.refs_3_ = bf16[64,32,256]{2,1,0:T(8,128)(2,1)S(1)} collective-permute-done((bf16[64,32,256]{2,1,0:T(8,128)(2,1)}, bf16[64,32,256]{2,1,0:T(8,128)(2,1)S(1)}, u32[]{:S(2)}, u32[]{:S(2)}) %collective-permute-start.13) | collective-permute-done | bytes 1048608 | tf_op jit(solution)/shard_map/ppermute | solution.py:344
  72.8 0.0 copy-done
  72.8 1.2 copy-done.1
  74.1 2.8 %to_slots.1 = bf16[160,32,256]{2,1,0:T(8,128)(2,1)} custom-call(s32[128]{0:T(128)S(1)} %get-tuple-element.38.slot, bf16[64,32,256]{2,1,0:T(8,128)(2,1)S(1)} %copy-done, bf16[64,32,256]{2,1,0:T(8,128)(2,1)S(1)} %collective-permute-done.11.refs_1_, bf16[64,32,256]{2,1,0:T(8,128)(2,1)S(1)} %copy-done.1, bf16[64,32,256]{2,1,0:T(8,128)(2,1)S(1)} %collective-permute-done.13.refs_3_), custom_call_target="tpu_custom_call" | custom-call | tf_op jit(solution)/shard_map/to_slots/pallas_call | solution.py:161
  76.8 8.9 %all-to-all-start.1 = ((bf16[32,5,32,256]{3,2,1,0:T(8,128)(2,1)}), bf16[32,5,32,256]{3,2,1,0:T(8,128)(2,1)S(1)}, u32[]{:S(2)}, u32[]{:S(2)}) async-start(bf16[32,5,32,256]{3,2,1,0:T(8,128)(2,1)} %bitcast.3), calls=%async_computation.1 | async-start | bytes 5242880 | tf_op jit(solution)/shard_map/all_to_all | solution.py:288
  85.8 1.2 compare_convert_fusion.live
  87.0 32.3 %all-to-all-done.1.strips = bf16[32,5,32,256]{3,2,1,0:T(8,128)(2,1)S(1)} async-done(((bf16[32,5,32,256]{3,2,1,0:T(8,128)(2,1)}), bf16[32,5,32,256]{3,2,1,0:T(8,128)(2,1)S(1)}, u32[]{:S(2)}, u32[]{:S(2)}) %all-to-all-start.1) | async-done | bytes 2621472 | tf_op jit(solution)/shard_map/all_to_all | solution.py:288
  119.3 1.5 copy-done.4
  120.8 6.2 %update.1 = (bf16[32,5,16,128]{3,2,1,0:T(8,128)(2,1)}, bf16[5,256,256]{2,1,0:T(8,128)(2,1)}, bf16[1,5,256,256]{3,2,1,0:T(8,128)(2,1)}, bf16[1,5,256,256]{3,2,1,0:T(8,128)(2,1)}) custom-call(s32[5]{0:T(128)} %compare_convert_fusion.live, bf16[32,5,32,256]{3,2,1,0:T(8,128)(2,1)} %copy-done.4, bf16[1,5,256,256]{3,2,1,0:T(8,128)(2,1)} %basis_left.1, ...), custom_call_target="tpu_custom_call" | custom-call | tf_op jit(solution)/shard_map/update/pallas_call | solution.py:241
  127.0 19.3 %all_to_all.21 = bf16[32,5,16,128]{3,2,1,0:T(8,128)(2,1)S(1)} all-to-all(bf16[32,5,16,128]{3,2,1,0:T(8,128)(2,1)} %get-tuple-element.31), channel_id=1, replica_groups=mesh['y'=4,'x'=4,'core'=2,'z'=8] {'y','x','core'}, dimensions={0} | all-to-all | bytes 1310720 | tf_op jit(solution)/shard_map/all_to_all | solution.py:288
  146.3 1.6 from_slots.1
  147.9 4.1 %all-to-all-start.3 = ((bf16[32,4,16,128]{3,2,1,0:T(8,128)(2,1)}), bf16[32,4,16,128]{3,2,1,0:T(8,128)(2,1)S(1)}, u32[]{:S(2)}, u32[]{:S(2)}) async-start(bf16[32,4,16,128]{3,2,1,0:T(8,128)(2,1)} %bitcast.5), calls=%async_computation.3 | async-start | bytes 1048576 | tf_op jit(solution)/shard_map/all_to_all | solution.py:288
  151.9 6.1 %factors.1 = (f32[1,5,256,256]{3,2,1,0:T(8,128)}, f32[1,5,256,256]{3,2,1,0:T(8,128)}) custom-call(s32[5]{0:T(128)} %compare_convert_fusion.live, bf16[5,256,256]{2,1,0:T(8,128)(2,1)} %get-tuple-element.32.grads, f32[1,5,256,256]{3,2,1,0:T(8,128)} %left.1, f32[1,5,256,256]{3,2,1,0:T(8,128)} %right.1), custom_call_target="tpu_custom_call" | custom-call | flops 335544320 | bytes 6291456 | tf_op jit(solution)/shard_map/factors/pallas_call | solution.py:270
  158.1 5.5 %all-to-all-done.3.tiles = bf16[32,4,16,128]{3,2,1,0:T(8,128)(2,1)S(1)} async-done(((bf16[32,4,16,128]{3,2,1,0:T(8,128)(2,1)}), bf16[32,4,16,128]{3,2,1,0:T(8,128)(2,1)S(1)}, u32[]{:S(2)}, u32[]{:S(2)}) %all-to-all-start.3) | async-done | bytes 524320 | tf_op jit(solution)/shard_map/all_to_all | solution.py:288
  163.6 0.9 assemble.1
  (16 shorter events, 0.1 us)
Async XLA Ops:
  0.6 1.0 copy-start.2
  11.2 24.1 %collective-permute-start.4 = (bf16[8,32,2048]{2,1,0:T(8,128)(2,1)}, bf16[8,32,2048]{2,1,0:T(8,128)(2,1)S(1)}, u32[]{:S(2)}, u32[]{:S(2)}) collective-permute-start(bf16[8,32,2048]{2,1,0:T(8,128)(2,1)} %bitcast.10), channel_id=1, source_target_pairs={{0,16},{16,32},{32,48},{48,0},{1,17},{17,33},{33,49},{49,1},{2,18}... | collective-permute-start | bytes 3145736 | tf_op jit(solution)/shard_map/ppermute | solution.py:300
  11.6 23.7 %collective-permute-start.5 = (bf16[8,32,2048]{2,1,0:T(8,128)(2,1)}, bf16[8,32,2048]{2,1,0:T(8,128)(2,1)}, u32[]{:S(2)}, u32[]{:S(2)}) collective-permute-start(bf16[8,32,2048]{2,1,0:T(8,128)(2,1)} %bitcast.11), channel_id=1, source_target_pairs={{0,48},{16,0},{32,16},{48,32},{1,49},{17,1},{33,17},{49,33},{2,50}... | collective-permute-start | bytes 3145736 | tf_op jit(solution)/shard_map/ppermute | solution.py:300
  15.2 30.1 %copy-start.3 = (bf16[1024,128]{1,0:T(8,128)(2,1)}, bf16[1024,128]{1,0:T(8,128)(2,1)S(1)}, u32[]{:S(2)}) copy-start(bf16[1024,128]{1,0:T(8,128)(2,1)S(1)} %turn.1.refs_0_) | copy-start | bytes 786436
  15.3 30.2 %copy-start.13 = (s32[8]{0:T(128)S(1)}, s32[8]{0:T(128)}, u32[]{:S(2)}) copy-start(s32[8]{0:T(128)} %constant.58.clone) | copy-start | bytes 100
  15.3 6.2 %collective-permute-start = (bf16[1024,128]{1,0:T(8,128)(2,1)S(1)}, bf16[1024,128]{1,0:T(8,128)(2,1)S(1)}, u32[]{:S(2)}, u32[]{:S(2)}) collective-permute-start(bf16[1024,128]{1,0:T(8,128)(2,1)S(1)} %turn.1.refs_0_), channel_id=1, source_target_pairs={{0,1},{1,2},{2,3},{3,4},{4,5},{5,6},{6,7},{7,0},{8,9},{9,10},{10,1... | collective-permute-start | bytes 786440 | tf_op jit(solution)/shard_map/ppermute | solution.py:302
  18.2 6.7 %collective-permute-start.1 = (bf16[1024,128]{1,0:T(8,128)(2,1)S(1)}, bf16[1024,128]{1,0:T(8,128)(2,1)S(1)}, u32[]{:S(2)}, u32[]{:S(2)}) collective-permute-start(bf16[1024,128]{1,0:T(8,128)(2,1)S(1)} %turn.1.refs_0_), channel_id=1, source_target_pairs={{0,7},{1,0},{2,1},{3,2},{4,3},{5,4},{6,5},{7,6},{8,15},{9,8},{10,9... | collective-permute-start | bytes 786440 | tf_op jit(solution)/shard_map/ppermute | solution.py:302
  21.5 23.9 %copy-start.9 = (bf16[1024,128]{1,0:T(8,128)(2,1)}, bf16[1024,128]{1,0:T(8,128)(2,1)S(1)}, u32[]{:S(2)}) copy-start(bf16[1024,128]{1,0:T(8,128)(2,1)S(1)} %collective-permute-done.refs_1_) | copy-start | bytes 786436
  21.5 6.7 %collective-permute-start.2 = (bf16[1024,128]{1,0:T(8,128)(2,1)S(1)}, bf16[1024,128]{1,0:T(8,128)(2,1)}, u32[]{:S(2)}, u32[]{:S(2)}) collective-permute-start(bf16[1024,128]{1,0:T(8,128)(2,1)S(1)} %collective-permute-done.refs_1_), channel_id=1, source_target_pairs={{0,1},{1,2},{2,3},{3,4},{4,5},{5,6},{6,7},{7,0},{8,9},{9,10},{10,1... | collective-permute-start | bytes 786440 | tf_op jit(solution)/shard_map/ppermute | solution.py:304
  24.9 17.1 %copy-start.10 = (bf16[1024,128]{1,0:T(8,128)(2,1)}, bf16[1024,128]{1,0:T(8,128)(2,1)S(1)}, u32[]{:S(2)}) copy-start(bf16[1024,128]{1,0:T(8,128)(2,1)S(1)} %collective-permute-done.1.refs_2_) | copy-start | bytes 786436
  24.9 6.7 %collective-permute-start.3 = (bf16[1024,128]{1,0:T(8,128)(2,1)S(1)}, bf16[1024,128]{1,0:T(8,128)(2,1)}, u32[]{:S(2)}, u32[]{:S(2)}) collective-permute-start(bf16[1024,128]{1,0:T(8,128)(2,1)S(1)} %collective-permute-done.1.refs_2_), channel_id=1, source_target_pairs={{0,7},{1,0},{2,1},{3,2},{4,3},{5,4},{6,5},{7,6},{8,15},{9,8},{10,9... | collective-permute-start | bytes 786440 | tf_op jit(solution)/shard_map/ppermute | solution.py:304
  35.3 10.1 %copy-start.5 = (bf16[8,32,2048]{2,1,0:T(8,128)(2,1)}, bf16[8,32,2048]{2,1,0:T(8,128)(2,1)S(1)}, u32[]{:S(2)}) copy-start(bf16[8,32,2048]{2,1,0:T(8,128)(2,1)S(1)} %collective-permute-done.4.refs_10_) | copy-start | bytes 3145732
  35.4 15.3 %collective-permute-start.10 = (bf16[8,32,1024]{2,1,0:T(8,128)(2,1)S(1)}, bf16[8,32,1024]{2,1,0:T(8,128)(2,1)}, u32[]{:S(2)}, u32[]{:S(2)}) collective-permute-start(bf16[8,32,1024]{2,1,0:T(8,128)(2,1)S(1)} %slice.14), channel_id=1, source_target_pairs={{0,16},{16,32},{32,48},{48,0},{1,17},{17,33},{33,49},{49,1},{2,18}... | collective-permute-start | bytes 1572872 | tf_op jit(solution)/shard_map/ppermute | solution.py:309
  35.5 6.6 %collective-permute-start.6 = (bf16[1024,128]{1,0:T(8,128)(2,1)}, bf16[1024,128]{1,0:T(8,128)(2,1)S(1)}, u32[]{:S(2)}, u32[]{:S(2)}) collective-permute-start(bf16[1024,128]{1,0:T(8,128)(2,1)} %collective-permute-done.2.refs_3_), channel_id=1, source_target_pairs={{0,1},{1,2},{2,3},{3,4},{4,5},{5,6},{6,7},{7,0},{8,9},{9,10},{10,1... | collective-permute-start | bytes 786440 | tf_op jit(solution)/shard_map/ppermute | solution.py:312
  38.3 7.0 %collective-permute-start.7 = (bf16[1024,128]{1,0:T(8,128)(2,1)}, bf16[1024,128]{1,0:T(8,128)(2,1)S(1)}, u32[]{:S(2)}, u32[]{:S(2)}) collective-permute-start(bf16[1024,128]{1,0:T(8,128)(2,1)} %collective-permute-done.3.refs_4_), channel_id=1, source_target_pairs={{0,7},{1,0},{2,1},{3,2},{4,3},{5,4},{6,5},{7,6},{8,15},{9,8},{10,9... | collective-permute-start | bytes 786440 | tf_op jit(solution)/shard_map/ppermute | solution.py:312
  39.4 23.9 %collective-permute-start.12 = (bf16[8,32,1024]{2,1,0:T(8,128)(2,1)S(1)}, bf16[8,32,1024]{2,1,0:T(8,128)(2,1)}, u32[]{:S(2)}, u32[]{:S(2)}) collective-permute-start(bf16[8,32,1024]{2,1,0:T(8,128)(2,1)S(1)} %slice.15), channel_id=1, source_target_pairs={{0,48},{16,0},{32,16},{48,32},{1,49},{17,1},{33,17},{49,33},{2,50}... | collective-permute-start | bytes 1572872 | tf_op jit(solution)/shard_map/ppermute | solution.py:310
  42.1 8.7 %copy-start.6 = (bf16[1024,128]{1,0:T(8,128)(2,1)}, bf16[1024,128]{1,0:T(8,128)(2,1)S(1)}, u32[]{:S(2)}) copy-start(bf16[1024,128]{1,0:T(8,128)(2,1)S(1)} %collective-permute-done.6.refs_5_) | copy-start | bytes 786436
  42.1 4.9 %collective-permute-start.8 = (bf16[512,128]{1,0:T(8,128)(2,1)S(1)}, bf16[512,128]{1,0:T(8,128)(2,1)S(1)}, u32[]{:S(2)}, u32[]{:S(2)}) collective-permute-start(bf16[512,128]{1,0:T(8,128)(2,1)S(1)} %slice.16), channel_id=1, source_target_pairs={{0,1},{1,2},{2,3},{3,4},{4,5},{5,6},{6,7},{7,0},{8,9},{9,10},{10,1... | collective-permute-start | bytes 393224 | tf_op jit(solution)/shard_map/ppermute | solution.py:315
  45.3 5.4 %copy-start.7 = (bf16[1024,128]{1,0:T(8,128)(2,1)}, bf16[1024,128]{1,0:T(8,128)(2,1)S(1)}, u32[]{:S(2)}) copy-start(bf16[1024,128]{1,0:T(8,128)(2,1)S(1)} %collective-permute-done.7.refs_6_) | copy-start | bytes 786436
  45.4 5.3 %collective-permute-start.9 = (bf16[512,128]{1,0:T(8,128)(2,1)S(1)}, bf16[512,128]{1,0:T(8,128)(2,1)S(1)}, u32[]{:S(2)}, u32[]{:S(2)}) collective-permute-start(bf16[512,128]{1,0:T(8,128)(2,1)S(1)} %slice.17), channel_id=1, source_target_pairs={{0,7},{1,0},{2,1},{3,2},{4,3},{5,4},{6,5},{7,6},{8,15},{9,8},{10,9... | collective-permute-start | bytes 393224 | tf_op jit(solution)/shard_map/ppermute | solution.py:316
  47.0 3.8 %copy-start.11 = (bf16[512,128]{1,0:T(8,128)(2,1)}, bf16[512,128]{1,0:T(8,128)(2,1)S(1)}, u32[]{:S(2)}) copy-start(bf16[512,128]{1,0:T(8,128)(2,1)S(1)} %collective-permute-done.8.refs_7_) | copy-start | bytes 393220
  50.7 0.7 copy-start.12
  58.0 12.2 %copy-start.8 = (s32[1,128]{1,0:T(1,128)S(1)}, s32[1,128]{1,0:T(1,128)}, u32[]{:S(2)}) copy-start(s32[1,128]{1,0:T(1,128)} %param.13) | copy-start | bytes 1540
  58.0 14.9 %copy-start = (bf16[64,32,256]{2,1,0:T(8,128)(2,1)S(1)}, bf16[64,32,256]{2,1,0:T(8,128)(2,1)}, u32[]{:S(2)}) copy-start(bf16[64,32,256]{2,1,0:T(8,128)(2,1)} %get-tuple-element.27.refs_0_) | copy-start | bytes 3145732
  58.0 13.0 %collective-permute-start.11 = (bf16[64,32,256]{2,1,0:T(8,128)(2,1)}, bf16[64,32,256]{2,1,0:T(8,128)(2,1)S(1)}, u32[]{:S(2)}, u32[]{:S(2)}) collective-permute-start(bf16[64,32,256]{2,1,0:T(8,128)(2,1)} %get-tuple-element.28), channel_id=1, source_target_pairs={{0,8},{8,0},{1,9},{9,1},{2,10},{10,2},{3,11},{11,3},{4,12},{12,4},... | collective-permute-start | bytes 3145736 | tf_op jit(solution)/shard_map/ppermute | solution.py:344
  69.9 2.9 %collective-permute-start.13 = (bf16[64,32,256]{2,1,0:T(8,128)(2,1)}, bf16[64,32,256]{2,1,0:T(8,128)(2,1)S(1)}, u32[]{:S(2)}, u32[]{:S(2)}) collective-permute-start(bf16[64,32,256]{2,1,0:T(8,128)(2,1)} %get-tuple-element.30), channel_id=1, source_target_pairs={{0,8},{8,0},{1,9},{9,1},{2,10},{10,2},{3,11},{11,3},{4,12},{12,4},... | collective-permute-start | bytes 3145736 | tf_op jit(solution)/shard_map/ppermute | solution.py:344
  72.8 1.2 copy-start.1
  76.8 42.5 %all-to-all-start.1 = ((bf16[32,5,32,256]{3,2,1,0:T(8,128)(2,1)}), bf16[32,5,32,256]{3,2,1,0:T(8,128)(2,1)S(1)}, u32[]{:S(2)}, u32[]{:S(2)}) async-start(bf16[32,5,32,256]{3,2,1,0:T(8,128)(2,1)} %bitcast.3), calls=%async_computation.1 | async-start | bytes 5242880 | tf_op jit(solution)/shard_map/all_to_all | solution.py:288
  119.3 1.5 copy-start.4
  147.9 15.8 %all-to-all-start.3 = ((bf16[32,4,16,128]{3,2,1,0:T(8,128)(2,1)}), bf16[32,4,16,128]{3,2,1,0:T(8,128)(2,1)S(1)}, u32[]{:S(2)}, u32[]{:S(2)}) async-start(bf16[32,4,16,128]{3,2,1,0:T(8,128)(2,1)} %bitcast.5), calls=%async_computation.3 | async-start | bytes 1048576 | tf_op jit(solution)/shard_map/all_to_all | solution.py:288

commit v3 on v2

v3 whole, which is shorter than its diff:
```python
import jax
import jax.numpy as jnp
from jax import lax
from jax.experimental import pallas as pl
from jax.experimental.pallas import tpu as pltpu
from jax.sharding import Mesh
from jax.sharding import PartitionSpec as P

BLOCK = 256
TILE_ROWS = 16
TILE_COLS = 128
Y, X, CORE = 4, 4, 2
N_DP = Y * X * CORE
N_TENSOR = 8
ROW = X * CORE
STRIP = BLOCK // ROW
SLOTS = 5
HOME = 4
NBLK = 128
ROW_BLOCKS = 16
COL_BLOCKS = 8
TOK_SUB = 32
LOCAL_ROWS = ROW_BLOCKS * STRIP
DP = ("y", "x", "core")
SHARD_K = ROW * TOK_SUB
SOURCES = ((0, 0), (0, 1), (-1, 0), (-1, 1), (1, 0), (1, 1), (2, 0), (2, 1))
WIDE = 2
CHUNK_K = NBLK // 2

factor_decay = 0.9
first_decay = 0.95
second_decay = 0.95
epsilon_value = 1e-08

MIB = 1024 * 1024
SMEM = pl.BlockSpec(memory_space=pltpu.SMEM)
VMEM = pl.BlockSpec(memory_space=pltpu.VMEM)


def params(mib):
    return pltpu.CompilerParams(vmem_limit_bytes=mib * MIB)


def tile_of(m):
    y, strip = m // ROW, m % ROW
    top, side = STRIP * strip + TILE_ROWS * (y // 2), TILE_COLS * (y % 2)
    return slice(top, top + TILE_ROWS), slice(side, side + TILE_COLS)


def cut_kernel(tokens, out):
    for strip in range(ROW):
        out[strip] = jnp.concatenate(
            [
                tokens[:, r * BLOCK + STRIP * strip : r * BLOCK + STRIP * (strip + 1)]
                for r in range(ROW_BLOCKS)
            ],
            axis=1,
        )


def cut_tokens(tokens):
    return pl.pallas_call(
        cut_kernel,
        out_shape=jax.ShapeDtypeStruct((ROW, TOK_SUB, LOCAL_ROWS), jnp.bfloat16),
        compiler_params=params(32),
        name="cut_tokens",
    )(tokens)


def turn_kernel(spot, pieces, out):
    places = [
        (spot[1] + dx + X) % X * CORE + (spot[2] + dc) % CORE for dx, dc in SOURCES
    ]
    out[...] = jnp.concatenate([pieces[place] for place in places], axis=0).T


def turn(spot, pieces):
    return pl.pallas_call(
        turn_kernel,
        in_specs=[SMEM, VMEM],
        out_shape=jax.ShapeDtypeStruct((LOCAL_ROWS, SHARD_K), jnp.bfloat16),
        compiler_params=params(32),
        name="turn",
    )(spot, pieces)


def gradient_kernel(spot, *refs):
    whole, halves, sources = refs[:7], refs[7:9], refs[9:17]
    outs, (left, right, tiles) = refs[17:21], refs[21:]

    @pl.when(pl.program_id(0) == 0)
    def join_tokens():
        for j in range(7):
            left[:, j * SHARD_K : (j + 1) * SHARD_K] = whole[j][...]
        middle = 7 * SHARD_K + SHARD_K // 2
        left[:, 7 * SHARD_K : middle] = halves[0][...]
        left[:, middle:] = halves[1][...]

    for j, step in enumerate((0, -1, 1, -2, 2, -3, 3, 4)):
        place = (spot[3] + step + N_TENSOR) % N_TENSOR
        for i in range(ROW):
            top = j * SHARD_K + i * TOK_SUB
            right[top : top + TOK_SUB] = sources[i][place]
    for column in range(WIDE):
        result = jnp.dot(
            left[...], right[:, column * BLOCK : (column + 1) * BLOCK],
            preferred_element_type=jnp.float32,
        ).astype(jnp.bfloat16)
        for r in range(ROW_BLOCKS):
            for y in range(Y):
                rows, cols = tile_of(y * ROW)
                top = r * STRIP + rows.start
                tiles[y, column * ROW_BLOCKS + r] = result[top : top + TILE_ROWS, cols]
    for step in range(Y):
        outs[step][...] = tiles[(spot[0] + step) % Y]


def gradient_tiles(chunk, spot, lefts, near, far):
    resident = lambda a: pl.BlockSpec(a.shape, lambda c, spot: (0, 0))
    steps = COL_BLOCKS // 2 // WIDE
    blocks = WIDE * ROW_BLOCKS
    shape = (N_TENSOR, TOK_SUB, WIDE * BLOCK)
    near_spec = pl.BlockSpec(shape, lambda c, spot: (0, 0, steps * chunk + c))
    far_spec = pl.BlockSpec(shape, lambda c, spot: (0, 0, c))
    part = pl.BlockSpec((blocks, TILE_ROWS, TILE_COLS), lambda c, spot: (c, 0, 0))
    return pl.pallas_call(
        gradient_kernel,
        grid_spec=pltpu.PrefetchScalarGridSpec(
            num_scalar_prefetch=1,
            grid=(steps,),
            in_specs=[resident(a) for a in lefts] + [near_spec] * 6 + [far_spec] * 2,
            out_specs=[part] * Y,
            scratch_shapes=[
                pltpu.VMEM((LOCAL_ROWS, N_TENSOR * SHARD_K), jnp.bfloat16),
                pltpu.VMEM((N_TENSOR * SHARD_K, WIDE * BLOCK), jnp.bfloat16),
                pltpu.VMEM((Y, blocks, TILE_ROWS, TILE_COLS), jnp.bfloat16),
            ],
        ),
        out_shape=[jax.ShapeDtypeStruct((CHUNK_K, TILE_ROWS, TILE_COLS), jnp.bfloat16)] * Y,
        compiler_params=params(60),
        cost_estimate=pl.CostEstimate(
            flops=2 * LOCAL_ROWS * N_TENSOR * SHARD_K * 4 * BLOCK,
            bytes_accessed=8 * MIB, transcendentals=0,
        ),
        name="gradient_tiles",
    )(spot, *lefts, *near, *far)


def to_slots_kernel(slot, *refs):
    out = refs[-1]
    out[...] = jnp.zeros_like(out)
    for chunk in range(2):
        mine, *others = refs[Y * chunk : Y * (chunk + 1)]

        def body(k, carry):
            total = mine[k].astype(jnp.float32)
            for part in others:
                total = total + part[k].astype(jnp.float32)
            out[slot[chunk * CHUNK_K + k]] = total.astype(jnp.bfloat16)
            return carry

        lax.fori_loop(0, CHUNK_K, body, 0, unroll=8)


def to_slots(slot, parts):
    return pl.pallas_call(
        to_slots_kernel,
        in_specs=[SMEM] + [VMEM] * len(parts),
        out_shape=jax.ShapeDtypeStruct((N_DP * SLOTS, TILE_ROWS, TILE_COLS), jnp.bfloat16),
        compiler_params=params(32),
        name="to_slots",
    )(slot, *parts)


def from_slots_kernel(slot, tiles, out):
    def body(k, carry):
        out[k] = tiles[slot[k]]
        return carry

    lax.fori_loop(0, NBLK, body, 0, unroll=8)


def from_slots(slot, tiles):
    return pl.pallas_call(
        from_slots_kernel,
        grid_spec=pltpu.PrefetchScalarGridSpec(
            num_scalar_prefetch=1,
            grid=(1,),
            in_specs=[pl.BlockSpec(tiles.shape, lambda i, slot: (0, 0, 0))],
            out_specs=pl.BlockSpec((NBLK, TILE_ROWS, TILE_COLS), lambda i, slot: (0, 0, 0)),
        ),
        out_shape=jax.ShapeDtypeStruct((NBLK, TILE_ROWS, TILE_COLS), jnp.bfloat16),
        compiler_params=params(40),
        name="from_slots",
    )(slot, tiles)


def assemble_kernel(tiles, out):
    for h in range(HOME):
        for m in range(N_DP):
            rows, cols = tile_of(m)
            out[0, h, rows, cols] = tiles[m, h]


def assemble(tiles):
    return pl.pallas_call(
        assemble_kernel,
        out_shape=jax.ShapeDtypeStruct((1, HOME, BLOCK, BLOCK), jnp.bfloat16),
        compiler_params=params(32),
        name="assemble",
    )(tiles)


def dot(a, b, ca, cb):
    return lax.dot_general(a, b, (((ca,), (cb,)), ((), ())), preferred_element_type=jnp.float32)


def update_kernel(
    live, tiles, basis_left, basis_right, first, second,
    update, grads, first_new, second_new,
):
    for s in range(SLOTS):
        for m in range(N_DP):
            rows, cols = tile_of(m)
            grads[s, rows, cols] = tiles[m, s]
        grad = grads[s]
        ql, qr = basis_left[0, s], basis_right[0, s]
        halfway = dot(ql, grad, 0, 0).astype(jnp.bfloat16)
        rotated = dot(halfway, qr, 1, 0)
        first_old, second_old = first[0, s], second[0, s]
        first_float = first_decay * first_old.astype(jnp.float32) + (1.0 - first_decay) * rotated
        second_float = (
            second_decay * second_old.astype(jnp.float32)
            + (1.0 - second_decay) * rotated * rotated
        )
        ratio = (first_float / (jnp.sqrt(second_float) + epsilon_value)).astype(jnp.bfloat16)
        turned = dot(ql, ratio, 1, 0).astype(jnp.bfloat16)
        result = dot(turned, qr, 1, 1).astype(jnp.bfloat16)
        for m in range(N_DP):
            rows, cols = tile_of(m)
            update[m, s] = result[rows, cols]
        alive = live[s] > 0
        first_new[0, s] = jnp.where(alive, first_float.astype(jnp.bfloat16), first_old)
        second_new[0, s] = jnp.where(alive, second_float.astype(jnp.bfloat16), second_old)


def update_blocks(live, tiles, basis_left, basis_right, first, second):
    like = lambda a: jax.ShapeDtypeStruct(a.shape, a.dtype)
    return pl.pallas_call(
        update_kernel,
        in_specs=[SMEM] + [VMEM] * 5,
        out_shape=[
            like(tiles),
            jax.ShapeDtypeStruct((SLOTS, BLOCK, BLOCK), jnp.bfloat16),
            like(first),
            like(second),
        ],
        compiler_params=params(60),
        name="update",
    )(live, tiles, basis_left, basis_right, first, second)


def factor_kernel(live, grads, left, right, left_new, right_new):
    alive = live[pl.program_id(0)] > 0
    grad = grads[0]
    scale = (1.0 - factor_decay) / BLOCK
    left_old, right_old = left[0, 0], right[0, 0]
    left_new[0, 0] = jnp.where(
        alive, factor_decay * left_old + scale * dot(grad, grad, 1, 1), left_old
    )
    right_new[0, 0] = jnp.where(
        alive, factor_decay * right_old + scale * dot(grad, grad, 0, 0), right_old
    )


def update_factors(live, grads, left, right):
    state = pl.BlockSpec((1, 1, BLOCK, BLOCK), lambda s, live: (0, s, 0, 0))
    return pl.pallas_call(
        factor_kernel,
        grid_spec=pltpu.PrefetchScalarGridSpec(
            num_scalar_prefetch=1,
            grid=(SLOTS,),
            in_specs=[pl.BlockSpec((1, BLOCK, BLOCK), lambda s, live: (s, 0, 0))] + [state] * 2,
            out_specs=[state] * 2,
        ),
        out_shape=[jax.ShapeDtypeStruct(a.shape, a.dtype) for a in (left, right)],
        compiler_params=params(60),
        cost_estimate=pl.CostEstimate(
            flops=4 * SLOTS * BLOCK**3, bytes_accessed=6 * MIB, transcendentals=0
        ),
        name="factors",
    )(live, grads, left, right)


def spread(array, axes):
    return lax.all_to_all(array, axes, split_axis=0, concat_axis=0, tiled=True)


def ring(size, step):
    return [(i, (i + step) % size) for i in range(size)]


def gather_row(spot, tokens, grads):
    up, down, swap = ring(N_TENSOR, 1), ring(N_TENSOR, -1), ring(CORE, 1)
    ahead, back = ring(X, 1), ring(X, -1)
    across = lambda a: [a, lax.ppermute(a, "core", swap)]

    pieces, grads = lax.optimization_barrier(
        (spread(cut_tokens(tokens), ("x", "core")), grads)
    )
    behind, before = lax.ppermute(grads, "x", ahead), lax.ppermute(grads, "x", back)
    mine = turn(spot, pieces)
    below, above = lax.ppermute(mine, "z", up), lax.ppermute(mine, "z", down)
    whole = [mine, below, above]
    near = across(grads)
    below, above = lax.ppermute(below, "z", up), lax.ppermute(above, "z", down)
    whole += [below, above]
    behind, before, below, above = lax.optimization_barrier((behind, before, below, above))
    half = grads.shape[-1] // 2
    first = lax.ppermute(behind[..., :half], "x", ahead)
    last = lax.ppermute(before[..., half:], "x", back)
    below, above = lax.ppermute(below, "z", up), lax.ppermute(above, "z", down)
    whole += [below, above]
    near += across(behind) + across(before)
    half = mine.shape[1] // 2
    halves = [
        lax.ppermute(below[:, :half], "z", up),
        lax.ppermute(above[:, half:], "z", down),
    ]
    return whole + halves, near, (across(first), across(last))


def sum_parts(parts):
    return [parts[0]] + [lax.ppermute(parts[step], "y", ring(Y, step)) for step in (2, 1, 3)]


def local(
    tokens, grad_out, owner, left_factor, right_factor,
    left_basis, right_basis, first_moment, second_moment,
):
    owner_row = owner[0]
    block_ids = jnp.arange(NBLK, dtype=jnp.int32)
    same = owner_row[:, None] == owner_row[None, :]
    before = block_ids[None, :] < block_ids[:, None]
    rank = jnp.sum((same & before).astype(jnp.int32), axis=1)
    slot = owner_row * SLOTS + rank
    held = jnp.sum((owner_row == lax.axis_index(DP)).astype(jnp.int32))
    live = (jnp.arange(SLOTS, dtype=jnp.int32) < held).astype(jnp.int32)

    spot = jnp.stack([lax.axis_index(axis) for axis in (*DP, "z")]).astype(jnp.int32)
    grads = grad_out.reshape(N_TENSOR, TOK_SUB, grad_out.shape[1])
    lefts, near, far = gather_row(spot, tokens, grads)
    parts = []
    for chunk in range(2):
        parts += sum_parts(gradient_tiles(chunk, spot, lefts, near, far[chunk]))
    tiles = to_slots(slot, parts).reshape(N_DP, SLOTS, TILE_ROWS, TILE_COLS)
    update, grad_blocks, first_new, second_new = update_blocks(
        live, spread(tiles, DP), left_basis, right_basis, first_moment, second_moment
    )
    left_new, right_new = update_factors(live, grad_blocks, left_factor, right_factor)
    back = spread(update, DP).reshape(N_DP * SLOTS, TILE_ROWS, TILE_COLS)
    picked = from_slots(slot, back).reshape(N_DP, HOME, TILE_ROWS, TILE_COLS)
    home_update = assemble(spread(picked, DP))
    return (home_update, left_new, right_new, first_new, second_new)


def solution(mesh):
    split = Mesh(mesh.devices.reshape(Y, X, CORE, N_TENSOR), ("y", "x", "core", "z"))
    state = P("z", DP, None, None)
    return jax.shard_map(
        local,
        mesh=split,
        in_specs=(P((*DP, "z"), None), P(DP, "z"), P("z", None)) + (state,) * 6,
        out_specs=(state,) * 5,
        check_vma=False,
    )
```

time: 165 us -> 170 us (1.030); the launches traced: 164 us -> 167 us
  starting transfers between devices: 36.2 us -> 47 us
  waiting for transfers between devices: 58.4 us -> 53.8 us
    all_to_all x2, waiting for transfers between devices: 37.9 us -> 17.2 us  [spread(): return lax.all_to_all(array, axes, split_axis=0, concat_axis=0, tiled=True)]
    ppermute x6 -> x15, waiting for transfers between devices: 6.53 us -> 18.7 us  [the longest x6 7.33 us: sum_parts(): lax.ppermute(parts[step], 'y', ring(Y, step))]
    ppermute x6 -> x15, starting transfers between devices: 11.3 us -> 19.8 us  [the longest x6 8.53 us: sum_parts(): lax.ppermute(parts[step], 'y', ring(Y, step))]
    ppermute x2, waiting for transfers between devices: 3.31 us -> 7.47 us  [gather_row(): lax.ppermute(below, 'z', up)]
    ppermute x1, waiting for transfers between devices: 3.66 us -> 0.01 us  [gather_row(): lax.ppermute(grads, 'x', ahead)]
    ppermute x2, waiting for transfers between devices: 3.32 us -> 5.74 us  [gather_row(): below, above = (lax.ppermute(mine, 'z', up), lax.ppermute(mine, 'z', down))]
    all_to_all x2, starting transfers between devices: 13 us -> 15.3 us  [spread(): return lax.all_to_all(array, axes, split_axis=0, concat_axis=0, tiled=True)]
    unnamed x28 -> x40, local copies, waits for them, and re-layouts: 4.35 us -> 4.4 us
  transfers between devices with their start and end apart: 16 -> 25, of which waited for: 10 -> 13; matrix products, arithmetic and copies ran while one was open for 3% -> 1% of each run, Pallas kernels for 12% -> 12%
where the time goes in v3:
time: 170 us; the launch traced here: 167 us
  waiting for transfers between devices  53.8 us (32%)
  starting transfers between devices  47 us (28%)
  Pallas kernels  30.6 us (18%)
  blocking collectives  28.4 us (17%)
  local copies, waits for them, and re-layouts  4.5 us (3%)
  other arithmetic  2.1 us (1%)
    all_to_all x2, blocking collectives, spread(): return lax.all_to_all(array, axes, split_axis=0, concat_axis=0, tiled=True)  28.4 us
    all_to_all x2, waiting for transfers between devices, spread(): return lax.all_to_all(array, axes, split_axis=0, concat_axis=0, tiled=True)  17.2 us
    all_to_all x2, starting transfers between devices, spread(): return lax.all_to_all(array, axes, split_axis=0, concat_axis=0, tiled=True)  15.3 us
    pallas_call x2, Pallas kernels, gradient_tiles(): pl.pallas_call(gradient_kernel, grid_spec=pltpu.PrefetchScalarGridSpec(nu...  13.7 us
    ppermute x6, starting transfers between devices, sum_parts(): lax.ppermute(parts[step], 'y', ring(Y, step))  8.53 us
    ppermute x2, waiting for transfers between devices, gather_row(): lax.ppermute(below, 'z', up)  7.47 us
    ppermute x6, waiting for transfers between devices, sum_parts(): lax.ppermute(parts[step], 'y', ring(Y, step))  7.33 us
    ppermute x5, starting transfers between devices, gather_row(): across = lambda a: [a, lax.ppermute(a, 'core', swap)]  7.24 us
  transfers between devices with their start and end apart: 25, of which 13 were waited for; matrix products, arithmetic and copies ran while one was open for 1% of the time, Pallas kernels for 12%

profile of v3, /device:TPU:97, one launch (start us, length us, event | category | flops | bytes accessed | tf_op | source)
XLA Modules:
  0.0 167.3 jit_solution(15284516138162993705)
XLA Ops:
  0.6 0.9 copy-done.3
  1.6 0.3 cut_tokens.1
  1.9 11.3 %all_to_all.20.pieces = bf16[8,32,512]{2,1,0:T(8,128)(2,1)S(1)} all-to-all(bf16[8,32,512]{2,1,0:T(8,128)(2,1)S(1)} %cut_tokens.1), channel_id=1, replica_groups=mesh['y'=4,'x'=4,'core'=2,'z'=8] {'x','core'}, dimensions={0} | all-to-all | bytes 524288 | tf_op jit(solution)/shard_map/all_to_all | solution.py:296
  13.1 0.3 collective-permute-start.4
  13.4 2.4 %collective-permute-start.5 = (bf16[8,32,2048]{2,1,0:T(8,128)(2,1)}, bf16[8,32,2048]{2,1,0:T(8,128)(2,1)S(1)}, u32[]{:S(2)}, u32[]{:S(2)}) collective-permute-start(bf16[8,32,2048]{2,1,0:T(8,128)(2,1)} %bitcast.13), channel_id=1, source_target_pairs={{0,48},{16,0},{32,16},{48,32},{1,49},{17,1},{33,17},{49,33},{2,50}... | collective-permute-start | bytes 3145736 | tf_op jit(solution)/shard_map/ppermute | solution.py:311
  15.8 1.6 collective-permute-start.10
  17.4 0.1 pad_add_fusion.spot
  17.5 0.7 turn.1.refs_0_
  18.2 0.0 copy-start
  18.2 2.9 %collective-permute-start = (bf16[512,256]{1,0:T(8,128)(2,1)S(1)}, bf16[512,256]{1,0:T(8,128)(2,1)S(1)}, u32[]{:S(2)}, u32[]{:S(2)}) collective-permute-start(bf16[512,256]{1,0:T(8,128)(2,1)S(1)} %turn.1.refs_0_), channel_id=1, source_target_pairs={{0,1},{1,2},{2,3},{3,4},{4,5},{5,6},{6,7},{7,0},{8,9},{9,10},{10,1... | collective-permute-start | bytes 786440 | tf_op jit(solution)/shard_map/ppermute | solution.py:313
  21.1 0.0 collective-permute-start.1
  21.1 5.7 %collective-permute-done.refs_1_ = bf16[512,256]{1,0:T(8,128)(2,1)S(1)} collective-permute-done((bf16[512,256]{1,0:T(8,128)(2,1)S(1)}, bf16[512,256]{1,0:T(8,128)(2,1)S(1)}, u32[]{:S(2)}, u32[]{:S(2)}) %collective-permute-start) | collective-permute-done | bytes 262176 | tf_op jit(solution)/shard_map/ppermute | solution.py:313
  26.8 3.4 %collective-permute-start.2 = (bf16[512,256]{1,0:T(8,128)(2,1)S(1)}, bf16[512,256]{1,0:T(8,128)(2,1)S(1)}, u32[]{:S(2)}, u32[]{:S(2)}) collective-permute-start(bf16[512,256]{1,0:T(8,128)(2,1)S(1)} %collective-permute-done.refs_1_), channel_id=1, source_target_pairs={{0,1},{1,2},{2,3},{3,4},{4,5},{5,6},{6,7},{7,0},{8,9},{9,10},{10,1... | collective-permute-start | bytes 786440 | tf_op jit(solution)/shard_map/ppermute | solution.py:316
  30.2 0.0 collective-permute-done.1.refs_2_
  30.3 0.0 collective-permute-start.3
  30.3 4.8 %collective-permute-done.2.refs_3_ = bf16[512,256]{1,0:T(8,128)(2,1)S(1)} collective-permute-done((bf16[512,256]{1,0:T(8,128)(2,1)S(1)}, bf16[512,256]{1,0:T(8,128)(2,1)S(1)}, u32[]{:S(2)}, u32[]{:S(2)}) %collective-permute-start.2) | collective-permute-done | bytes 262176 | tf_op jit(solution)/shard_map/ppermute | solution.py:316
  35.1 3.1 %collective-permute-done.3.refs_4_ = bf16[512,256]{1,0:T(8,128)(2,1)S(1)} collective-permute-done((bf16[512,256]{1,0:T(8,128)(2,1)S(1)}, bf16[512,256]{1,0:T(8,128)(2,1)S(1)}, u32[]{:S(2)}, u32[]{:S(2)}) %collective-permute-start.3) | collective-permute-done | bytes 262176 | tf_op jit(solution)/shard_map/ppermute | solution.py:316
  38.2 0.0 collective-permute-done.4.refs_11_
  38.2 0.0 copy-start.5
  38.3 2.1 %collective-permute-start.11 = (bf16[8,32,2048]{2,1,0:T(8,128)(2,1)S(1)}, bf16[8,32,2048]{2,1,0:T(8,128)(2,1)S(1)}, u32[]{:S(2)}, u32[]{:S(2)}) collective-permute-start(bf16[8,32,2048]{2,1,0:T(8,128)(2,1)S(1)} %collective-permute-done.4.refs_11_), channel_id=1, source_target_pairs={{0,8},{8,0},{1,9},{9,1},{2,10},{10,2},{3,11},{11,3},{4,12},{12,4},... | collective-permute-start | bytes 3145736 | tf_op jit(solution)/shard_map/ppermute | solution.py:306
  40.4 0.1 collective-permute-start.12
  40.5 0.1 collective-permute-start.13
  40.6 2.8 %collective-permute-start.6 = (bf16[512,256]{1,0:T(8,128)(2,1)S(1)}, bf16[512,256]{1,0:T(8,128)(2,1)S(1)}, u32[]{:S(2)}, u32[]{:S(2)}) collective-permute-start(bf16[512,256]{1,0:T(8,128)(2,1)S(1)} %collective-permute-done.2.refs_3_), channel_id=1, source_target_pairs={{0,1},{1,2},{2,3},{3,4},{4,5},{5,6},{6,7},{7,0},{8,9},{9,10},{10,1... | collective-permute-start | bytes 786440 | tf_op jit(solution)/shard_map/ppermute | solution.py:322
  43.5 0.0 collective-permute-done.10.refs_10_
  43.5 2.7 %collective-permute-start.18 = (bf16[8,32,1024]{2,1,0:T(8,128)(2,1)S(1)}, bf16[8,32,1024]{2,1,0:T(8,128)(2,1)}, u32[]{:S(2)}, u32[]{:S(2)}) collective-permute-start(bf16[8,32,1024]{2,1,0:T(8,128)(2,1)S(1)} %slice.15), channel_id=1, source_target_pairs={{0,48},{16,0},{32,16},{48,32},{1,49},{17,1},{33,17},{49,33},{2,50}... | collective-permute-start | bytes 1572872 | tf_op jit(solution)/shard_map/ppermute | solution.py:321
  46.1 2.6 %collective-permute-done.6.refs_5_ = bf16[512,256]{1,0:T(8,128)(2,1)S(1)} collective-permute-done((bf16[512,256]{1,0:T(8,128)(2,1)S(1)}, bf16[512,256]{1,0:T(8,128)(2,1)S(1)}, u32[]{:S(2)}, u32[]{:S(2)}) %collective-permute-start.6) | collective-permute-done | bytes 262176 | tf_op jit(solution)/shard_map/ppermute | solution.py:322
  48.8 0.0 collective-permute-start.7
  48.8 6.1 %collective-permute-done.13.refs_15_ = bf16[8,32,1024]{2,1,0:T(8,128)(2,1)S(1)} collective-permute-done((bf16[8,32,1024]{2,1,0:T(8,128)(2,1)S(1)}, bf16[8,32,1024]{2,1,0:T(8,128)(2,1)S(1)}, u32[]{:S(2)}, u32[]{:S(2)}) %collective-permute-start.13) | collective-permute-done | bytes 524320 | tf_op jit(solution)/shard_map/ppermute | solution.py:320
  54.8 1.3 collective-permute-start.14
  56.1 1.5 collective-permute-done.7.refs_6_
  57.7 1.3 collective-permute-start.8
  59.0 0.0 collective-permute-done.18.refs_15_
  59.0 2.2 %collective-permute-start.19 = (bf16[8,32,1024]{2,1,0:T(8,128)(2,1)}, bf16[8,32,1024]{2,1,0:T(8,128)(2,1)}, u32[]{:S(2)}, u32[]{:S(2)}) collective-permute-start(bf16[8,32,1024]{2,1,0:T(8,128)(2,1)} %collective-permute-done.18.refs_15_), channel_id=1, source_target_pairs={{0,8},{8,0},{1,9},{9,1},{2,10},{10,2},{3,11},{11,3},{4,12},{12,4},... | collective-permute-start | bytes 1572872 | tf_op jit(solution)/shard_map/ppermute | solution.py:306
  61.2 0.3 collective-permute-done.8.refs_7_
  61.5 0.0 collective-permute-start.9
  61.5 5.0 %collective-permute-done.9.refs_8_ = bf16[512,128]{1,0:T(8,128)(2,1)S(1)} collective-permute-done((bf16[512,128]{1,0:T(8,128)(2,1)S(1)}, bf16[512,128]{1,0:T(8,128)(2,1)S(1)}, u32[]{:S(2)}, u32[]{:S(2)}) %collective-permute-start.9) | collective-permute-done | bytes 131104 | tf_op jit(solution)/shard_map/ppermute | solution.py:328
  66.5 0.6 copy-done.17
  67.2 1.0 copy-done.8
  68.2 6.9 %gradient_tiles.2 = (bf16[64,16,128]{2,1,0:T(8,128)(2,1)}, bf16[64,16,128]{2,1,0:T(8,128)(2,1)}, bf16[64,16,128]{2,1,0:T(8,128)(2,1)}, bf16[64,16,128]{2,1,0:T(8,128)(2,1)}) custom-call(s32[4]{0:T(128)} %copy-done.4, bf16[512,256]{1,0:T(8,128)(2,1)} %copy-done, bf16[512,256]{1,0:T(8,128)(2,1)} %copy-done.12, bf16[512,256]{1,0:T(8,128)(2,1)} %copy-done.13, ...), custom_call_target="tpu_custom_call" | custom-call | flops 2147483648 | bytes 8388608 | tf_op jit(solution)/shard_map/gradient_tiles/pallas_call | solution.py:126
  75.1 3.0 %collective-permute-start.15 = (bf16[64,16,128]{2,1,0:T(8,128)(2,1)}, bf16[64,16,128]{2,1,0:T(8,128)(2,1)S(1)}, u32[]{:S(2)}, u32[]{:S(2)}) collective-permute-start(bf16[64,16,128]{2,1,0:T(8,128)(2,1)} %get-tuple-element.32), channel_id=1, source_target_pairs={{0,128},{64,192},{128,0},{192,64},{1,129},{65,193},{129,1},{193,65... | collective-permute-start | bytes 786440 | tf_op jit(solution)/shard_map/ppermute | solution.py:334
  78.1 0.4 collective-permute-start.16
  78.5 2.3 %collective-permute-start.17 = (bf16[64,16,128]{2,1,0:T(8,128)(2,1)}, bf16[64,16,128]{2,1,0:T(8,128)(2,1)S(1)}, u32[]{:S(2)}, u32[]{:S(2)}) collective-permute-start(bf16[64,16,128]{2,1,0:T(8,128)(2,1)} %get-tuple-element.34), channel_id=1, source_target_pairs={{0,192},{64,0},{128,64},{192,128},{1,193},{65,1},{129,65},{193,129... | collective-permute-start | bytes 786440 | tf_op jit(solution)/shard_map/ppermute | solution.py:334
  80.8 6.8 %gradient_tiles.3 = (bf16[64,16,128]{2,1,0:T(8,128)(2,1)}, bf16[64,16,128]{2,1,0:T(8,128)(2,1)}, bf16[64,16,128]{2,1,0:T(8,128)(2,1)}, bf16[64,16,128]{2,1,0:T(8,128)(2,1)}) custom-call(s32[4]{0:T(128)} %copy-done.4, bf16[512,256]{1,0:T(8,128)(2,1)} %copy-done, bf16[512,256]{1,0:T(8,128)(2,1)} %copy-done.12, bf16[512,256]{1,0:T(8,128)(2,1)} %copy-done.13, ...), custom_call_target="tpu_custom_call" | custom-call | flops 2147483648 | bytes 8388608 | tf_op jit(solution)/shard_map/gradient_tiles/pallas_call | solution.py:126
  87.6 0.1 collective-permute-start.20
  87.7 0.7 collective-permute-start.21
  88.5 2.0 %collective-permute-start.22 = (bf16[64,16,128]{2,1,0:T(8,128)(2,1)}, bf16[64,16,128]{2,1,0:T(8,128)(2,1)S(1)}, u32[]{:S(2)}, u32[]{:S(2)}) collective-permute-start(bf16[64,16,128]{2,1,0:T(8,128)(2,1)} %get-tuple-element.38), channel_id=1, source_target_pairs={{0,192},{64,0},{128,64},{192,128},{1,193},{65,1},{129,65},{193,129... | collective-permute-start | bytes 786440 | tf_op jit(solution)/shard_map/ppermute | solution.py:334
  90.5 0.2 convert_reduce_fusion
  90.7 0.6 fusion.1
  91.3 3.4 %collective-permute-done.20.refs_5_ = bf16[64,16,128]{2,1,0:T(8,128)(2,1)S(1)} collective-permute-done((bf16[64,16,128]{2,1,0:T(8,128)(2,1)}, bf16[64,16,128]{2,1,0:T(8,128)(2,1)S(1)}, u32[]{:S(2)}, u32[]{:S(2)}) %collective-permute-start.20) | collective-permute-done | bytes 262176 | tf_op jit(solution)/shard_map/ppermute | solution.py:334
  94.8 3.4 %collective-permute-done.21.refs_6_ = bf16[64,16,128]{2,1,0:T(8,128)(2,1)S(1)} collective-permute-done((bf16[64,16,128]{2,1,0:T(8,128)(2,1)}, bf16[64,16,128]{2,1,0:T(8,128)(2,1)S(1)}, u32[]{:S(2)}, u32[]{:S(2)}) %collective-permute-start.21) | collective-permute-done | bytes 262176 | tf_op jit(solution)/shard_map/ppermute | solution.py:334
  98.1 0.5 collective-permute-done.22.refs_7_
  98.6 0.9 copy-done.2
  99.6 1.8 %to_slots.1 = bf16[160,16,128]{2,1,0:T(8,128)(2,1)} custom-call(s32[128]{0:T(128)S(1)} %get-tuple-element.46.slot, bf16[64,16,128]{2,1,0:T(8,128)(2,1)S(1)} %copy-done.1, bf16[64,16,128]{2,1,0:T(8,128)(2,1)S(1)} %collective-permute-done.15.refs_1_, bf16[64,16,128]{2,1,0:T(8,128)(2,1)S(1)} %collective-permute-done.16.refs_2_, ...), custom_call_target="tpu_custom_call" | custom-call | tf_op jit(solution)/shard_map/to_slots/pallas_call | solution.py:166
  101.4 11.2 %all-to-all-start.1 = ((bf16[32,5,16,128]{3,2,1,0:T(8,128)(2,1)}), bf16[32,5,16,128]{3,2,1,0:T(8,128)(2,1)S(1)}, u32[]{:S(2)}, u32[]{:S(2)}) async-start(bf16[32,5,16,128]{3,2,1,0:T(8,128)(2,1)} %bitcast.6), calls=%async_computation.1 | async-start | bytes 1310720 | tf_op jit(solution)/shard_map/all_to_all | solution.py:296
  112.6 1.2 compare_convert_fusion.live
  113.9 11.7 %all-to-all-done.1.tiles = bf16[32,5,16,128]{3,2,1,0:T(8,128)(2,1)S(1)} async-done(((bf16[32,5,16,128]{3,2,1,0:T(8,128)(2,1)}), bf16[32,5,16,128]{3,2,1,0:T(8,128)(2,1)S(1)}, u32[]{:S(2)}, u32[]{:S(2)}) %all-to-all-start.1) | async-done | bytes 655392 | tf_op jit(solution)/shard_map/all_to_all | solution.py:296
  125.6 0.8 copy-done.9
  126.4 5.6 %update.1 = (bf16[32,5,16,128]{3,2,1,0:T(8,128)(2,1)}, bf16[5,256,256]{2,1,0:T(8,128)(2,1)}, bf16[1,5,256,256]{3,2,1,0:T(8,128)(2,1)}, bf16[1,5,256,256]{3,2,1,0:T(8,128)(2,1)}) custom-call(s32[5]{0:T(128)} %compare_convert_fusion.live, bf16[32,5,16,128]{3,2,1,0:T(8,128)(2,1)} %copy-done.9, bf16[1,5,256,256]{3,2,1,0:T(8,128)(2,1)} %basis_left.1, ...), custom_call_target="tpu_custom_call" | custom-call | tf_op jit(solution)/shard_map/update/pallas_call | solution.py:249
  132.0 17.1 %all_to_all.21 = bf16[32,5,16,128]{3,2,1,0:T(8,128)(2,1)S(1)} all-to-all(bf16[32,5,16,128]{3,2,1,0:T(8,128)(2,1)} %get-tuple-element.39), channel_id=1, replica_groups=mesh['y'=4,'x'=4,'core'=2,'z'=8] {'y','x','core'}, dimensions={0} | all-to-all | bytes 1310720 | tf_op jit(solution)/shard_map/all_to_all | solution.py:296
  149.1 1.6 from_slots.1
  150.6 4.1 %all-to-all-start.3 = ((bf16[32,4,16,128]{3,2,1,0:T(8,128)(2,1)}), bf16[32,4,16,128]{3,2,1,0:T(8,128)(2,1)S(1)}, u32[]{:S(2)}, u32[]{:S(2)}) async-start(bf16[32,4,16,128]{3,2,1,0:T(8,128)(2,1)} %bitcast.8), calls=%async_computation.3 | async-start | bytes 1048576 | tf_op jit(solution)/shard_map/all_to_all | solution.py:296
  154.7 6.1 %factors.1 = (f32[1,5,256,256]{3,2,1,0:T(8,128)}, f32[1,5,256,256]{3,2,1,0:T(8,128)}) custom-call(s32[5]{0:T(128)} %compare_convert_fusion.live, bf16[5,256,256]{2,1,0:T(8,128)(2,1)} %get-tuple-element.40.grads, f32[1,5,256,256]{3,2,1,0:T(8,128)} %left.1, f32[1,5,256,256]{3,2,1,0:T(8,128)} %right.1), custom_call_target="tpu_custom_call" | custom-call | flops 335544320 | bytes 6291456 | tf_op jit(solution)/shard_map/factors/pallas_call | solution.py:278
  160.8 5.5 %all-to-all-done.3.tiles = bf16[32,4,16,128]{3,2,1,0:T(8,128)(2,1)S(1)} async-done(((bf16[32,4,16,128]{3,2,1,0:T(8,128)(2,1)}), bf16[32,4,16,128]{3,2,1,0:T(8,128)(2,1)S(1)}, u32[]{:S(2)}, u32[]{:S(2)}) %all-to-all-start.3) | async-done | bytes 524320 | tf_op jit(solution)/shard_map/all_to_all | solution.py:296
  166.4 0.9 assemble.1
  (45 shorter events, 0.2 us)
Async XLA Ops:
  0.6 1.0 copy-start.3
  13.1 25.1 %collective-permute-start.4 = (bf16[8,32,2048]{2,1,0:T(8,128)(2,1)}, bf16[8,32,2048]{2,1,0:T(8,128)(2,1)S(1)}, u32[]{:S(2)}, u32[]{:S(2)}) collective-permute-start(bf16[8,32,2048]{2,1,0:T(8,128)(2,1)} %bitcast.12), channel_id=1, source_target_pairs={{0,16},{16,32},{32,48},{48,0},{1,17},{17,33},{33,49},{49,1},{2,18}... | collective-permute-start | bytes 3145736 | tf_op jit(solution)/shard_map/ppermute | solution.py:311
  13.4 24.8 %collective-permute-start.5 = (bf16[8,32,2048]{2,1,0:T(8,128)(2,1)}, bf16[8,32,2048]{2,1,0:T(8,128)(2,1)S(1)}, u32[]{:S(2)}, u32[]{:S(2)}) collective-permute-start(bf16[8,32,2048]{2,1,0:T(8,128)(2,1)} %bitcast.13), channel_id=1, source_target_pairs={{0,48},{16,0},{32,16},{48,32},{1,49},{17,1},{33,17},{49,33},{2,50}... | collective-permute-start | bytes 3145736 | tf_op jit(solution)/shard_map/ppermute | solution.py:311
  15.8 27.7 %collective-permute-start.10 = (bf16[8,32,2048]{2,1,0:T(8,128)(2,1)}, bf16[8,32,2048]{2,1,0:T(8,128)(2,1)}, u32[]{:S(2)}, u32[]{:S(2)}) collective-permute-start(bf16[8,32,2048]{2,1,0:T(8,128)(2,1)} %bitcast.14), channel_id=1, source_target_pairs={{0,8},{8,0},{1,9},{9,1},{2,10},{10,2},{3,11},{11,3},{4,12},{12,4},... | collective-permute-start | bytes 3145736 | tf_op jit(solution)/shard_map/ppermute | solution.py:306
  17.5 26.0 %copy-start.4 = (s32[4]{0:T(128)}, s32[4]{0:T(128)S(1)}, u32[]{:S(2)}) copy-start(s32[4]{0:T(128)S(1)} %pad_add_fusion.spot) | copy-start | bytes 52
  18.2 50.0 %copy-start = (bf16[512,256]{1,0:T(8,128)(2,1)}, bf16[512,256]{1,0:T(8,128)(2,1)S(1)}, u32[]{:S(2)}) copy-start(bf16[512,256]{1,0:T(8,128)(2,1)S(1)} %turn.1.refs_0_) | copy-start | bytes 786436
  18.2 8.7 %collective-permute-start = (bf16[512,256]{1,0:T(8,128)(2,1)S(1)}, bf16[512,256]{1,0:T(8,128)(2,1)S(1)}, u32[]{:S(2)}, u32[]{:S(2)}) collective-permute-start(bf16[512,256]{1,0:T(8,128)(2,1)S(1)} %turn.1.refs_0_), channel_id=1, source_target_pairs={{0,1},{1,2},{2,3},{3,4},{4,5},{5,6},{6,7},{7,0},{8,9},{9,10},{10,1... | collective-permute-start | bytes 786440 | tf_op jit(solution)/shard_map/ppermute | solution.py:313
  21.1 9.2 %collective-permute-start.1 = (bf16[512,256]{1,0:T(8,128)(2,1)S(1)}, bf16[512,256]{1,0:T(8,128)(2,1)S(1)}, u32[]{:S(2)}, u32[]{:S(2)}) collective-permute-start(bf16[512,256]{1,0:T(8,128)(2,1)S(1)} %turn.1.refs_0_), channel_id=1, source_target_pairs={{0,7},{1,0},{2,1},{3,2},{4,3},{5,4},{6,5},{7,6},{8,15},{9,8},{10,9... | collective-permute-start | bytes 786440 | tf_op jit(solution)/shard_map/ppermute | solution.py:313
  26.8 11.4 %copy-start.12 = (bf16[512,256]{1,0:T(8,128)(2,1)}, bf16[512,256]{1,0:T(8,128)(2,1)S(1)}, u32[]{:S(2)}) copy-start(bf16[512,256]{1,0:T(8,128)(2,1)S(1)} %collective-permute-done.refs_1_) | copy-start | bytes 786436
  26.8 8.3 %collective-permute-start.2 = (bf16[512,256]{1,0:T(8,128)(2,1)S(1)}, bf16[512,256]{1,0:T(8,128)(2,1)S(1)}, u32[]{:S(2)}, u32[]{:S(2)}) collective-permute-start(bf16[512,256]{1,0:T(8,128)(2,1)S(1)} %collective-permute-done.refs_1_), channel_id=1, source_target_pairs={{0,1},{1,2},{2,3},{3,4},{4,5},{5,6},{6,7},{7,0},{8,9},{9,10},{10,1... | collective-permute-start | bytes 786440 | tf_op jit(solution)/shard_map/ppermute | solution.py:316
  30.3 8.0 %copy-start.13 = (bf16[512,256]{1,0:T(8,128)(2,1)}, bf16[512,256]{1,0:T(8,128)(2,1)S(1)}, u32[]{:S(2)}) copy-start(bf16[512,256]{1,0:T(8,128)(2,1)S(1)} %collective-permute-done.1.refs_2_) | copy-start | bytes 786436
  30.3 7.9 %collective-permute-start.3 = (bf16[512,256]{1,0:T(8,128)(2,1)S(1)}, bf16[512,256]{1,0:T(8,128)(2,1)S(1)}, u32[]{:S(2)}, u32[]{:S(2)}) collective-permute-start(bf16[512,256]{1,0:T(8,128)(2,1)S(1)} %collective-permute-done.1.refs_2_), channel_id=1, source_target_pairs={{0,7},{1,0},{2,1},{3,2},{4,3},{5,4},{6,5},{7,6},{8,15},{9,8},{10,9... | collective-permute-start | bytes 786440 | tf_op jit(solution)/shard_map/ppermute | solution.py:316
  35.1 11.0 %copy-start.14 = (bf16[512,256]{1,0:T(8,128)(2,1)}, bf16[512,256]{1,0:T(8,128)(2,1)S(1)}, u32[]{:S(2)}) copy-start(bf16[512,256]{1,0:T(8,128)(2,1)S(1)} %collective-permute-done.2.refs_3_) | copy-start | bytes 786436
  38.2 28.3 %copy-start.15 = (bf16[512,256]{1,0:T(8,128)(2,1)}, bf16[512,256]{1,0:T(8,128)(2,1)S(1)}, u32[]{:S(2)}) copy-start(bf16[512,256]{1,0:T(8,128)(2,1)S(1)} %collective-permute-done.3.refs_4_) | copy-start | bytes 786436
  38.2 29.9 %copy-start.5 = (bf16[8,32,2048]{2,1,0:T(8,128)(2,1)}, bf16[8,32,2048]{2,1,0:T(8,128)(2,1)S(1)}, u32[]{:S(2)}) copy-start(bf16[8,32,2048]{2,1,0:T(8,128)(2,1)S(1)} %collective-permute-done.4.refs_11_) | copy-start | bytes 3145732
  38.2 29.9 %copy-start.6 = (bf16[8,32,2048]{2,1,0:T(8,128)(2,1)}, bf16[8,32,2048]{2,1,0:T(8,128)(2,1)S(1)}, u32[]{:S(2)}) copy-start(bf16[8,32,2048]{2,1,0:T(8,128)(2,1)S(1)} %collective-permute-done.5.refs_13_) | copy-start | bytes 3145732
  38.3 28.3 %collective-permute-start.11 = (bf16[8,32,2048]{2,1,0:T(8,128)(2,1)S(1)}, bf16[8,32,2048]{2,1,0:T(8,128)(2,1)S(1)}, u32[]{:S(2)}, u32[]{:S(2)}) collective-permute-start(bf16[8,32,2048]{2,1,0:T(8,128)(2,1)S(1)} %collective-permute-done.4.refs_11_), channel_id=1, source_target_pairs={{0,8},{8,0},{1,9},{9,1},{2,10},{10,2},{3,11},{11,3},{4,12},{12,4},... | collective-permute-start | bytes 3145736 | tf_op jit(solution)/shard_map/ppermute | solution.py:306
  40.4 26.1 %collective-permute-start.12 = (bf16[8,32,2048]{2,1,0:T(8,128)(2,1)S(1)}, bf16[8,32,2048]{2,1,0:T(8,128)(2,1)S(1)}, u32[]{:S(2)}, u32[]{:S(2)}) collective-permute-start(bf16[8,32,2048]{2,1,0:T(8,128)(2,1)S(1)} %collective-permute-done.5.refs_13_), channel_id=1, source_target_pairs={{0,8},{8,0},{1,9},{9,1},{2,10},{10,2},{3,11},{11,3},{4,12},{12,4},... | collective-permute-start | bytes 3145736 | tf_op jit(solution)/shard_map/ppermute | solution.py:306
  40.5 14.4 %collective-permute-start.13 = (bf16[8,32,1024]{2,1,0:T(8,128)(2,1)S(1)}, bf16[8,32,1024]{2,1,0:T(8,128)(2,1)S(1)}, u32[]{:S(2)}, u32[]{:S(2)}) collective-permute-start(bf16[8,32,1024]{2,1,0:T(8,128)(2,1)S(1)} %slice.14), channel_id=1, source_target_pairs={{0,16},{16,32},{32,48},{48,0},{1,17},{17,33},{33,49},{49,1},{2,18}... | collective-permute-start | bytes 1572872 | tf_op jit(solution)/shard_map/ppermute | solution.py:320
  40.6 8.2 %collective-permute-start.6 = (bf16[512,256]{1,0:T(8,128)(2,1)S(1)}, bf16[512,256]{1,0:T(8,128)(2,1)S(1)}, u32[]{:S(2)}, u32[]{:S(2)}) collective-permute-start(bf16[512,256]{1,0:T(8,128)(2,1)S(1)} %collective-permute-done.2.refs_3_), channel_id=1, source_target_pairs={{0,1},{1,2},{2,3},{3,4},{4,5},{5,6},{6,7},{7,0},{8,9},{9,10},{10,1... | collective-permute-start | bytes 786440 | tf_op jit(solution)/shard_map/ppermute | solution.py:322
  43.5 15.5 %collective-permute-start.18 = (bf16[8,32,1024]{2,1,0:T(8,128)(2,1)S(1)}, bf16[8,32,1024]{2,1,0:T(8,128)(2,1)}, u32[]{:S(2)}, u32[]{:S(2)}) collective-permute-start(bf16[8,32,1024]{2,1,0:T(8,128)(2,1)S(1)} %slice.15), channel_id=1, source_target_pairs={{0,48},{16,0},{32,16},{48,32},{1,49},{17,1},{33,17},{49,33},{2,50}... | collective-permute-start | bytes 1572872 | tf_op jit(solution)/shard_map/ppermute | solution.py:321
  48.8 19.4 %copy-start.10 = (bf16[512,256]{1,0:T(8,128)(2,1)}, bf16[512,256]{1,0:T(8,128)(2,1)S(1)}, u32[]{:S(2)}) copy-start(bf16[512,256]{1,0:T(8,128)(2,1)S(1)} %collective-permute-done.6.refs_5_) | copy-start | bytes 786436
  48.8 8.9 %collective-permute-start.7 = (bf16[512,256]{1,0:T(8,128)(2,1)S(1)}, bf16[512,256]{1,0:T(8,128)(2,1)S(1)}, u32[]{:S(2)}, u32[]{:S(2)}) collective-permute-start(bf16[512,256]{1,0:T(8,128)(2,1)S(1)} %collective-permute-done.3.refs_4_), channel_id=1, source_target_pairs={{0,7},{1,0},{2,1},{3,2},{4,3},{5,4},{6,5},{7,6},{8,15},{9,8},{10,9... | collective-permute-start | bytes 786440 | tf_op jit(solution)/shard_map/ppermute | solution.py:322
  54.8 11.7 %copy-start.18 = (bf16[8,32,1024]{2,1,0:T(8,128)(2,1)}, bf16[8,32,1024]{2,1,0:T(8,128)(2,1)S(1)}, u32[]{:S(2)}) copy-start(bf16[8,32,1024]{2,1,0:T(8,128)(2,1)S(1)} %collective-permute-done.13.refs_15_) | copy-start | bytes 1572868
  54.8 13.3 %collective-permute-start.14 = (bf16[8,32,1024]{2,1,0:T(8,128)(2,1)S(1)}, bf16[8,32,1024]{2,1,0:T(8,128)(2,1)}, u32[]{:S(2)}, u32[]{:S(2)}) collective-permute-start(bf16[8,32,1024]{2,1,0:T(8,128)(2,1)S(1)} %collective-permute-done.13.refs_15_), channel_id=1, source_target_pairs={{0,8},{8,0},{1,9},{9,1},{2,10},{10,2},{3,11},{11,3},{4,12},{12,4},... | collective-permute-start | bytes 1572872 | tf_op jit(solution)/shard_map/ppermute | solution.py:306
  57.7 10.5 %copy-start.11 = (bf16[512,256]{1,0:T(8,128)(2,1)}, bf16[512,256]{1,0:T(8,128)(2,1)S(1)}, u32[]{:S(2)}) copy-start(bf16[512,256]{1,0:T(8,128)(2,1)S(1)} %collective-permute-done.7.refs_6_) | copy-start | bytes 786436
  57.7 3.8 %collective-permute-start.8 = (bf16[512,128]{1,0:T(8,128)(2,1)S(1)}, bf16[512,128]{1,0:T(8,128)(2,1)S(1)}, u32[]{:S(2)}, u32[]{:S(2)}) collective-permute-start(bf16[512,128]{1,0:T(8,128)(2,1)S(1)} %slice.16), channel_id=1, source_target_pairs={{0,1},{1,2},{2,3},{3,4},{4,5},{5,6},{6,7},{7,0},{8,9},{9,10},{10,1... | collective-permute-start | bytes 393224 | tf_op jit(solution)/shard_map/ppermute | solution.py:327
  59.0 21.8 %collective-permute-start.19 = (bf16[8,32,1024]{2,1,0:T(8,128)(2,1)}, bf16[8,32,1024]{2,1,0:T(8,128)(2,1)}, u32[]{:S(2)}, u32[]{:S(2)}) collective-permute-start(bf16[8,32,1024]{2,1,0:T(8,128)(2,1)} %collective-permute-done.18.refs_15_), channel_id=1, source_target_pairs={{0,8},{8,0},{1,9},{9,1},{2,10},{10,2},{3,11},{11,3},{4,12},{12,4},... | collective-permute-start | bytes 1572872 | tf_op jit(solution)/shard_map/ppermute | solution.py:306
  61.5 6.7 %copy-start.16 = (bf16[512,128]{1,0:T(8,128)(2,1)}, bf16[512,128]{1,0:T(8,128)(2,1)S(1)}, u32[]{:S(2)}) copy-start(bf16[512,128]{1,0:T(8,128)(2,1)S(1)} %collective-permute-done.8.refs_7_) | copy-start | bytes 393220
  61.5 5.0 %collective-permute-start.9 = (bf16[512,128]{1,0:T(8,128)(2,1)S(1)}, bf16[512,128]{1,0:T(8,128)(2,1)S(1)}, u32[]{:S(2)}, u32[]{:S(2)}) collective-permute-start(bf16[512,128]{1,0:T(8,128)(2,1)S(1)} %slice.17), channel_id=1, source_target_pairs={{0,7},{1,0},{2,1},{3,2},{4,3},{5,4},{6,5},{7,6},{8,15},{9,8},{10,9... | collective-permute-start | bytes 393224 | tf_op jit(solution)/shard_map/ppermute | solution.py:328
  66.5 0.7 copy-start.17
  66.5 1.7 %copy-start.7 = (bf16[8,32,2048]{2,1,0:T(8,128)(2,1)}, bf16[8,32,2048]{2,1,0:T(8,128)(2,1)S(1)}, u32[]{:S(2)}) copy-start(bf16[8,32,2048]{2,1,0:T(8,128)(2,1)S(1)} %collective-permute-done.11.refs_12_) | copy-start | bytes 3145732
  67.2 1.0 copy-start.8
  75.1 13.3 %collective-permute-start.15 = (bf16[64,16,128]{2,1,0:T(8,128)(2,1)}, bf16[64,16,128]{2,1,0:T(8,128)(2,1)S(1)}, u32[]{:S(2)}, u32[]{:S(2)}) collective-permute-start(bf16[64,16,128]{2,1,0:T(8,128)(2,1)} %get-tuple-element.32), channel_id=1, source_target_pairs={{0,128},{64,192},{128,0},{192,64},{1,129},{65,193},{129,1},{193,65... | collective-permute-start | bytes 786440 | tf_op jit(solution)/shard_map/ppermute | solution.py:334
  78.1 13.2 %collective-permute-start.16 = (bf16[64,16,128]{2,1,0:T(8,128)(2,1)}, bf16[64,16,128]{2,1,0:T(8,128)(2,1)S(1)}, u32[]{:S(2)}, u32[]{:S(2)}) collective-permute-start(bf16[64,16,128]{2,1,0:T(8,128)(2,1)} %get-tuple-element.33), channel_id=1, source_target_pairs={{0,64},{64,128},{128,192},{192,0},{1,65},{65,129},{129,193},{193,1... | collective-permute-start | bytes 786440 | tf_op jit(solution)/shard_map/ppermute | solution.py:334
  78.5 12.0 %copy-start.19 = (s32[1,128]{1,0:T(1,128)S(1)}, s32[1,128]{1,0:T(1,128)}, u32[]{:S(2)}) copy-start(s32[1,128]{1,0:T(1,128)} %param.11) | copy-start | bytes 1540
  78.5 20.1 %copy-start.1 = (bf16[64,16,128]{2,1,0:T(8,128)(2,1)S(1)}, bf16[64,16,128]{2,1,0:T(8,128)(2,1)}, u32[]{:S(2)}) copy-start(bf16[64,16,128]{2,1,0:T(8,128)(2,1)} %get-tuple-element.31.refs_0_) | copy-start | bytes 786436
  78.5 12.8 %collective-permute-start.17 = (bf16[64,16,128]{2,1,0:T(8,128)(2,1)}, bf16[64,16,128]{2,1,0:T(8,128)(2,1)S(1)}, u32[]{:S(2)}, u32[]{:S(2)}) collective-permute-start(bf16[64,16,128]{2,1,0:T(8,128)(2,1)} %get-tuple-element.34), channel_id=1, source_target_pairs={{0,192},{64,0},{128,64},{192,128},{1,193},{65,1},{129,65},{193,129... | collective-permute-start | bytes 786440 | tf_op jit(solution)/shard_map/ppermute | solution.py:334
  87.6 7.1 %collective-permute-start.20 = (bf16[64,16,128]{2,1,0:T(8,128)(2,1)}, bf16[64,16,128]{2,1,0:T(8,128)(2,1)S(1)}, u32[]{:S(2)}, u32[]{:S(2)}) collective-permute-start(bf16[64,16,128]{2,1,0:T(8,128)(2,1)} %get-tuple-element.36), channel_id=1, source_target_pairs={{0,128},{64,192},{128,0},{192,64},{1,129},{65,193},{129,1},{193,65... | collective-permute-start | bytes 786440 | tf_op jit(solution)/shard_map/ppermute | solution.py:334
  87.7 10.4 %collective-permute-start.21 = (bf16[64,16,128]{2,1,0:T(8,128)(2,1)}, bf16[64,16,128]{2,1,0:T(8,128)(2,1)S(1)}, u32[]{:S(2)}, u32[]{:S(2)}) collective-permute-start(bf16[64,16,128]{2,1,0:T(8,128)(2,1)} %get-tuple-element.37), channel_id=1, source_target_pairs={{0,64},{64,128},{128,192},{192,0},{1,65},{65,129},{129,193},{193,1... | collective-permute-start | bytes 786440 | tf_op jit(solution)/shard_map/ppermute | solution.py:334
  88.5 10.2 %collective-permute-start.22 = (bf16[64,16,128]{2,1,0:T(8,128)(2,1)}, bf16[64,16,128]{2,1,0:T(8,128)(2,1)S(1)}, u32[]{:S(2)}, u32[]{:S(2)}) collective-permute-start(bf16[64,16,128]{2,1,0:T(8,128)(2,1)} %get-tuple-element.38), channel_id=1, source_target_pairs={{0,192},{64,0},{128,64},{192,128},{1,193},{65,1},{129,65},{193,129... | collective-permute-start | bytes 786440 | tf_op jit(solution)/shard_map/ppermute | solution.py:334
  98.6 1.0 copy-start.2
  101.4 24.1 %all-to-all-start.1 = ((bf16[32,5,16,128]{3,2,1,0:T(8,128)(2,1)}), bf16[32,5,16,128]{3,2,1,0:T(8,128)(2,1)S(1)}, u32[]{:S(2)}, u32[]{:S(2)}) async-start(bf16[32,5,16,128]{3,2,1,0:T(8,128)(2,1)} %bitcast.6), calls=%async_computation.1 | async-start | bytes 1310720 | tf_op jit(solution)/shard_map/all_to_all | solution.py:296
  125.6 0.8 copy-start.9
  150.6 15.8 %all-to-all-start.3 = ((bf16[32,4,16,128]{3,2,1,0:T(8,128)(2,1)}), bf16[32,4,16,128]{3,2,1,0:T(8,128)(2,1)S(1)}, u32[]{:S(2)}, u32[]{:S(2)}) async-start(bf16[32,4,16,128]{3,2,1,0:T(8,128)(2,1)} %bitcast.8), calls=%async_computation.3 | async-start | bytes 1048576 | tf_op jit(solution)/shard_map/all_to_all | solution.py:296

commit v4 on v2

--- a/solution.py
+++ b/solution.py
@@ -24,6 +24,7 @@
 DP = ("y", "x", "core")
 CHIP_ROWS = LOCAL_ROWS * CORE
 SHARD_K = X * TOK_SUB
+SOURCES = (0, -1, 1, 2)
 WIDE = 2
 CHUNK_K = NBLK // 2
 
@@ -47,7 +48,7 @@
     return slice(top, top + TILE_ROWS), slice(side, side + TILE_COLS)
 
 
-def cut_kernel(core, tokens, out):
+def cut_kernel(spot, tokens, out):
     def strips_from(first):
         for chip in range(X):
             for i in range(CORE):
@@ -61,37 +62,37 @@
                 )
 
     for first in range(CORE):
-        pl.when(core[0] == first)(lambda: strips_from(first))
-
-
-def cut_tokens(core, tokens):
+        pl.when(spot[2] == first)(lambda: strips_from(first))
+
+
+def cut_tokens(spot, tokens):
     return pl.pallas_call(
         cut_kernel,
         in_specs=[SMEM, VMEM],
         out_shape=jax.ShapeDtypeStruct((X, TOK_SUB, CHIP_ROWS), jnp.bfloat16),
         compiler_params=params(32),
         name="cut_tokens",
-    )(core, tokens)
-
-
-def turn_kernel(source, pieces, out):
-    joined = jnp.concatenate([pieces[source[i]] for i in range(X)], axis=0)
-    out[...] = joined.T
-
-
-def turn(source, pieces):
+    )(spot, tokens)
+
+
+def turn_kernel(spot, pieces, out):
+    joined = [pieces[(spot[1] + step + X) % X] for step in SOURCES]
+    out[...] = jnp.concatenate(joined, axis=0).T
+
+
+def turn(spot, pieces):
     return pl.pallas_call(
         turn_kernel,
         in_specs=[SMEM, VMEM],
         out_shape=jax.ShapeDtypeStruct((CHIP_ROWS, SHARD_K), jnp.bfloat16),
         compiler_params=params(32),
         name="turn",
-    )(source, pieces)
-
-
-def gradient_kernel(place, *refs):
+    )(spot, pieces)
+
+
+def gradient_kernel(spot, *refs):
     whole, halves, sources = refs[:7], refs[7:9], refs[9:13]
-    outs, (left, right) = refs[13:15], refs[15:]
+    mine, other, (left, right, tiles) = refs[13:17], refs[17], refs[18:]
 
     @pl.when(pl.program_id(0) == 0)
     def join_tokens():
@@ -100,71 +101,108 @@
         left[:LOCAL_ROWS, 7 * SHARD_K :] = halves[0][...]
         left[LOCAL_ROWS:, 7 * SHARD_K :] = halves[1][...]
 
-    for j in range(N_TENSOR):
+    for j, step in enumerate((0, -1, 1, -2, 2, -3, 3, 4)):
+        place = (spot[3] + step + N_TENSOR) % N_TENSOR
         for i in range(X):
             top = j * SHARD_K + i * TOK_SUB
-            right[top : top + TOK_SUB] = sources[i][place[j]]
+            right[top : top + TOK_SUB] = sources[i][place]
     for column in range(WIDE):
-        blocks = slice(column * ROW_BLOCKS, (column + 1) * ROW_BLOCKS)
         result = jnp.dot(
             left[...], right[:, column * BLOCK : (column + 1) * BLOCK],
             preferred_element_type=jnp.float32,
         ).astype(jnp.bfloat16)
-        for out, part in zip(outs, (result[:LOCAL_ROWS], result[LOCAL_ROWS:])):
-            out[blocks] = part.reshape(ROW_BLOCKS, STRIP, BLOCK)
-
-
-def gradient_strips(chunk, place, lefts, near, far):
-    resident = lambda a: pl.BlockSpec(a.shape, lambda c, place: (0, 0))
+        for side in range(CORE):
+            for r in range(ROW_BLOCKS):
+                for y in range(Y):
+                    rows, cols = tile_of(y * ROW)
+                    top = side * LOCAL_ROWS + r * STRIP + rows.start
+                    tiles[side, y, column * ROW_BLOCKS + r] = result[top : top + TILE_ROWS, cols]
+    for step in range(Y):
+        place = (spot[0] + step) % Y
+        mine[step][...] = tiles[0, place]
+        other[step] = tiles[1, place]
+
+
+def gradient_tiles(chunk, spot, lefts, near, far):
+    resident = lambda a: pl.BlockSpec(a.shape, lambda c, spot: (0, 0))
     steps = COL_BLOCKS // 2 // WIDE
+    blocks = WIDE * ROW_BLOCKS
     shape = (N_TENSOR, TOK_SUB, WIDE * BLOCK)
-    near_spec = pl.BlockSpec(shape, lambda c, place: (0, 0, steps * chunk + c))
-    far_spec = pl.BlockSpec(shape, lambda c, place: (0, 0, c))
-    strips = pl.BlockSpec((WIDE * ROW_BLOCKS, STRIP, BLOCK), lambda c, place: (c, 0, 0))
+    near_spec = pl.BlockSpec(shape, lambda c, spot: (0, 0, steps * chunk + c))
+    far_spec = pl.BlockSpec(shape, lambda c, spot: (0, 0, c))
+    part = pl.BlockSpec((blocks, TILE_ROWS, TILE_COLS), lambda c, spot: (c, 0, 0))
     return pl.pallas_call(
         gradient_kernel,
         grid_spec=pltpu.PrefetchScalarGridSpec(
             num_scalar_prefetch=1,
             grid=(steps,),
             in_specs=[resident(a) for a in lefts] + [near_spec] * 3 + [far_spec],
-            out_specs=[strips] * CORE,
+            out_specs=[part] * Y
+            + [pl.BlockSpec((Y, blocks, TILE_ROWS, TILE_COLS), lambda c, spot: (0, c, 0, 0))],
             scratch_shapes=[
                 pltpu.VMEM((CHIP_ROWS, N_TENSOR * SHARD_K), jnp.bfloat16),
                 pltpu.VMEM((N_TENSOR * SHARD_K, WIDE * BLOCK), jnp.bfloat16),
+                pltpu.VMEM((CORE, Y, blocks, TILE_ROWS, TILE_COLS), jnp.bfloat16),
             ],
         ),
-        out_shape=[jax.ShapeDtypeStruct((CHUNK_K, STRIP, BLOCK), jnp.bfloat16)] * CORE,
+        out_shape=[jax.ShapeDtypeStruct((CHUNK_K, TILE_ROWS, TILE_COLS), jnp.bfloat16)] * Y
+        + [jax.ShapeDtypeStruct((Y, CHUNK_K, TILE_ROWS, TILE_COLS), jnp.bfloat16)],
         compiler_params=params(60),
         cost_estimate=pl.CostEstimate(
             flops=2 * CHIP_ROWS * N_TENSOR * SHARD_K * 4 * BLOCK,
             bytes_accessed=8 * MIB, transcendentals=0,
         ),
-        name="gradient_strips",
-    )(place, *lefts, *near, far)
+        name="gradient_tiles",
+    )(spot, *lefts, *near, far)
+
+
+def add_cores_kernel(one, two, three, other, *outs):
+    for d, (mine, out) in enumerate(zip((one, two, three), outs), 1):
+        out[...] = (mine[...].astype(jnp.float32) + other[d].astype(jnp.float32)).astype(
+            jnp.bfloat16
+        )
+
+
+def add_cores(parts, other):
+    blocks = CHUNK_K // 4
+    part = pl.BlockSpec((blocks, TILE_ROWS, TILE_COLS), lambda c: (c, 0, 0))
+    return pl.pallas_call(
+        add_cores_kernel,
+        grid=(4,),
+        in_specs=[part] * 3
+        + [pl.BlockSpec((Y, blocks, TILE_ROWS, TILE_COLS), lambda c: (0, c, 0, 0))],
+        out_specs=[part] * 3,
+        out_shape=[jax.ShapeDtypeStruct(a.shape, a.dtype) for a in parts[1:]],
+        compiler_params=params(60),
+        name="add_cores",
+    )(*parts[1:], other)
 
 
 def to_slots_kernel(slot, *refs):
     out = refs[-1]
     out[...] = jnp.zeros_like(out)
     for chunk in range(2):
-        one, two = refs[2 * chunk : 2 * chunk + 2]
+        mine, other, *rest = refs[5 * chunk : 5 * chunk + 5]
 
         def body(k, carry):
-            total = one[k].astype(jnp.float32) + two[k].astype(jnp.float32)
+            total = mine[k].astype(jnp.float32) + other[0, k].astype(jnp.float32)
+            for part in rest:
+                total = total + part[k].astype(jnp.float32)
             out[slot[chunk * CHUNK_K + k]] = total.astype(jnp.bfloat16)
             return carry
 
         lax.fori_loop(0, CHUNK_K, body, 0, unroll=8)
 
 
-def to_slots(slot, parts):
+def to_slots(slot, chunks):
+    flat = [a for chunk in chunks for a in chunk]
     return pl.pallas_call(
         to_slots_kernel,
-        in_specs=[SMEM] + [VMEM] * len(parts),
-        out_shape=jax.ShapeDtypeStruct((N_DP * SLOTS, STRIP, BLOCK), jnp.bfloat16),
+        in_specs=[SMEM] + [VMEM] * len(flat),
+        out_shape=jax.ShapeDtypeStruct((N_DP * SLOTS, TILE_ROWS, TILE_COLS), jnp.bfloat16),
         compiler_params=params(32),
         name="to_slots",
-    )(slot, *parts)
+    )(slot, *flat)
 
 
 def from_slots_kernel(slot, tiles, out):
@@ -206,15 +244,13 @@
 
 
 def update_kernel(
-    live, strips, basis_left, basis_right, first, second,
+    live, tiles, basis_left, basis_right, first, second,
     update, grads, first_new, second_new,
 ):
     for s in range(SLOTS):
-        for strip in range(ROW):
-            total = strips[strip, s].astype(jnp.float32)
-            for y in range(1, Y):
-                total = total + strips[y * ROW + strip, s].astype(jnp.float32)
-            grads[s, strip * STRIP : (strip + 1) * STRIP] = total.astype(jnp.bfloat16)
+        for m in range(N_DP):
+            rows, cols = tile_of(m)
+            grads[s, rows, cols] = tiles[m, s]
         grad = grads[s]
         ql, qr = basis_left[0, s], basis_right[0, s]
         halfway = dot(ql, grad, 0, 0).astype(jnp.bfloat16)
@@ -236,20 +272,20 @@
         second_new[0, s] = jnp.where(alive, second_float.astype(jnp.bfloat16), second_old)
 
 
-def update_blocks(live, strips, basis_left, basis_right, first, second):
+def update_blocks(live, tiles, basis_left, basis_right, first, second):
     like = lambda a: jax.ShapeDtypeStruct(a.shape, a.dtype)
     return pl.pallas_call(
         update_kernel,
         in_specs=[SMEM] + [VMEM] * 5,
         out_shape=[
-            jax.ShapeDtypeStruct((N_DP, SLOTS, TILE_ROWS, TILE_COLS), jnp.bfloat16),
+            like(tiles),
             jax.ShapeDtypeStruct((SLOTS, BLOCK, BLOCK), jnp.bfloat16),
             like(first),
             like(second),
         ],
         compiler_params=params(60),
         name="update",
-    )(live, strips, basis_left, basis_right, first, second)
+    )(live, tiles, basis_left, basis_right, first, second)
 
 
 def factor_kernel(live, grads, left, right, left_new, right_new):
@@ -292,13 +328,13 @@
     return [(i, (i + step) % size) for i in range(size)]
 
 
-def gather_row(tokens, grads, source, core):
+def gather_row(spot, tokens, grads):
     up, down = ring(N_TENSOR, 1), ring(N_TENSOR, -1)
     ahead, back = ring(X, 1), ring(X, -1)
 
-    pieces, grads = lax.optimization_barrier((spread(cut_tokens(core, tokens), "x"), grads))
+    pieces, grads = lax.optimization_barrier((spread(cut_tokens(spot, tokens), "x"), grads))
     behind, before = lax.ppermute(grads, "x", ahead), lax.ppermute(grads, "x", back)
-    mine = turn(source, pieces)
+    mine = turn(spot, pieces)
     below, above = lax.ppermute(mine, "z", up), lax.ppermute(mine, "z", down)
     whole = [mine, below, above]
     below, above = lax.ppermute(below, "z", up), lax.ppermute(above, "z", down)
@@ -318,6 +354,15 @@
     return whole + halves, [grads, behind, before], far
 
 
+def sum_parts(parts):
+    mine, other = parts[:Y], lax.ppermute(parts[Y], "core", ring(CORE, 1))
+    one, two, three = add_cores(mine, other)
+    moved = [
+        lax.ppermute(a, "y", ring(Y, step)) for a, step in ((two, 2), (one, 1), (three, 3))
+    ]
+    return [mine[0], other] + moved
+
+
 def local(
     tokens, grad_out, owner, left_factor, right_factor,
     left_basis, right_basis, first_moment, second_moment,
@@ -331,20 +376,15 @@
     held = jnp.sum((owner_row == lax.axis_index(DP)).astype(jnp.int32))
     live = (jnp.arange(SLOTS, dtype=jnp.int32) < held).astype(jnp.int32)
 
-    steps = jnp.array([0, -1, 1, -2, 2, -3, 3, 4], jnp.int32)
-    place = (lax.axis_index("z") + steps + N_TENSOR) % N_TENSOR
-    along = jnp.array([0, -1, 1, 2], jnp.int32)
-    source = (lax.axis_index("x") + along + X) % X
-    core = lax.axis_index("core").astype(jnp.int32).reshape(1)
+    spot = jnp.stack([lax.axis_index(axis) for axis in (*DP, "z")]).astype(jnp.int32)
     grads = grad_out.reshape(N_TENSOR, TOK_SUB, grad_out.shape[1])
-    lefts, near, far = gather_row(tokens, grads, source, core)
-    parts = []
-    for chunk in range(2):
-        mine, other = gradient_strips(chunk, place, lefts, near, far[chunk])
-        parts += [mine, lax.ppermute(other, "core", ring(CORE, 1))]
-    strips = to_slots(slot, parts).reshape(N_DP, SLOTS, STRIP, BLOCK)
+    lefts, near, far = gather_row(spot, tokens, grads)
+    chunks = [
+        sum_parts(gradient_tiles(chunk, spot, lefts, near, far[chunk])) for chunk in range(2)
+    ]
+    tiles = to_slots(slot, chunks).reshape(N_DP, SLOTS, TILE_ROWS, TILE_COLS)
     update, grad_blocks, first_new, second_new = update_blocks(
-        live, spread(strips, DP), left_basis, right_basis, first_moment, second_moment
+        live, spread(tiles, DP), left_basis, right_basis, first_moment, second_moment
     )
     left_new, right_new = update_factors(live, grad_blocks, left_factor, right_factor)
     back = spread(update, DP).reshape(N_DP * SLOTS, TILE_ROWS, TILE_COLS)

time: 165 us -> 171 us (1.036)
  starting transfers between devices: 36.2 us -> 44.9 us
  waiting for transfers between devices: 58.4 us -> 50.8 us
  Pallas kernels: 31.6 us -> 38.2 us
  blocking collectives: 28.7 us -> 26.5 us
    all_to_all x2, waiting for transfers between devices: 37.9 us -> 17.3 us  [spread(): return lax.all_to_all(array, axes, split_axis=0, concat_axis=0, tiled=True)]
    ppermute x2 -> x8, waiting for transfers between devices: 1.88 us -> 13.1 us  [the longest x6 13.1 us: sum_parts(): lax.ppermute(a, 'y', ring(Y, step))]
    ppermute x2 -> x8, starting transfers between devices: 5.53 us -> 13.9 us  [the longest x6 8.43 us: sum_parts(): lax.ppermute(a, 'y', ring(Y, step))]
    pallas_call x4 -> x6, Pallas kernels: 22.1 us -> 28.2 us  [the longest x2 13.7 us: gradient_tiles(): pl.pallas_call(gradient_kernel, grid_spec=pltpu.PrefetchScalarGridSpec(nu...]
    all_to_all x2, blocking collectives: 28.7 us -> 26.5 us  [spread(): return lax.all_to_all(array, axes, split_axis=0, concat_axis=0, tiled=True)]
    unnamed x28 -> x44, local copies, waits for them, and re-layouts: 4.35 us -> 6.45 us
  transfers between devices with their start and end apart: 16 -> 22, of which waited for: 10 -> 13; matrix products, arithmetic and copies ran while one was open for 3% -> 1% of each run, Pallas kernels for 12% -> 16%
where the time goes in v4:
time: 171 us; the launch traced here: 170 us
  waiting for transfers between devices  50.8 us (30%)
  starting transfers between devices  44.9 us (26%)
  Pallas kernels  38.2 us (22%)
  blocking collectives  26.5 us (15%)
  local copies, waits for them, and re-layouts  6.54 us (4%)
  other arithmetic  2.04 us (1%)
    all_to_all x2, blocking collectives, spread(): return lax.all_to_all(array, axes, split_axis=0, concat_axis=0, tiled=True)  26.5 us
    all_to_all x2, waiting for transfers between devices, spread(): return lax.all_to_all(array, axes, split_axis=0, concat_axis=0, tiled=True)  17.3 us
    pallas_call x2, Pallas kernels, gradient_tiles(): pl.pallas_call(gradient_kernel, grid_spec=pltpu.PrefetchScalarGridSpec(nu...  13.7 us
    ppermute x6, waiting for transfers between devices, sum_parts(): lax.ppermute(a, 'y', ring(Y, step))  13.1 us
    all_to_all x2, starting transfers between devices, spread(): return lax.all_to_all(array, axes, split_axis=0, concat_axis=0, tiled=True)  13.1 us
    ppermute x6, starting transfers between devices, sum_parts(): lax.ppermute(a, 'y', ring(Y, step))  8.43 us
    pallas_call x2, Pallas kernels, add_cores(): pl.pallas_call(add_cores_kernel, grid=(4,), in_specs=[part] * 3 + [pl.Blo...  7.02 us
    unnamed x44, local copies, waits for them, and re-layouts  6.45 us
  transfers between devices with their start and end apart: 22, of which 13 were waited for; matrix products, arithmetic and copies ran while one was open for 1% of the time, Pallas kernels for 16%

profile of v4, /device:TPU:97, one launch (start us, length us, event | category | flops | bytes accessed | tf_op | source)
XLA Modules:
  0.0 169.9 jit_solution(5118392847358139610)
XLA Ops:
  0.6 0.1 pad_add_fusion.spot
  0.7 0.9 copy-done.6
  1.7 0.8 cut_tokens.1
  2.5 9.4 %all_to_all.20.pieces = bf16[4,32,1024]{2,1,0:T(8,128)(2,1)S(1)} all-to-all(bf16[4,32,1024]{2,1,0:T(8,128)(2,1)S(1)} %cut_tokens.1), channel_id=1, replica_groups=mesh['y'=4,'x'=4,'core'=2,'z'=8] {'x'}, dimensions={0} | all-to-all | bytes 524288 | tf_op jit(solution)/shard_map/all_to_all | solution.py:324
  11.9 0.4 collective-permute-start.4
  12.2 2.3 %collective-permute-start.5 = (bf16[8,32,2048]{2,1,0:T(8,128)(2,1)}, bf16[8,32,2048]{2,1,0:T(8,128)(2,1)S(1)}, u32[]{:S(2)}, u32[]{:S(2)}) collective-permute-start(bf16[8,32,2048]{2,1,0:T(8,128)(2,1)} %bitcast.14), channel_id=1, source_target_pairs={{0,48},{16,0},{32,16},{48,32},{1,49},{17,1},{33,17},{49,33},{2,50}... | collective-permute-start | bytes 3145736 | tf_op jit(solution)/shard_map/ppermute | solution.py:336
  14.5 0.7 turn.1.refs_0_
  15.2 0.0 copy-start.7
  15.2 2.9 %collective-permute-start = (bf16[1024,128]{1,0:T(8,128)(2,1)S(1)}, bf16[1024,128]{1,0:T(8,128)(2,1)S(1)}, u32[]{:S(2)}, u32[]{:S(2)}) collective-permute-start(bf16[1024,128]{1,0:T(8,128)(2,1)S(1)} %turn.1.refs_0_), channel_id=1, source_target_pairs={{0,1},{1,2},{2,3},{3,4},{4,5},{5,6},{6,7},{7,0},{8,9},{9,10},{10,1... | collective-permute-start | bytes 786440 | tf_op jit(solution)/shard_map/ppermute | solution.py:338
  18.2 0.0 collective-permute-start.1
  18.2 3.3 %collective-permute-done.refs_1_ = bf16[1024,128]{1,0:T(8,128)(2,1)S(1)} collective-permute-done((bf16[1024,128]{1,0:T(8,128)(2,1)S(1)}, bf16[1024,128]{1,0:T(8,128)(2,1)S(1)}, u32[]{:S(2)}, u32[]{:S(2)}) %collective-permute-start) | collective-permute-done | bytes 262176 | tf_op jit(solution)/shard_map/ppermute | solution.py:338
  21.5 3.4 %collective-permute-start.2 = (bf16[1024,128]{1,0:T(8,128)(2,1)S(1)}, bf16[1024,128]{1,0:T(8,128)(2,1)S(1)}, u32[]{:S(2)}, u32[]{:S(2)}) collective-permute-start(bf16[1024,128]{1,0:T(8,128)(2,1)S(1)} %collective-permute-done.refs_1_), channel_id=1, source_target_pairs={{0,1},{1,2},{2,3},{3,4},{4,5},{5,6},{6,7},{7,0},{8,9},{9,10},{10,1... | collective-permute-start | bytes 786440 | tf_op jit(solution)/shard_map/ppermute | solution.py:340
  24.9 0.0 collective-permute-done.1.refs_2_
  24.9 3.3 %collective-permute-done.2.refs_3_ = bf16[1024,128]{1,0:T(8,128)(2,1)S(1)} collective-permute-done((bf16[1024,128]{1,0:T(8,128)(2,1)S(1)}, bf16[1024,128]{1,0:T(8,128)(2,1)S(1)}, u32[]{:S(2)}, u32[]{:S(2)}) %collective-permute-start.2) | collective-permute-done | bytes 262176 | tf_op jit(solution)/shard_map/ppermute | solution.py:340
  28.2 3.4 %collective-permute-done.3.refs_4_ = bf16[1024,128]{1,0:T(8,128)(2,1)S(1)} collective-permute-done((bf16[1024,128]{1,0:T(8,128)(2,1)S(1)}, bf16[1024,128]{1,0:T(8,128)(2,1)S(1)}, u32[]{:S(2)}, u32[]{:S(2)}) %collective-permute-start.3) | collective-permute-done | bytes 262176 | tf_op jit(solution)/shard_map/ppermute | solution.py:340
  31.6 4.2 %collective-permute-done.4.refs_10_ = bf16[8,32,2048]{2,1,0:T(8,128)(2,1)S(1)} collective-permute-done((bf16[8,32,2048]{2,1,0:T(8,128)(2,1)}, bf16[8,32,2048]{2,1,0:T(8,128)(2,1)S(1)}, u32[]{:S(2)}, u32[]{:S(2)}) %collective-permute-start.4) | collective-permute-done | bytes 1048608 | tf_op jit(solution)/shard_map/ppermute | solution.py:336
  35.9 0.0 collective-permute-done.5.refs_11_
  35.9 0.1 collective-permute-start.10
  36.0 2.9 %collective-permute-start.6 = (bf16[1024,128]{1,0:T(8,128)(2,1)S(1)}, bf16[1024,128]{1,0:T(8,128)(2,1)S(1)}, u32[]{:S(2)}, u32[]{:S(2)}) collective-permute-start(bf16[1024,128]{1,0:T(8,128)(2,1)S(1)} %collective-permute-done.2.refs_3_), channel_id=1, source_target_pairs={{0,1},{1,2},{2,3},{3,4},{4,5},{5,6},{6,7},{7,0},{8,9},{9,10},{10,1... | collective-permute-start | bytes 786440 | tf_op jit(solution)/shard_map/ppermute | solution.py:348
  39.0 2.7 %collective-permute-start.15 = (bf16[8,32,1024]{2,1,0:T(8,128)(2,1)S(1)}, bf16[8,32,1024]{2,1,0:T(8,128)(2,1)}, u32[]{:S(2)}, u32[]{:S(2)}) collective-permute-start(bf16[8,32,1024]{2,1,0:T(8,128)(2,1)S(1)} %slice.15), channel_id=1, source_target_pairs={{0,48},{16,0},{32,16},{48,32},{1,49},{17,1},{33,17},{49,33},{2,50}... | collective-permute-start | bytes 1572872 | tf_op jit(solution)/shard_map/ppermute | solution.py:346
  41.7 0.6 collective-permute-done.6.refs_5_
  42.3 3.2 %collective-permute-start.8 = (bf16[512,128]{1,0:T(8,128)(2,1)S(1)}, bf16[512,128]{1,0:T(8,128)(2,1)S(1)}, u32[]{:S(2)}, u32[]{:S(2)}) collective-permute-start(bf16[512,128]{1,0:T(8,128)(2,1)S(1)} %slice.16), channel_id=1, source_target_pairs={{0,1},{1,2},{2,3},{3,4},{4,5},{5,6},{6,7},{7,0},{8,9},{9,10},{10,1... | collective-permute-start | bytes 393224 | tf_op jit(solution)/shard_map/ppermute | solution.py:351
  45.5 0.2 collective-permute-done.7.refs_6_
  45.7 0.1 collective-permute-start.9
  45.8 1.6 collective-permute-done.8.refs_7_
  47.4 3.7 %collective-permute-done.9.refs_8_ = bf16[512,128]{1,0:T(8,128)(2,1)S(1)} collective-permute-done((bf16[512,128]{1,0:T(8,128)(2,1)S(1)}, bf16[512,128]{1,0:T(8,128)(2,1)S(1)}, u32[]{:S(2)}, u32[]{:S(2)}) %collective-permute-start.9) | collective-permute-done | bytes 131104 | tf_op jit(solution)/shard_map/ppermute | solution.py:352
  51.1 0.6 copy-done.21
  51.8 0.0 collective-permute-done.10.refs_12_
  51.8 0.0 copy-start.15
  51.8 0.8 copy-done.15
  52.6 6.9 %gradient_tiles.2 = (bf16[64,16,128]{2,1,0:T(8,128)(2,1)}, bf16[64,16,128]{2,1,0:T(8,128)(2,1)}, bf16[64,16,128]{2,1,0:T(8,128)(2,1)}, bf16[64,16,128]{2,1,0:T(8,128)(2,1)}, bf16[4,64,16,128]{3,2,1,0:T(8,128)(2,1)}) custom-call(s32[4]{0:T(128)} %copy-done.8, bf16[1024,128]{1,0:T(8,128)(2,1)} %copy-done.7, bf16[1024,128]{1,0:T(8,128)(2,1)} %copy-done.16, ...), custom_call_target="tpu_custom_call" | custom-call | flops 2147483648 | bytes 8388608 | tf_op jit(solution)/shard_map/gradient_tiles/pallas_call | solution.py:134
  59.5 5.3 %collective-permute-start.11 = (bf16[4,64,16,128]{3,2,1,0:T(8,128)(2,1)}, bf16[4,64,16,128]{3,2,1,0:T(8,128)(2,1)S(1)}, u32[]{:S(2)}, u32[]{:S(2)}) collective-permute-start(bf16[4,64,16,128]{3,2,1,0:T(8,128)(2,1)} %get-tuple-element.40), channel_id=1, source_target_pairs={{0,8},{8,0},{1,9},{9,1},{2,10},{10,2},{3,11},{11,3},{4,12},{12,4},... | collective-permute-start | bytes 3145736 | tf_op jit(solution)/shard_map/ppermute | solution.py:358
  64.8 6.9 %gradient_tiles.3 = (bf16[64,16,128]{2,1,0:T(8,128)(2,1)}, bf16[64,16,128]{2,1,0:T(8,128)(2,1)}, bf16[64,16,128]{2,1,0:T(8,128)(2,1)}, bf16[64,16,128]{2,1,0:T(8,128)(2,1)}, bf16[4,64,16,128]{3,2,1,0:T(8,128)(2,1)}) custom-call(s32[4]{0:T(128)} %copy-done.8, bf16[1024,128]{1,0:T(8,128)(2,1)} %copy-done.7, bf16[1024,128]{1,0:T(8,128)(2,1)} %copy-done.16, ...), custom_call_target="tpu_custom_call" | custom-call | flops 2147483648 | bytes 8388608 | tf_op jit(solution)/shard_map/gradient_tiles/pallas_call | solution.py:134
  71.7 0.1 collective-permute-start.16
  71.8 0.0 collective-permute-done.11.other.refs_1_
  71.8 1.0 copy-done
  72.8 3.5 %add_cores.2 = (bf16[64,16,128]{2,1,0:T(8,128)(2,1)}, bf16[64,16,128]{2,1,0:T(8,128)(2,1)}, bf16[64,16,128]{2,1,0:T(8,128)(2,1)}) custom-call(bf16[64,16,128]{2,1,0:T(8,128)(2,1)} %get-tuple-element.41.one, bf16[64,16,128]{2,1,0:T(8,128)(2,1)} %get-tuple-element.42.two, bf16[64,16,128]{2,1,0:T(8,128)(2,1)} %get-tuple-element.43.three, ...), custom_call_target="tpu_custom_call" | custom-call | tf_op jit(solution)/shard_map/add_cores/pallas_call | solution.py:169
  76.3 3.0 %collective-permute-start.12 = (bf16[64,16,128]{2,1,0:T(8,128)(2,1)}, bf16[64,16,128]{2,1,0:T(8,128)(2,1)S(1)}, u32[]{:S(2)}, u32[]{:S(2)}) collective-permute-start(bf16[64,16,128]{2,1,0:T(8,128)(2,1)} %get-tuple-element.44), channel_id=1, source_target_pairs={{0,128},{64,192},{128,0},{192,64},{1,129},{65,193},{129,1},{193,65... | collective-permute-start | bytes 786440 | tf_op jit(solution)/shard_map/ppermute | solution.py:361
  79.3 0.4 collective-permute-start.13
  79.7 2.3 %collective-permute-start.14 = (bf16[64,16,128]{2,1,0:T(8,128)(2,1)}, bf16[64,16,128]{2,1,0:T(8,128)(2,1)S(1)}, u32[]{:S(2)}, u32[]{:S(2)}) collective-permute-start(bf16[64,16,128]{2,1,0:T(8,128)(2,1)} %get-tuple-element.46), channel_id=1, source_target_pairs={{0,192},{64,0},{128,64},{192,128},{1,193},{65,1},{129,65},{193,129... | collective-permute-start | bytes 786440 | tf_op jit(solution)/shard_map/ppermute | solution.py:361
  82.0 0.0 collective-permute-done.16.other.refs_6_
  82.0 1.0 copy-done.2
  83.0 3.5 %add_cores.3 = (bf16[64,16,128]{2,1,0:T(8,128)(2,1)}, bf16[64,16,128]{2,1,0:T(8,128)(2,1)}, bf16[64,16,128]{2,1,0:T(8,128)(2,1)}) custom-call(bf16[64,16,128]{2,1,0:T(8,128)(2,1)} %get-tuple-element.49.one, bf16[64,16,128]{2,1,0:T(8,128)(2,1)} %get-tuple-element.50.two, bf16[64,16,128]{2,1,0:T(8,128)(2,1)} %get-tuple-element.51.three, ...), custom_call_target="tpu_custom_call" | custom-call | tf_op jit(solution)/shard_map/add_cores/pallas_call | solution.py:169
  86.5 0.6 collective-permute-start.18
  87.1 2.2 %collective-permute-start.19 = (bf16[64,16,128]{2,1,0:T(8,128)(2,1)}, bf16[64,16,128]{2,1,0:T(8,128)(2,1)S(1)}, u32[]{:S(2)}, u32[]{:S(2)}) collective-permute-start(bf16[64,16,128]{2,1,0:T(8,128)(2,1)} %get-tuple-element.54), channel_id=1, source_target_pairs={{0,192},{64,0},{128,64},{192,128},{1,193},{65,1},{129,65},{193,129... | collective-permute-start | bytes 786440 | tf_op jit(solution)/shard_map/ppermute | solution.py:361
  89.3 0.2 convert_reduce_fusion
  89.5 0.7 fusion.1
  90.1 2.6 %collective-permute-done.13.refs_3_ = bf16[64,16,128]{2,1,0:T(8,128)(2,1)S(1)} collective-permute-done((bf16[64,16,128]{2,1,0:T(8,128)(2,1)}, bf16[64,16,128]{2,1,0:T(8,128)(2,1)S(1)}, u32[]{:S(2)}, u32[]{:S(2)}) %collective-permute-start.13) | collective-permute-done | bytes 262176 | tf_op jit(solution)/shard_map/ppermute | solution.py:361
  92.8 4.1 %collective-permute-done.17.refs_7_ = bf16[64,16,128]{2,1,0:T(8,128)(2,1)S(1)} collective-permute-done((bf16[64,16,128]{2,1,0:T(8,128)(2,1)}, bf16[64,16,128]{2,1,0:T(8,128)(2,1)S(1)}, u32[]{:S(2)}, u32[]{:S(2)}) %collective-permute-start.17) | collective-permute-done | bytes 262176 | tf_op jit(solution)/shard_map/ppermute | solution.py:361
  96.9 6.3 %collective-permute-done.18.refs_8_ = bf16[64,16,128]{2,1,0:T(8,128)(2,1)S(1)} collective-permute-done((bf16[64,16,128]{2,1,0:T(8,128)(2,1)}, bf16[64,16,128]{2,1,0:T(8,128)(2,1)S(1)}, u32[]{:S(2)}, u32[]{:S(2)}) %collective-permute-start.18) | collective-permute-done | bytes 262176 | tf_op jit(solution)/shard_map/ppermute | solution.py:361
  103.2 0.0 copy-start.3
  103.3 1.2 copy-done.3
  104.5 1.9 %to_slots.1 = bf16[160,16,128]{2,1,0:T(8,128)(2,1)} custom-call(s32[128]{0:T(128)S(1)} %get-tuple-element.62.slot, bf16[64,16,128]{2,1,0:T(8,128)(2,1)S(1)} %copy-done.4, bf16[4,64,16,128]{3,2,1,0:T(8,128)(2,1)S(1)} %copy-done.1, bf16[64,16,128]{2,1,0:T(8,128)(2,1)S(1)} %collective-permute-done.12.refs_2_, ...), custom_call_target="tpu_custom_call" | custom-call | tf_op jit(solution)/shard_map/to_slots/pallas_call | solution.py:199
  106.3 9.0 %all-to-all-start.1 = ((bf16[32,5,16,128]{3,2,1,0:T(8,128)(2,1)}), bf16[32,5,16,128]{3,2,1,0:T(8,128)(2,1)S(1)}, u32[]{:S(2)}, u32[]{:S(2)}) async-start(bf16[32,5,16,128]{3,2,1,0:T(8,128)(2,1)} %bitcast.6), calls=%async_computation.1 | async-start | bytes 1310720 | tf_op jit(solution)/shard_map/all_to_all | solution.py:324
  115.3 1.1 compare_convert_fusion.live
  116.5 11.8 %all-to-all-done.1.tiles = bf16[32,5,16,128]{3,2,1,0:T(8,128)(2,1)S(1)} async-done(((bf16[32,5,16,128]{3,2,1,0:T(8,128)(2,1)}), bf16[32,5,16,128]{3,2,1,0:T(8,128)(2,1)S(1)}, u32[]{:S(2)}, u32[]{:S(2)}) %all-to-all-start.1) | async-done | bytes 655392 | tf_op jit(solution)/shard_map/all_to_all | solution.py:324
  128.2 0.8 copy-done.9
  129.1 5.6 %update.1 = (bf16[32,5,16,128]{3,2,1,0:T(8,128)(2,1)}, bf16[5,256,256]{2,1,0:T(8,128)(2,1)}, bf16[1,5,256,256]{3,2,1,0:T(8,128)(2,1)}, bf16[1,5,256,256]{3,2,1,0:T(8,128)(2,1)}) custom-call(s32[5]{0:T(128)} %compare_convert_fusion.live, bf16[32,5,16,128]{3,2,1,0:T(8,128)(2,1)} %copy-done.9, bf16[1,5,256,256]{3,2,1,0:T(8,128)(2,1)} %basis_left.1, ...), custom_call_target="tpu_custom_call" | custom-call | tf_op jit(solution)/shard_map/update/pallas_call | solution.py:277
  134.6 17.1 %all_to_all.21 = bf16[32,5,16,128]{3,2,1,0:T(8,128)(2,1)S(1)} all-to-all(bf16[32,5,16,128]{3,2,1,0:T(8,128)(2,1)} %get-tuple-element.55), channel_id=1, replica_groups=mesh['y'=4,'x'=4,'core'=2,'z'=8] {'y','x','core'}, dimensions={0} | all-to-all | bytes 1310720 | tf_op jit(solution)/shard_map/all_to_all | solution.py:324
  151.7 1.6 from_slots.1
  153.3 4.1 %all-to-all-start.3 = ((bf16[32,4,16,128]{3,2,1,0:T(8,128)(2,1)}), bf16[32,4,16,128]{3,2,1,0:T(8,128)(2,1)S(1)}, u32[]{:S(2)}, u32[]{:S(2)}) async-start(bf16[32,4,16,128]{3,2,1,0:T(8,128)(2,1)} %bitcast.8), calls=%async_computation.3 | async-start | bytes 1048576 | tf_op jit(solution)/shard_map/all_to_all | solution.py:324
  157.4 6.1 %factors.1 = (f32[1,5,256,256]{3,2,1,0:T(8,128)}, f32[1,5,256,256]{3,2,1,0:T(8,128)}) custom-call(s32[5]{0:T(128)} %compare_convert_fusion.live, bf16[5,256,256]{2,1,0:T(8,128)(2,1)} %get-tuple-element.56.grads, f32[1,5,256,256]{3,2,1,0:T(8,128)} %left.1, f32[1,5,256,256]{3,2,1,0:T(8,128)} %right.1), custom_call_target="tpu_custom_call" | custom-call | flops 335544320 | bytes 6291456 | tf_op jit(solution)/shard_map/factors/pallas_call | solution.py:306
  163.5 5.5 %all-to-all-done.3.tiles = bf16[32,4,16,128]{3,2,1,0:T(8,128)(2,1)S(1)} async-done(((bf16[32,4,16,128]{3,2,1,0:T(8,128)(2,1)}), bf16[32,4,16,128]{3,2,1,0:T(8,128)(2,1)S(1)}, u32[]{:S(2)}, u32[]{:S(2)}) %all-to-all-start.3) | async-done | bytes 524320 | tf_op jit(solution)/shard_map/all_to_all | solution.py:324
  169.0 0.9 assemble.1
  (45 shorter events, 0.2 us)
Async XLA Ops:
  0.7 1.0 copy-start.6
  1.7 34.2 %copy-start.8 = (s32[4]{0:T(128)}, s32[4]{0:T(128)S(1)}, u32[]{:S(2)}) copy-start(s32[4]{0:T(128)S(1)} %pad_add_fusion.spot) | copy-start | bytes 52
  11.9 24.0 %collective-permute-start.4 = (bf16[8,32,2048]{2,1,0:T(8,128)(2,1)}, bf16[8,32,2048]{2,1,0:T(8,128)(2,1)S(1)}, u32[]{:S(2)}, u32[]{:S(2)}) collective-permute-start(bf16[8,32,2048]{2,1,0:T(8,128)(2,1)} %bitcast.13), channel_id=1, source_target_pairs={{0,16},{16,32},{32,48},{48,0},{1,17},{17,33},{33,49},{49,1},{2,18}... | collective-permute-start | bytes 3145736 | tf_op jit(solution)/shard_map/ppermute | solution.py:336
  12.2 23.6 %collective-permute-start.5 = (bf16[8,32,2048]{2,1,0:T(8,128)(2,1)}, bf16[8,32,2048]{2,1,0:T(8,128)(2,1)S(1)}, u32[]{:S(2)}, u32[]{:S(2)}) collective-permute-start(bf16[8,32,2048]{2,1,0:T(8,128)(2,1)} %bitcast.14), channel_id=1, source_target_pairs={{0,48},{16,0},{32,16},{48,32},{1,49},{17,1},{33,17},{49,33},{2,50}... | collective-permute-start | bytes 3145736 | tf_op jit(solution)/shard_map/ppermute | solution.py:336
  15.2 30.5 %copy-start.7 = (bf16[1024,128]{1,0:T(8,128)(2,1)}, bf16[1024,128]{1,0:T(8,128)(2,1)S(1)}, u32[]{:S(2)}) copy-start(bf16[1024,128]{1,0:T(8,128)(2,1)S(1)} %turn.1.refs_0_) | copy-start | bytes 786436
  15.2 6.2 %collective-permute-start = (bf16[1024,128]{1,0:T(8,128)(2,1)S(1)}, bf16[1024,128]{1,0:T(8,128)(2,1)S(1)}, u32[]{:S(2)}, u32[]{:S(2)}) collective-permute-start(bf16[1024,128]{1,0:T(8,128)(2,1)S(1)} %turn.1.refs_0_), channel_id=1, source_target_pairs={{0,1},{1,2},{2,3},{3,4},{4,5},{5,6},{6,7},{7,0},{8,9},{9,10},{10,1... | collective-permute-start | bytes 786440 | tf_op jit(solution)/shard_map/ppermute | solution.py:338
  18.2 6.7 %collective-permute-start.1 = (bf16[1024,128]{1,0:T(8,128)(2,1)S(1)}, bf16[1024,128]{1,0:T(8,128)(2,1)S(1)}, u32[]{:S(2)}, u32[]{:S(2)}) collective-permute-start(bf16[1024,128]{1,0:T(8,128)(2,1)S(1)} %turn.1.refs_0_), channel_id=1, source_target_pairs={{0,7},{1,0},{2,1},{3,2},{4,3},{5,4},{6,5},{7,6},{8,15},{9,8},{10,9... | collective-permute-start | bytes 786440 | tf_op jit(solution)/shard_map/ppermute | solution.py:338
  21.5 30.3 %copy-start.16 = (bf16[1024,128]{1,0:T(8,128)(2,1)}, bf16[1024,128]{1,0:T(8,128)(2,1)S(1)}, u32[]{:S(2)}) copy-start(bf16[1024,128]{1,0:T(8,128)(2,1)S(1)} %collective-permute-done.refs_1_) | copy-start | bytes 786436
  21.5 6.7 %collective-permute-start.2 = (bf16[1024,128]{1,0:T(8,128)(2,1)S(1)}, bf16[1024,128]{1,0:T(8,128)(2,1)S(1)}, u32[]{:S(2)}, u32[]{:S(2)}) collective-permute-start(bf16[1024,128]{1,0:T(8,128)(2,1)S(1)} %collective-permute-done.refs_1_), channel_id=1, source_target_pairs={{0,1},{1,2},{2,3},{3,4},{4,5},{5,6},{6,7},{7,0},{8,9},{9,10},{10,1... | collective-permute-start | bytes 786440 | tf_op jit(solution)/shard_map/ppermute | solution.py:340
  24.9 11.0 %copy-start.17 = (bf16[1024,128]{1,0:T(8,128)(2,1)}, bf16[1024,128]{1,0:T(8,128)(2,1)S(1)}, u32[]{:S(2)}) copy-start(bf16[1024,128]{1,0:T(8,128)(2,1)S(1)} %collective-permute-done.1.refs_2_) | copy-start | bytes 786436
  24.9 6.7 %collective-permute-start.3 = (bf16[1024,128]{1,0:T(8,128)(2,1)S(1)}, bf16[1024,128]{1,0:T(8,128)(2,1)S(1)}, u32[]{:S(2)}, u32[]{:S(2)}) collective-permute-start(bf16[1024,128]{1,0:T(8,128)(2,1)S(1)} %collective-permute-done.1.refs_2_), channel_id=1, source_target_pairs={{0,7},{1,0},{2,1},{3,2},{4,3},{5,4},{6,5},{7,6},{8,15},{9,8},{10,9... | collective-permute-start | bytes 786440 | tf_op jit(solution)/shard_map/ppermute | solution.py:340
  28.2 13.5 %copy-start.18 = (bf16[1024,128]{1,0:T(8,128)(2,1)}, bf16[1024,128]{1,0:T(8,128)(2,1)S(1)}, u32[]{:S(2)}) copy-start(bf16[1024,128]{1,0:T(8,128)(2,1)S(1)} %collective-permute-done.2.refs_3_) | copy-start | bytes 786436
  31.6 19.5 %copy-start.19 = (bf16[1024,128]{1,0:T(8,128)(2,1)}, bf16[1024,128]{1,0:T(8,128)(2,1)S(1)}, u32[]{:S(2)}) copy-start(bf16[1024,128]{1,0:T(8,128)(2,1)S(1)} %collective-permute-done.3.refs_4_) | copy-start | bytes 786436
  35.9 9.8 %copy-start.10 = (bf16[8,32,2048]{2,1,0:T(8,128)(2,1)}, bf16[8,32,2048]{2,1,0:T(8,128)(2,1)S(1)}, u32[]{:S(2)}) copy-start(bf16[8,32,2048]{2,1,0:T(8,128)(2,1)S(1)} %collective-permute-done.4.refs_10_) | copy-start | bytes 3145732
  35.9 9.8 %copy-start.11 = (bf16[8,32,2048]{2,1,0:T(8,128)(2,1)}, bf16[8,32,2048]{2,1,0:T(8,128)(2,1)S(1)}, u32[]{:S(2)}) copy-start(bf16[8,32,2048]{2,1,0:T(8,128)(2,1)S(1)} %collective-permute-done.5.refs_11_) | copy-start | bytes 3145732
  35.9 15.8 %collective-permute-start.10 = (bf16[8,32,1024]{2,1,0:T(8,128)(2,1)S(1)}, bf16[8,32,1024]{2,1,0:T(8,128)(2,1)S(1)}, u32[]{:S(2)}, u32[]{:S(2)}) collective-permute-start(bf16[8,32,1024]{2,1,0:T(8,128)(2,1)S(1)} %slice.14), channel_id=1, source_target_pairs={{0,16},{16,32},{32,48},{48,0},{1,17},{17,33},{33,49},{49,1},{2,18}... | collective-permute-start | bytes 1572872 | tf_op jit(solution)/shard_map/ppermute | solution.py:345
  36.0 6.2 %collective-permute-start.6 = (bf16[1024,128]{1,0:T(8,128)(2,1)S(1)}, bf16[1024,128]{1,0:T(8,128)(2,1)S(1)}, u32[]{:S(2)}, u32[]{:S(2)}) collective-permute-start(bf16[1024,128]{1,0:T(8,128)(2,1)S(1)} %collective-permute-done.2.refs_3_), channel_id=1, source_target_pairs={{0,1},{1,2},{2,3},{3,4},{4,5},{5,6},{6,7},{7,0},{8,9},{9,10},{10,1... | collective-permute-start | bytes 786440 | tf_op jit(solution)/shard_map/ppermute | solution.py:348
  39.0 6.7 %collective-permute-start.7 = (bf16[1024,128]{1,0:T(8,128)(2,1)S(1)}, bf16[1024,128]{1,0:T(8,128)(2,1)S(1)}, u32[]{:S(2)}, u32[]{:S(2)}) collective-permute-start(bf16[1024,128]{1,0:T(8,128)(2,1)S(1)} %collective-permute-done.3.refs_4_), channel_id=1, source_target_pairs={{0,7},{1,0},{2,1},{3,2},{4,3},{5,4},{6,5},{7,6},{8,15},{9,8},{10,9... | collective-permute-start | bytes 786440 | tf_op jit(solution)/shard_map/ppermute | solution.py:348
  39.0 25.8 %collective-permute-start.15 = (bf16[8,32,1024]{2,1,0:T(8,128)(2,1)S(1)}, bf16[8,32,1024]{2,1,0:T(8,128)(2,1)}, u32[]{:S(2)}, u32[]{:S(2)}) collective-permute-start(bf16[8,32,1024]{2,1,0:T(8,128)(2,1)S(1)} %slice.15), channel_id=1, source_target_pairs={{0,48},{16,0},{32,16},{48,32},{1,49},{17,1},{33,17},{49,33},{2,50}... | collective-permute-start | bytes 1572872 | tf_op jit(solution)/shard_map/ppermute | solution.py:346
  42.3 9.5 %copy-start.12 = (bf16[1024,128]{1,0:T(8,128)(2,1)}, bf16[1024,128]{1,0:T(8,128)(2,1)S(1)}, u32[]{:S(2)}) copy-start(bf16[1024,128]{1,0:T(8,128)(2,1)S(1)} %collective-permute-done.6.refs_5_) | copy-start | bytes 786436
  42.3 5.1 %collective-permute-start.8 = (bf16[512,128]{1,0:T(8,128)(2,1)S(1)}, bf16[512,128]{1,0:T(8,128)(2,1)S(1)}, u32[]{:S(2)}, u32[]{:S(2)}) collective-permute-start(bf16[512,128]{1,0:T(8,128)(2,1)S(1)} %slice.16), channel_id=1, source_target_pairs={{0,1},{1,2},{2,3},{3,4},{4,5},{5,6},{6,7},{7,0},{8,9},{9,10},{10,1... | collective-permute-start | bytes 393224 | tf_op jit(solution)/shard_map/ppermute | solution.py:351
  45.7 6.1 %copy-start.13 = (bf16[1024,128]{1,0:T(8,128)(2,1)}, bf16[1024,128]{1,0:T(8,128)(2,1)S(1)}, u32[]{:S(2)}) copy-start(bf16[1024,128]{1,0:T(8,128)(2,1)S(1)} %collective-permute-done.7.refs_6_) | copy-start | bytes 786436
  45.7 5.4 %collective-permute-start.9 = (bf16[512,128]{1,0:T(8,128)(2,1)S(1)}, bf16[512,128]{1,0:T(8,128)(2,1)S(1)}, u32[]{:S(2)}, u32[]{:S(2)}) collective-permute-start(bf16[512,128]{1,0:T(8,128)(2,1)S(1)} %slice.17), channel_id=1, source_target_pairs={{0,7},{1,0},{2,1},{3,2},{4,3},{5,4},{6,5},{7,6},{8,15},{9,8},{10,9... | collective-permute-start | bytes 393224 | tf_op jit(solution)/shard_map/ppermute | solution.py:352
  47.4 4.4 %copy-start.20 = (bf16[512,128]{1,0:T(8,128)(2,1)}, bf16[512,128]{1,0:T(8,128)(2,1)S(1)}, u32[]{:S(2)}) copy-start(bf16[512,128]{1,0:T(8,128)(2,1)S(1)} %collective-permute-done.8.refs_7_) | copy-start | bytes 393220
  51.1 0.7 copy-start.21
  51.8 0.8 copy-start.15
  59.5 12.3 %collective-permute-start.11 = (bf16[4,64,16,128]{3,2,1,0:T(8,128)(2,1)}, bf16[4,64,16,128]{3,2,1,0:T(8,128)(2,1)S(1)}, u32[]{:S(2)}, u32[]{:S(2)}) collective-permute-start(bf16[4,64,16,128]{3,2,1,0:T(8,128)(2,1)} %get-tuple-element.40), channel_id=1, source_target_pairs={{0,8},{8,0},{1,9},{9,1},{2,10},{10,2},{3,11},{11,3},{4,12},{12,4},... | collective-permute-start | bytes 3145736 | tf_op jit(solution)/shard_map/ppermute | solution.py:358
  71.7 10.3 %collective-permute-start.16 = (bf16[4,64,16,128]{3,2,1,0:T(8,128)(2,1)}, bf16[4,64,16,128]{3,2,1,0:T(8,128)(2,1)S(1)}, u32[]{:S(2)}, u32[]{:S(2)}) collective-permute-start(bf16[4,64,16,128]{3,2,1,0:T(8,128)(2,1)} %get-tuple-element.48), channel_id=1, source_target_pairs={{0,8},{8,0},{1,9},{9,1},{2,10},{10,2},{3,11},{11,3},{4,12},{12,4},... | collective-permute-start | bytes 3145736 | tf_op jit(solution)/shard_map/ppermute | solution.py:358
  71.8 1.0 copy-start
  76.3 13.0 %copy-start.14 = (s32[1,128]{1,0:T(1,128)S(1)}, s32[1,128]{1,0:T(1,128)}, u32[]{:S(2)}) copy-start(s32[1,128]{1,0:T(1,128)} %param.11) | copy-start | bytes 1540
  76.3 26.9 %copy-start.1 = (bf16[4,64,16,128]{3,2,1,0:T(8,128)(2,1)S(1)}, bf16[4,64,16,128]{3,2,1,0:T(8,128)(2,1)}, u32[]{:S(2)}) copy-start(bf16[4,64,16,128]{3,2,1,0:T(8,128)(2,1)} %copy-done) | copy-start | bytes 3145732
  76.3 26.9 %copy-start.4 = (bf16[64,16,128]{2,1,0:T(8,128)(2,1)S(1)}, bf16[64,16,128]{2,1,0:T(8,128)(2,1)}, u32[]{:S(2)}) copy-start(bf16[64,16,128]{2,1,0:T(8,128)(2,1)} %get-tuple-element.39.refs_0_) | copy-start | bytes 786436
  76.3 26.9 %copy-start.5 = (bf16[64,16,128]{2,1,0:T(8,128)(2,1)S(1)}, bf16[64,16,128]{2,1,0:T(8,128)(2,1)}, u32[]{:S(2)}) copy-start(bf16[64,16,128]{2,1,0:T(8,128)(2,1)} %get-tuple-element.47.refs_5_) | copy-start | bytes 786436
  76.3 10.8 %collective-permute-start.12 = (bf16[64,16,128]{2,1,0:T(8,128)(2,1)}, bf16[64,16,128]{2,1,0:T(8,128)(2,1)S(1)}, u32[]{:S(2)}, u32[]{:S(2)}) collective-permute-start(bf16[64,16,128]{2,1,0:T(8,128)(2,1)} %get-tuple-element.44), channel_id=1, source_target_pairs={{0,128},{64,192},{128,0},{192,64},{1,129},{65,193},{129,1},{193,65... | collective-permute-start | bytes 786440 | tf_op jit(solution)/shard_map/ppermute | solution.py:361
  79.3 13.4 %collective-permute-start.13 = (bf16[64,16,128]{2,1,0:T(8,128)(2,1)}, bf16[64,16,128]{2,1,0:T(8,128)(2,1)S(1)}, u32[]{:S(2)}, u32[]{:S(2)}) collective-permute-start(bf16[64,16,128]{2,1,0:T(8,128)(2,1)} %get-tuple-element.45), channel_id=1, source_target_pairs={{0,64},{64,128},{128,192},{192,0},{1,65},{65,129},{129,193},{193,1... | collective-permute-start | bytes 786440 | tf_op jit(solution)/shard_map/ppermute | solution.py:361
  79.7 13.0 %collective-permute-start.14 = (bf16[64,16,128]{2,1,0:T(8,128)(2,1)}, bf16[64,16,128]{2,1,0:T(8,128)(2,1)S(1)}, u32[]{:S(2)}, u32[]{:S(2)}) collective-permute-start(bf16[64,16,128]{2,1,0:T(8,128)(2,1)} %get-tuple-element.46), channel_id=1, source_target_pairs={{0,192},{64,0},{128,64},{192,128},{1,193},{65,1},{129,65},{193,129... | collective-permute-start | bytes 786440 | tf_op jit(solution)/shard_map/ppermute | solution.py:361
  82.0 1.0 copy-start.2
  86.5 10.4 %collective-permute-start.17 = (bf16[64,16,128]{2,1,0:T(8,128)(2,1)}, bf16[64,16,128]{2,1,0:T(8,128)(2,1)S(1)}, u32[]{:S(2)}, u32[]{:S(2)}) collective-permute-start(bf16[64,16,128]{2,1,0:T(8,128)(2,1)} %get-tuple-element.52), channel_id=1, source_target_pairs={{0,128},{64,192},{128,0},{192,64},{1,129},{65,193},{129,1},{193,65... | collective-permute-start | bytes 786440 | tf_op jit(solution)/shard_map/ppermute | solution.py:361
  86.5 16.7 %collective-permute-start.18 = (bf16[64,16,128]{2,1,0:T(8,128)(2,1)}, bf16[64,16,128]{2,1,0:T(8,128)(2,1)S(1)}, u32[]{:S(2)}, u32[]{:S(2)}) collective-permute-start(bf16[64,16,128]{2,1,0:T(8,128)(2,1)} %get-tuple-element.53), channel_id=1, source_target_pairs={{0,64},{64,128},{128,192},{192,0},{1,65},{65,129},{129,193},{193,1... | collective-permute-start | bytes 786440 | tf_op jit(solution)/shard_map/ppermute | solution.py:361
  87.1 16.1 %collective-permute-start.19 = (bf16[64,16,128]{2,1,0:T(8,128)(2,1)}, bf16[64,16,128]{2,1,0:T(8,128)(2,1)S(1)}, u32[]{:S(2)}, u32[]{:S(2)}) collective-permute-start(bf16[64,16,128]{2,1,0:T(8,128)(2,1)} %get-tuple-element.54), channel_id=1, source_target_pairs={{0,192},{64,0},{128,64},{192,128},{1,193},{65,1},{129,65},{193,129... | collective-permute-start | bytes 786440 | tf_op jit(solution)/shard_map/ppermute | solution.py:361
  103.2 1.2 copy-start.3
  106.3 21.9 %all-to-all-start.1 = ((bf16[32,5,16,128]{3,2,1,0:T(8,128)(2,1)}), bf16[32,5,16,128]{3,2,1,0:T(8,128)(2,1)S(1)}, u32[]{:S(2)}, u32[]{:S(2)}) async-start(bf16[32,5,16,128]{3,2,1,0:T(8,128)(2,1)} %bitcast.6), calls=%async_computation.1 | async-start | bytes 1310720 | tf_op jit(solution)/shard_map/all_to_all | solution.py:324
  128.2 0.8 copy-start.9
  153.3 15.8 %all-to-all-start.3 = ((bf16[32,4,16,128]{3,2,1,0:T(8,128)(2,1)}), bf16[32,4,16,128]{3,2,1,0:T(8,128)(2,1)S(1)}, u32[]{:S(2)}, u32[]{:S(2)}) async-start(bf16[32,4,16,128]{3,2,1,0:T(8,128)(2,1)} %bitcast.8), calls=%async_computation.3 | async-start | bytes 1048576 | tf_op jit(solution)/shard_map/all_to_all | solution.py:324

commit v5 on v4

--- a/solution.py
+++ b/solution.py
@@ -24,7 +24,6 @@
 DP = ("y", "x", "core")
 CHIP_ROWS = LOCAL_ROWS * CORE
 SHARD_K = X * TOK_SUB
-SOURCES = (0, -1, 1, 2)
 WIDE = 2
 CHUNK_K = NBLK // 2
 
@@ -48,46 +47,53 @@
     return slice(top, top + TILE_ROWS), slice(side, side + TILE_COLS)
 
 
-def cut_kernel(spot, tokens, out):
-    def strips_from(first):
-        for chip in range(X):
-            for i in range(CORE):
-                start = STRIP * (chip * CORE + (first + i) % CORE)
-                out[chip, :, i * LOCAL_ROWS : (i + 1) * LOCAL_ROWS] = jnp.concatenate(
-                    [
-                        tokens[:, r * BLOCK + start : r * BLOCK + start + STRIP]
-                        for r in range(ROW_BLOCKS)
-                    ],
-                    axis=1,
-                )
-
-    for first in range(CORE):
-        pl.when(spot[2] == first)(lambda: strips_from(first))
+def cut_kernel(spot, tokens, *refs):
+    outs, (held, pieces, sem) = refs[:X], refs[X:]
+    copy = pltpu.make_async_copy(tokens, held, sem)
+    copy.start()
+    copy.wait()
+    for strip in range(ROW):
+        pieces[strip // CORE, strip % CORE] = jnp.concatenate(
+            [
+                held[:, r * BLOCK + STRIP * strip : r * BLOCK + STRIP * (strip + 1)]
+                for r in range(ROW_BLOCKS)
+            ],
+            axis=1,
+        )
+    for step in range(X):
+        chip = (spot[1] + step) % X
+        for i in range(CORE):
+            core = (spot[2] + i) % CORE
+            outs[step][:, i * LOCAL_ROWS : (i + 1) * LOCAL_ROWS] = pieces[chip, core]
 
 
 def cut_tokens(spot, tokens):
     return pl.pallas_call(
         cut_kernel,
-        in_specs=[SMEM, VMEM],
-        out_shape=jax.ShapeDtypeStruct((X, TOK_SUB, CHIP_ROWS), jnp.bfloat16),
-        compiler_params=params(32),
+        in_specs=[SMEM, pl.BlockSpec(memory_space=pl.ANY)],
+        out_shape=[jax.ShapeDtypeStruct((TOK_SUB, CHIP_ROWS), jnp.bfloat16)] * X,
+        scratch_shapes=[
+            pltpu.VMEM(tokens.shape, jnp.bfloat16),
+            pltpu.VMEM((X, CORE, TOK_SUB, LOCAL_ROWS), jnp.bfloat16),
+            pltpu.SemaphoreType.DMA(()),
+        ],
+        compiler_params=params(16),
         name="cut_tokens",
     )(spot, tokens)
 
 
-def turn_kernel(spot, pieces, out):
-    joined = [pieces[(spot[1] + step + X) % X] for step in SOURCES]
-    out[...] = jnp.concatenate(joined, axis=0).T
-
-
-def turn(spot, pieces):
+def turn_kernel(*refs):
+    out = refs[X]
+    out[...] = jnp.concatenate([piece[...] for piece in refs[:X]], axis=0).T
+
+
+def turn(pieces):
     return pl.pallas_call(
         turn_kernel,
-        in_specs=[SMEM, VMEM],
         out_shape=jax.ShapeDtypeStruct((CHIP_ROWS, SHARD_K), jnp.bfloat16),
-        compiler_params=params(32),
+        compiler_params=params(16),
         name="turn",
-    )(spot, pieces)
+    )(*pieces)
 
 
 def gradient_kernel(spot, *refs):
@@ -147,7 +153,7 @@
         ),
         out_shape=[jax.ShapeDtypeStruct((CHUNK_K, TILE_ROWS, TILE_COLS), jnp.bfloat16)] * Y
         + [jax.ShapeDtypeStruct((Y, CHUNK_K, TILE_ROWS, TILE_COLS), jnp.bfloat16)],
-        compiler_params=params(60),
+        compiler_params=params(30),
         cost_estimate=pl.CostEstimate(
             flops=2 * CHIP_ROWS * N_TENSOR * SHARD_K * 4 * BLOCK,
             bytes_accessed=8 * MIB, transcendentals=0,
@@ -173,7 +179,7 @@
         + [pl.BlockSpec((Y, blocks, TILE_ROWS, TILE_COLS), lambda c: (0, c, 0, 0))],
         out_specs=[part] * 3,
         out_shape=[jax.ShapeDtypeStruct(a.shape, a.dtype) for a in parts[1:]],
-        compiler_params=params(60),
+        compiler_params=params(16),
         name="add_cores",
     )(*parts[1:], other)
 
@@ -200,7 +206,7 @@
         to_slots_kernel,
         in_specs=[SMEM] + [VMEM] * len(flat),
         out_shape=jax.ShapeDtypeStruct((N_DP * SLOTS, TILE_ROWS, TILE_COLS), jnp.bfloat16),
-        compiler_params=params(32),
+        compiler_params=params(16),
         name="to_slots",
     )(slot, *flat)
 
@@ -218,7 +224,7 @@
         from_slots_kernel,
         in_specs=[SMEM, VMEM],
         out_shape=jax.ShapeDtypeStruct((NBLK, TILE_ROWS, TILE_COLS), jnp.bfloat16),
-        compiler_params=params(32),
+        compiler_params=params(16),
         name="from_slots",
     )(slot, tiles)
 
@@ -234,7 +240,7 @@
     return pl.pallas_call(
         assemble_kernel,
         out_shape=jax.ShapeDtypeStruct((1, HOME, BLOCK, BLOCK), jnp.bfloat16),
-        compiler_params=params(32),
+        compiler_params=params(16),
         name="assemble",
     )(tiles)
 
@@ -283,7 +289,7 @@
             like(first),
             like(second),
         ],
-        compiler_params=params(60),
+        compiler_params=params(63),
         name="update",
     )(live, tiles, basis_left, basis_right, first, second)
 
@@ -312,7 +318,7 @@
             out_specs=[state] * 2,
         ),
         out_shape=[jax.ShapeDtypeStruct(a.shape, a.dtype) for a in (left, right)],
-        compiler_params=params(60),
+        compiler_params=params(32),
         cost_estimate=pl.CostEstimate(
             flops=4 * SLOTS * BLOCK**3, bytes_accessed=6 * MIB, transcendentals=0
         ),
@@ -332,9 +338,11 @@
     up, down = ring(N_TENSOR, 1), ring(N_TENSOR, -1)
     ahead, back = ring(X, 1), ring(X, -1)
 
-    pieces, grads = lax.optimization_barrier((spread(cut_tokens(spot, tokens), "x"), grads))
+    cut = cut_tokens(spot, tokens)
+    pieces = [cut[0]] + [lax.ppermute(cut[step], "x", ring(X, step)) for step in (1, 3, 2)]
+    pieces, grads = lax.optimization_barrier((pieces, grads))
     behind, before = lax.ppermute(grads, "x", ahead), lax.ppermute(grads, "x", back)
-    mine = turn(spot, pieces)
+    mine = turn(pieces)
     below, above = lax.ppermute(mine, "z", up), lax.ppermute(mine, "z", down)
     whole = [mine, below, above]
     below, above = lax.ppermute(below, "z", up), lax.ppermute(above, "z", down)

time: 171 us -> 158 us (0.924)
  Pallas kernels: 38.2 us -> 26.4 us
  blocking collectives: 26.5 us -> 17.2 us
  waiting for transfers between devices: 50.8 us -> 57.7 us
  starting transfers between devices: 44.9 us -> 50.4 us
  local copies, waits for them, and re-layouts: 6.54 us -> 2.98 us
    all_to_all x2 -> x1, blocking collectives: 26.5 us -> 17.2 us  [spread(): return lax.all_to_all(array, axes, split_axis=0, concat_axis=0, tiled=True)]
    pallas_call x2, Pallas kernels: 13.7 us -> 8.23 us  [gradient_tiles(): pl.pallas_call(gradient_kernel, grid_spec=pltpu.PrefetchScalarGridSpec(nu...]
    ppermute x0 -> x3, starting transfers between devices: none -> 4.29 us  [gather_row(): lax.ppermute(cut[step], 'x', ring(X, step))]
    pallas_call x2, Pallas kernels: 7.02 us -> 3 us  [add_cores(): pl.pallas_call(add_cores_kernel, grid=(4,), in_specs=[part] * 3 + [pl.Blo...]
    unnamed x44 -> x16, local copies, waits for them, and re-layouts: 6.45 us -> 2.89 us
    ppermute x0 -> x3, waiting for transfers between devices: none -> 3.09 us  [gather_row(): lax.ppermute(cut[step], 'x', ring(X, step))]
    pallas_call x1, Pallas kernels: 6.13 us -> 3.71 us  [update_factors(): pl.pallas_call(factor_kernel, grid_spec=pltpu.PrefetchScalarGridSpec(num_...]
    ppermute x6, waiting for transfers between devices: 13.1 us -> 15.4 us  [sum_parts(): lax.ppermute(a, 'y', ring(Y, step))]
  transfers between devices with their start and end apart: 22 -> 25, of which waited for: 13 -> 16; matrix products, arithmetic and copies ran while one was open for 1% -> 1% of each run, Pallas kernels for 16% -> 10%
where the time goes in v5:
time: 158 us; the launch traced here: 157 us
  waiting for transfers between devices  57.7 us (37%)
  starting transfers between devices  50.4 us (32%)
  Pallas kernels  26.4 us (17%)
  blocking collectives  17.2 us (11%)
  local copies, waits for them, and re-layouts  2.98 us (2%)
  other arithmetic  1.9 us (1%)
    all_to_all x2, waiting for transfers between devices, spread(): return lax.all_to_all(array, axes, split_axis=0, concat_axis=0, tiled=True)  18.7 us
    all_to_all x1, blocking collectives, spread(): return lax.all_to_all(array, axes, split_axis=0, concat_axis=0, tiled=True)  17.2 us
    ppermute x6, waiting for transfers between devices, sum_parts(): lax.ppermute(a, 'y', ring(Y, step))  15.4 us
    all_to_all x2, starting transfers between devices, spread(): return lax.all_to_all(array, axes, split_axis=0, concat_axis=0, tiled=True)  13 us
    ppermute x6, starting transfers between devices, sum_parts(): lax.ppermute(a, 'y', ring(Y, step))  8.95 us
    pallas_call x2, Pallas kernels, gradient_tiles(): pl.pallas_call(gradient_kernel, grid_spec=pltpu.PrefetchScalarGridSpec(nu...  8.23 us
    ppermute x2, starting transfers between devices, gather_row(): lax.ppermute(below, 'z', up)  6.34 us
    ppermute x2, starting transfers between devices, sum_parts(): mine, other = (parts[:Y], lax.ppermute(parts[Y], 'core', ring(CORE, 1)))  6.06 us
  transfers between devices with their start and end apart: 25, of which 16 were waited for; matrix products, arithmetic and copies ran while one was open for 1% of the time, Pallas kernels for 10%

profile of v5, /device:TPU:97, one launch (start us, length us, event | category | flops | bytes accessed | tf_op | source)
XLA Modules:
  0.0 157.5 jit_solution(3053936637602434902)
XLA Ops:
  0.6 0.1 pad_add_fusion.spot
  0.7 0.9 copy-done.3
  1.7 0.9 cut_tokens.1
  2.5 1.3 collective-permute-start
  3.8 1.5 collective-permute-start.1
  5.3 1.5 collective-permute-start.2
  6.8 0.1 collective-permute-done.refs_1_
  6.9 0.0 collective-permute-done.1.refs_2_
  6.9 3.0 %collective-permute-done.2.refs_3_ = bf16[32,1024]{1,0:T(8,128)(2,1)S(1)} collective-permute-done((bf16[32,1024]{1,0:T(8,128)(2,1)S(1)}, bf16[32,1024]{1,0:T(8,128)(2,1)S(1)}, u32[]{:S(2)}, u32[]{:S(2)}) %collective-permute-start.2) | collective-permute-done | bytes 65568 | tf_op jit(solution)/shard_map/ppermute | solution.py:342
  9.9 0.4 collective-permute-start.7
  10.3 2.3 %collective-permute-start.8 = (bf16[8,32,2048]{2,1,0:T(8,128)(2,1)}, bf16[8,32,2048]{2,1,0:T(8,128)(2,1)S(1)}, u32[]{:S(2)}, u32[]{:S(2)}) collective-permute-start(bf16[8,32,2048]{2,1,0:T(8,128)(2,1)} %bitcast.13), channel_id=1, source_target_pairs={{0,48},{16,0},{32,16},{48,32},{1,49},{17,1},{33,17},{49,33},{2,50}... | collective-permute-start | bytes 3145736 | tf_op jit(solution)/shard_map/ppermute | solution.py:344
  12.6 0.1 turn.1.refs_0_
  12.7 0.0 copy-start.5
  12.7 2.9 %collective-permute-start.3 = (bf16[1024,128]{1,0:T(8,128)(2,1)S(1)}, bf16[1024,128]{1,0:T(8,128)(2,1)S(1)}, u32[]{:S(2)}, u32[]{:S(2)}) collective-permute-start(bf16[1024,128]{1,0:T(8,128)(2,1)S(1)} %turn.1.refs_0_), channel_id=1, source_target_pairs={{0,1},{1,2},{2,3},{3,4},{4,5},{5,6},{6,7},{7,0},{8,9},{9,10},{10,1... | collective-permute-start | bytes 786440 | tf_op jit(solution)/shard_map/ppermute | solution.py:346
  15.7 0.0 collective-permute-start.4
  15.7 3.3 %collective-permute-done.3.refs_1_ = bf16[1024,128]{1,0:T(8,128)(2,1)S(1)} collective-permute-done((bf16[1024,128]{1,0:T(8,128)(2,1)S(1)}, bf16[1024,128]{1,0:T(8,128)(2,1)S(1)}, u32[]{:S(2)}, u32[]{:S(2)}) %collective-permute-start.3) | collective-permute-done | bytes 262176 | tf_op jit(solution)/shard_map/ppermute | solution.py:346
  19.0 3.4 %collective-permute-start.5 = (bf16[1024,128]{1,0:T(8,128)(2,1)S(1)}, bf16[1024,128]{1,0:T(8,128)(2,1)S(1)}, u32[]{:S(2)}, u32[]{:S(2)}) collective-permute-start(bf16[1024,128]{1,0:T(8,128)(2,1)S(1)} %collective-permute-done.3.refs_1_), channel_id=1, source_target_pairs={{0,1},{1,2},{2,3},{3,4},{4,5},{5,6},{6,7},{7,0},{8,9},{9,10},{10,1... | collective-permute-start | bytes 786440 | tf_op jit(solution)/shard_map/ppermute | solution.py:348
  22.4 0.0 collective-permute-done.4.refs_2_
  22.4 0.0 collective-permute-start.6
  22.4 3.3 %collective-permute-done.5.refs_3_ = bf16[1024,128]{1,0:T(8,128)(2,1)S(1)} collective-permute-done((bf16[1024,128]{1,0:T(8,128)(2,1)S(1)}, bf16[1024,128]{1,0:T(8,128)(2,1)S(1)}, u32[]{:S(2)}, u32[]{:S(2)}) %collective-permute-start.5) | collective-permute-done | bytes 262176 | tf_op jit(solution)/shard_map/ppermute | solution.py:348
  25.7 3.4 %collective-permute-done.6.refs_4_ = bf16[1024,128]{1,0:T(8,128)(2,1)S(1)} collective-permute-done((bf16[1024,128]{1,0:T(8,128)(2,1)S(1)}, bf16[1024,128]{1,0:T(8,128)(2,1)S(1)}, u32[]{:S(2)}, u32[]{:S(2)}) %collective-permute-start.6) | collective-permute-done | bytes 262176 | tf_op jit(solution)/shard_map/ppermute | solution.py:348
  29.1 4.5 %collective-permute-done.7.refs_10_ = bf16[8,32,2048]{2,1,0:T(8,128)(2,1)S(1)} collective-permute-done((bf16[8,32,2048]{2,1,0:T(8,128)(2,1)}, bf16[8,32,2048]{2,1,0:T(8,128)(2,1)S(1)}, u32[]{:S(2)}, u32[]{:S(2)}) %collective-permute-start.7) | collective-permute-done | bytes 1048608 | tf_op jit(solution)/shard_map/ppermute | solution.py:344
  33.6 0.0 collective-permute-done.8.refs_11_
  33.7 0.1 collective-permute-start.13
  33.7 2.9 %collective-permute-start.9 = (bf16[1024,128]{1,0:T(8,128)(2,1)S(1)}, bf16[1024,128]{1,0:T(8,128)(2,1)S(1)}, u32[]{:S(2)}, u32[]{:S(2)}) collective-permute-start(bf16[1024,128]{1,0:T(8,128)(2,1)S(1)} %collective-permute-done.5.refs_3_), channel_id=1, source_target_pairs={{0,1},{1,2},{2,3},{3,4},{4,5},{5,6},{6,7},{7,0},{8,9},{9,10},{10,1... | collective-permute-start | bytes 786440 | tf_op jit(solution)/shard_map/ppermute | solution.py:356
  36.7 2.7 %collective-permute-start.18 = (bf16[8,32,1024]{2,1,0:T(8,128)(2,1)S(1)}, bf16[8,32,1024]{2,1,0:T(8,128)(2,1)S(1)}, u32[]{:S(2)}, u32[]{:S(2)}) collective-permute-start(bf16[8,32,1024]{2,1,0:T(8,128)(2,1)S(1)} %slice.15), channel_id=1, source_target_pairs={{0,48},{16,0},{32,16},{48,32},{1,49},{17,1},{33,17},{49,33},{2,50}... | collective-permute-start | bytes 1572872 | tf_op jit(solution)/shard_map/ppermute | solution.py:354
  39.4 0.6 collective-permute-done.9.refs_5_
  40.0 3.2 %collective-permute-start.11 = (bf16[512,128]{1,0:T(8,128)(2,1)S(1)}, bf16[512,128]{1,0:T(8,128)(2,1)S(1)}, u32[]{:S(2)}, u32[]{:S(2)}) collective-permute-start(bf16[512,128]{1,0:T(8,128)(2,1)S(1)} %slice.16), channel_id=1, source_target_pairs={{0,1},{1,2},{2,3},{3,4},{4,5},{5,6},{6,7},{7,0},{8,9},{9,10},{10,1... | collective-permute-start | bytes 393224 | tf_op jit(solution)/shard_map/ppermute | solution.py:359
  43.2 0.2 collective-permute-done.10.refs_6_
  43.4 0.3 collective-permute-start.12
  43.7 1.7 %collective-permute-done.11.refs_7_ = bf16[512,128]{1,0:T(8,128)(2,1)S(1)} collective-permute-done((bf16[512,128]{1,0:T(8,128)(2,1)S(1)}, bf16[512,128]{1,0:T(8,128)(2,1)S(1)}, u32[]{:S(2)}, u32[]{:S(2)}) %collective-permute-start.11) | collective-permute-done | bytes 131104 | tf_op jit(solution)/shard_map/ppermute | solution.py:359
  45.3 3.5 %collective-permute-done.12.refs_8_ = bf16[512,128]{1,0:T(8,128)(2,1)S(1)} collective-permute-done((bf16[512,128]{1,0:T(8,128)(2,1)S(1)}, bf16[512,128]{1,0:T(8,128)(2,1)S(1)}, u32[]{:S(2)}, u32[]{:S(2)}) %collective-permute-start.12) | collective-permute-done | bytes 131104 | tf_op jit(solution)/shard_map/ppermute | solution.py:360
  48.9 0.0 collective-permute-done.13.refs_12_
  48.9 4.1 %gradient_tiles.2 = (bf16[64,16,128]{2,1,0:T(8,128)(2,1)S(1)}, bf16[64,16,128]{2,1,0:T(8,128)(2,1)S(1)}, bf16[64,16,128]{2,1,0:T(8,128)(2,1)S(1)}, bf16[64,16,12...) custom-call(s32[4]{0:T(128)S(1)} %pad_add_fusion.spot, bf16[1024,128]{1,0:T(8,128)(2,1)S(1)} %turn.1.refs_0_, ...), custom_call_target="tpu_custom_call" | custom-call | flops 2147483648 | bytes 8388608 | tf_op jit(solution)/shard_map/gradient_tiles/pallas_call | solution.py:140
  53.0 5.9 %collective-permute-start.14 = (bf16[4,64,16,128]{3,2,1,0:T(8,128)(2,1)S(1)}, bf16[4,64,16,128]{3,2,1,0:T(8,128)(2,1)S(1)}, u32[]{:S(2)}, u32[]{:S(2)}) collective-permute-start(bf16[4,64,16,128]{3,2,1,0:T(8,128)(2,1)S(1)} %get-tuple-element.54), channel_id=1, source_target_pairs={{0,8},{8,0},{1,9},{9,1},{2,10},{10,2},{3,11},{11,3},{4,12},{12,4},... | collective-permute-start | bytes 3145736 | tf_op jit(solution)/shard_map/ppermute | solution.py:366
  59.0 0.0 collective-permute-done.18.refs_12_
  59.0 4.1 %gradient_tiles.3 = (bf16[64,16,128]{2,1,0:T(8,128)(2,1)S(1)}, bf16[64,16,128]{2,1,0:T(8,128)(2,1)S(1)}, bf16[64,16,128]{2,1,0:T(8,128)(2,1)S(1)}, bf16[64,16,12...) custom-call(s32[4]{0:T(128)S(1)} %pad_add_fusion.spot, bf16[1024,128]{1,0:T(8,128)(2,1)S(1)} %turn.1.refs_0_, ...), custom_call_target="tpu_custom_call" | custom-call | flops 2147483648 | bytes 8388608 | tf_op jit(solution)/shard_map/gradient_tiles/pallas_call | solution.py:140
  63.1 0.1 collective-permute-start.19
  63.2 1.5 add_cores.2
  64.7 2.9 %collective-permute-start.15 = (bf16[64,16,128]{2,1,0:T(8,128)(2,1)S(1)}, bf16[64,16,128]{2,1,0:T(8,128)(2,1)S(1)}, u32[]{:S(2)}, u32[]{:S(2)}) collective-permute-start(bf16[64,16,128]{2,1,0:T(8,128)(2,1)S(1)} %get-tuple-element.58), channel_id=1, source_target_pairs={{0,128},{64,192},{128,0},{192,64},{1,129},{65,193},{129,1},{193,65... | collective-permute-start | bytes 786440 | tf_op jit(solution)/shard_map/ppermute | solution.py:369
  67.6 0.4 collective-permute-start.16
  68.0 2.3 %collective-permute-start.17 = (bf16[64,16,128]{2,1,0:T(8,128)(2,1)}, bf16[64,16,128]{2,1,0:T(8,128)(2,1)S(1)}, u32[]{:S(2)}, u32[]{:S(2)}) collective-permute-start(bf16[64,16,128]{2,1,0:T(8,128)(2,1)} %get-tuple-element.60), channel_id=1, source_target_pairs={{0,192},{64,0},{128,64},{192,128},{1,193},{65,1},{129,65},{193,129... | collective-permute-start | bytes 786440 | tf_op jit(solution)/shard_map/ppermute | solution.py:369
  70.3 1.5 add_cores.3
  71.8 0.6 collective-permute-start.21
  72.4 1.2 collective-permute-done.15.refs_2_
  73.6 2.8 %collective-permute-start.22 = (bf16[64,16,128]{2,1,0:T(8,128)(2,1)}, bf16[64,16,128]{2,1,0:T(8,128)(2,1)}, u32[]{:S(2)}, u32[]{:S(2)}) collective-permute-start(bf16[64,16,128]{2,1,0:T(8,128)(2,1)} %get-tuple-element.68), channel_id=1, source_target_pairs={{0,192},{64,0},{128,64},{192,128},{1,193},{65,1},{129,65},{193,129... | collective-permute-start | bytes 786440 | tf_op jit(solution)/shard_map/ppermute | solution.py:369
  76.4 0.2 convert_reduce_fusion
  76.6 0.6 fusion.1
  77.2 3.6 %collective-permute-done.16.refs_3_ = bf16[64,16,128]{2,1,0:T(8,128)(2,1)S(1)} collective-permute-done((bf16[64,16,128]{2,1,0:T(8,128)(2,1)}, bf16[64,16,128]{2,1,0:T(8,128)(2,1)S(1)}, u32[]{:S(2)}, u32[]{:S(2)}) %collective-permute-start.16) | collective-permute-done | bytes 262176 | tf_op jit(solution)/shard_map/ppermute | solution.py:369
  80.8 4.2 %collective-permute-done.20.refs_7_ = bf16[64,16,128]{2,1,0:T(8,128)(2,1)} collective-permute-done((bf16[64,16,128]{2,1,0:T(8,128)(2,1)}, bf16[64,16,128]{2,1,0:T(8,128)(2,1)}, u32[]{:S(2)}, u32[]{:S(2)}) %collective-permute-start.20) | collective-permute-done | bytes 262176 | tf_op jit(solution)/shard_map/ppermute | solution.py:369
  85.0 6.4 %collective-permute-done.21.refs_8_ = bf16[64,16,128]{2,1,0:T(8,128)(2,1)} collective-permute-done((bf16[64,16,128]{2,1,0:T(8,128)(2,1)}, bf16[64,16,128]{2,1,0:T(8,128)(2,1)}, u32[]{:S(2)}, u32[]{:S(2)}) %collective-permute-start.21) | collective-permute-done | bytes 262176 | tf_op jit(solution)/shard_map/ppermute | solution.py:369
  91.4 2.5 %to_slots.1 = bf16[160,16,128]{2,1,0:T(8,128)(2,1)} custom-call(s32[128]{0:T(128)S(1)} %get-tuple-element.76.slot, bf16[64,16,128]{2,1,0:T(8,128)(2,1)S(1)} %get-tuple-element.53.refs_0_, bf16[4,64,16,128]{3,2,1,0:T(8,128)(2,1)S(1)} %collective-permute-done.14.other.refs_1_, bf16[64,16,128]{2,1,0:T(8,128)(2,1)S(1)} %collective-permute-done.15.refs_2_, ...), custom_call_target="tpu_custom_call" | custom-call | tf_op jit(solution)/shard_map/to_slots/pallas_call | solution.py:205
  93.8 8.9 %all-to-all-start = ((bf16[32,5,16,128]{3,2,1,0:T(8,128)(2,1)}), bf16[32,5,16,128]{3,2,1,0:T(8,128)(2,1)S(1)}, u32[]{:S(2)}, u32[]{:S(2)}) async-start(bf16[32,5,16,128]{3,2,1,0:T(8,128)(2,1)} %bitcast.6), calls=%async_computation | async-start | bytes 1310720 | tf_op jit(solution)/shard_map/all_to_all | solution.py:330
  102.7 1.1 compare_convert_fusion.live
  103.8 11.9 %all-to-all-done.tiles = bf16[32,5,16,128]{3,2,1,0:T(8,128)(2,1)S(1)} async-done(((bf16[32,5,16,128]{3,2,1,0:T(8,128)(2,1)}), bf16[32,5,16,128]{3,2,1,0:T(8,128)(2,1)S(1)}, u32[]{:S(2)}, u32[]{:S(2)}) %all-to-all-start) | async-done | bytes 655392 | tf_op jit(solution)/shard_map/all_to_all | solution.py:330
  115.6 0.8 copy-done.6
  116.5 5.6 %update.1 = (bf16[32,5,16,128]{3,2,1,0:T(8,128)(2,1)}, bf16[5,256,256]{2,1,0:T(8,128)(2,1)}, bf16[1,5,256,256]{3,2,1,0:T(8,128)(2,1)}, bf16[1,5,256,256]{3,2,1,0:T(8,128)(2,1)}) custom-call(s32[5]{0:T(128)} %compare_convert_fusion.live, bf16[32,5,16,128]{3,2,1,0:T(8,128)(2,1)} %copy-done.6, bf16[1,5,256,256]{3,2,1,0:T(8,128)(2,1)} %basis_left.1, ...), custom_call_target="tpu_custom_call" | custom-call | tf_op jit(solution)/shard_map/update/pallas_call | solution.py:283
  122.0 17.2 %all_to_all.15 = bf16[32,5,16,128]{3,2,1,0:T(8,128)(2,1)S(1)} all-to-all(bf16[32,5,16,128]{3,2,1,0:T(8,128)(2,1)} %get-tuple-element.69), channel_id=1, replica_groups=mesh['y'=4,'x'=4,'core'=2,'z'=8] {'y','x','core'}, dimensions={0} | all-to-all | bytes 1310720 | tf_op jit(solution)/shard_map/all_to_all | solution.py:330
  139.3 1.6 from_slots.1
  140.8 4.1 %all-to-all-start.2 = ((bf16[32,4,16,128]{3,2,1,0:T(8,128)(2,1)}), bf16[32,4,16,128]{3,2,1,0:T(8,128)(2,1)S(1)}, u32[]{:S(2)}, u32[]{:S(2)}) async-start(bf16[32,4,16,128]{3,2,1,0:T(8,128)(2,1)} %bitcast.8), calls=%async_computation.2 | async-start | bytes 1048576 | tf_op jit(solution)/shard_map/all_to_all | solution.py:330
  145.0 1.1 copy-done.2
  146.0 3.7 %factors.1 = (f32[1,5,256,256]{3,2,1,0:T(8,128)}, f32[1,5,256,256]{3,2,1,0:T(8,128)}) custom-call(s32[5]{0:T(128)S(1)} %copy-done.4, bf16[5,256,256]{2,1,0:T(8,128)(2,1)S(1)} %copy-done.2, f32[1,5,256,256]{3,2,1,0:T(8,128)S(1)} %copy-done, f32[1,5,256,256]{3,2,1,0:T(8,128)S(1)} %copy-done.1), custom_call_target="tpu_custom_call" | custom-call | flops 335544320 | bytes 6291456 | tf_op jit(solution)/shard_map/factors/pallas_call | solution.py:312
  149.7 6.8 %all-to-all-done.2.tiles = bf16[32,4,16,128]{3,2,1,0:T(8,128)(2,1)S(1)} async-done(((bf16[32,4,16,128]{3,2,1,0:T(8,128)(2,1)}), bf16[32,4,16,128]{3,2,1,0:T(8,128)(2,1)S(1)}, u32[]{:S(2)}, u32[]{:S(2)}) %all-to-all-start.2) | async-done | bytes 524320 | tf_op jit(solution)/shard_map/all_to_all | solution.py:330
  156.6 0.9 assemble.1
  (22 shorter events, 0.1 us)
Async XLA Ops:
  0.7 1.0 copy-start.3
  2.5 4.4 %collective-permute-start = (bf16[32,1024]{1,0:T(8,128)(2,1)S(1)}, bf16[32,1024]{1,0:T(8,128)(2,1)S(1)}, u32[]{:S(2)}, u32[]{:S(2)}) collective-permute-start(bf16[32,1024]{1,0:T(8,128)(2,1)S(1)} %get-tuple-element.41), channel_id=1, source_target_pairs={{0,16},{16,32},{32,48},{48,0},{1,17},{17,33},{33,49},{49,1},{2,18}... | collective-permute-start | bytes 196616 | tf_op jit(solution)/shard_map/ppermute | solution.py:342
  3.8 3.1 %collective-permute-start.1 = (bf16[32,1024]{1,0:T(8,128)(2,1)S(1)}, bf16[32,1024]{1,0:T(8,128)(2,1)S(1)}, u32[]{:S(2)}, u32[]{:S(2)}) collective-permute-start(bf16[32,1024]{1,0:T(8,128)(2,1)S(1)} %get-tuple-element.42), channel_id=1, source_target_pairs={{0,48},{16,0},{32,16},{48,32},{1,49},{17,1},{33,17},{49,33},{2,50}... | collective-permute-start | bytes 196616 | tf_op jit(solution)/shard_map/ppermute | solution.py:342
  5.3 4.6 %collective-permute-start.2 = (bf16[32,1024]{1,0:T(8,128)(2,1)S(1)}, bf16[32,1024]{1,0:T(8,128)(2,1)S(1)}, u32[]{:S(2)}, u32[]{:S(2)}) collective-permute-start(bf16[32,1024]{1,0:T(8,128)(2,1)S(1)} %get-tuple-element.43), channel_id=1, source_target_pairs={{0,32},{16,48},{32,0},{48,16},{1,33},{17,49},{33,1},{49,17},{2,34}... | collective-permute-start | bytes 196616 | tf_op jit(solution)/shard_map/ppermute | solution.py:342
  9.9 23.7 %collective-permute-start.7 = (bf16[8,32,2048]{2,1,0:T(8,128)(2,1)}, bf16[8,32,2048]{2,1,0:T(8,128)(2,1)S(1)}, u32[]{:S(2)}, u32[]{:S(2)}) collective-permute-start(bf16[8,32,2048]{2,1,0:T(8,128)(2,1)} %bitcast.12), channel_id=1, source_target_pairs={{0,16},{16,32},{32,48},{48,0},{1,17},{17,33},{33,49},{49,1},{2,18}... | collective-permute-start | bytes 3145736 | tf_op jit(solution)/shard_map/ppermute | solution.py:344
  10.3 23.3 %collective-permute-start.8 = (bf16[8,32,2048]{2,1,0:T(8,128)(2,1)}, bf16[8,32,2048]{2,1,0:T(8,128)(2,1)S(1)}, u32[]{:S(2)}, u32[]{:S(2)}) collective-permute-start(bf16[8,32,2048]{2,1,0:T(8,128)(2,1)} %bitcast.13), channel_id=1, source_target_pairs={{0,48},{16,0},{32,16},{48,32},{1,49},{17,1},{33,17},{49,33},{2,50}... | collective-permute-start | bytes 3145736 | tf_op jit(solution)/shard_map/ppermute | solution.py:344
  12.7 36.2 %copy-start.5 = (bf16[256,2048]{1,0:T(8,128)(2,1)S(1)}, bf16[256,2048]{1,0:T(8,128)(2,1)}, u32[]{:S(2)}) copy-start(bf16[256,2048]{1,0:T(8,128)(2,1)} %param.10) | copy-start | bytes 3145732
  12.7 6.2 %collective-permute-start.3 = (bf16[1024,128]{1,0:T(8,128)(2,1)S(1)}, bf16[1024,128]{1,0:T(8,128)(2,1)S(1)}, u32[]{:S(2)}, u32[]{:S(2)}) collective-permute-start(bf16[1024,128]{1,0:T(8,128)(2,1)S(1)} %turn.1.refs_0_), channel_id=1, source_target_pairs={{0,1},{1,2},{2,3},{3,4},{4,5},{5,6},{6,7},{7,0},{8,9},{9,10},{10,1... | collective-permute-start | bytes 786440 | tf_op jit(solution)/shard_map/ppermute | solution.py:346
  15.7 6.7 %collective-permute-start.4 = (bf16[1024,128]{1,0:T(8,128)(2,1)S(1)}, bf16[1024,128]{1,0:T(8,128)(2,1)S(1)}, u32[]{:S(2)}, u32[]{:S(2)}) collective-permute-start(bf16[1024,128]{1,0:T(8,128)(2,1)S(1)} %turn.1.refs_0_), channel_id=1, source_target_pairs={{0,7},{1,0},{2,1},{3,2},{4,3},{5,4},{6,5},{7,6},{8,15},{9,8},{10,9... | collective-permute-start | bytes 786440 | tf_op jit(solution)/shard_map/ppermute | solution.py:346
  19.0 6.7 %collective-permute-start.5 = (bf16[1024,128]{1,0:T(8,128)(2,1)S(1)}, bf16[1024,128]{1,0:T(8,128)(2,1)S(1)}, u32[]{:S(2)}, u32[]{:S(2)}) collective-permute-start(bf16[1024,128]{1,0:T(8,128)(2,1)S(1)} %collective-permute-done.3.refs_1_), channel_id=1, source_target_pairs={{0,1},{1,2},{2,3},{3,4},{4,5},{5,6},{6,7},{7,0},{8,9},{9,10},{10,1... | collective-permute-start | bytes 786440 | tf_op jit(solution)/shard_map/ppermute | solution.py:348
  22.4 6.7 %collective-permute-start.6 = (bf16[1024,128]{1,0:T(8,128)(2,1)S(1)}, bf16[1024,128]{1,0:T(8,128)(2,1)S(1)}, u32[]{:S(2)}, u32[]{:S(2)}) collective-permute-start(bf16[1024,128]{1,0:T(8,128)(2,1)S(1)} %collective-permute-done.4.refs_2_), channel_id=1, source_target_pairs={{0,7},{1,0},{2,1},{3,2},{4,3},{5,4},{6,5},{7,6},{8,15},{9,8},{10,9... | collective-permute-start | bytes 786440 | tf_op jit(solution)/shard_map/ppermute | solution.py:348
  33.7 15.2 %collective-permute-start.13 = (bf16[8,32,1024]{2,1,0:T(8,128)(2,1)S(1)}, bf16[8,32,1024]{2,1,0:T(8,128)(2,1)S(1)}, u32[]{:S(2)}, u32[]{:S(2)}) collective-permute-start(bf16[8,32,1024]{2,1,0:T(8,128)(2,1)S(1)} %slice.14), channel_id=1, source_target_pairs={{0,16},{16,32},{32,48},{48,0},{1,17},{17,33},{33,49},{49,1},{2,18}... | collective-permute-start | bytes 1572872 | tf_op jit(solution)/shard_map/ppermute | solution.py:353
  33.7 6.2 %collective-permute-start.9 = (bf16[1024,128]{1,0:T(8,128)(2,1)S(1)}, bf16[1024,128]{1,0:T(8,128)(2,1)S(1)}, u32[]{:S(2)}, u32[]{:S(2)}) collective-permute-start(bf16[1024,128]{1,0:T(8,128)(2,1)S(1)} %collective-permute-done.5.refs_3_), channel_id=1, source_target_pairs={{0,1},{1,2},{2,3},{3,4},{4,5},{5,6},{6,7},{7,0},{8,9},{9,10},{10,1... | collective-permute-start | bytes 786440 | tf_op jit(solution)/shard_map/ppermute | solution.py:356
  36.7 6.7 %collective-permute-start.10 = (bf16[1024,128]{1,0:T(8,128)(2,1)S(1)}, bf16[1024,128]{1,0:T(8,128)(2,1)S(1)}, u32[]{:S(2)}, u32[]{:S(2)}) collective-permute-start(bf16[1024,128]{1,0:T(8,128)(2,1)S(1)} %collective-permute-done.6.refs_4_), channel_id=1, source_target_pairs={{0,7},{1,0},{2,1},{3,2},{4,3},{5,4},{6,5},{7,6},{8,15},{9,8},{10,9... | collective-permute-start | bytes 786440 | tf_op jit(solution)/shard_map/ppermute | solution.py:356
  36.7 22.2 %collective-permute-start.18 = (bf16[8,32,1024]{2,1,0:T(8,128)(2,1)S(1)}, bf16[8,32,1024]{2,1,0:T(8,128)(2,1)S(1)}, u32[]{:S(2)}, u32[]{:S(2)}) collective-permute-start(bf16[8,32,1024]{2,1,0:T(8,128)(2,1)S(1)} %slice.15), channel_id=1, source_target_pairs={{0,48},{16,0},{32,16},{48,32},{1,49},{17,1},{33,17},{49,33},{2,50}... | collective-permute-start | bytes 1572872 | tf_op jit(solution)/shard_map/ppermute | solution.py:354
  40.0 5.3 %collective-permute-start.11 = (bf16[512,128]{1,0:T(8,128)(2,1)S(1)}, bf16[512,128]{1,0:T(8,128)(2,1)S(1)}, u32[]{:S(2)}, u32[]{:S(2)}) collective-permute-start(bf16[512,128]{1,0:T(8,128)(2,1)S(1)} %slice.16), channel_id=1, source_target_pairs={{0,1},{1,2},{2,3},{3,4},{4,5},{5,6},{6,7},{7,0},{8,9},{9,10},{10,1... | collective-permute-start | bytes 393224 | tf_op jit(solution)/shard_map/ppermute | solution.py:359
  43.4 5.5 %collective-permute-start.12 = (bf16[512,128]{1,0:T(8,128)(2,1)S(1)}, bf16[512,128]{1,0:T(8,128)(2,1)S(1)}, u32[]{:S(2)}, u32[]{:S(2)}) collective-permute-start(bf16[512,128]{1,0:T(8,128)(2,1)S(1)} %slice.17), channel_id=1, source_target_pairs={{0,7},{1,0},{2,1},{3,2},{4,3},{5,4},{6,5},{7,6},{8,15},{9,8},{10,9... | collective-permute-start | bytes 393224 | tf_op jit(solution)/shard_map/ppermute | solution.py:360
  53.0 10.2 %collective-permute-start.14 = (bf16[4,64,16,128]{3,2,1,0:T(8,128)(2,1)S(1)}, bf16[4,64,16,128]{3,2,1,0:T(8,128)(2,1)S(1)}, u32[]{:S(2)}, u32[]{:S(2)}) collective-permute-start(bf16[4,64,16,128]{3,2,1,0:T(8,128)(2,1)S(1)} %get-tuple-element.54), channel_id=1, source_target_pairs={{0,8},{8,0},{1,9},{9,1},{2,10},{10,2},{3,11},{11,3},{4,12},{12,4},... | collective-permute-start | bytes 3145736 | tf_op jit(solution)/shard_map/ppermute | solution.py:366
  63.1 7.2 %collective-permute-start.19 = (bf16[4,64,16,128]{3,2,1,0:T(8,128)(2,1)S(1)}, bf16[4,64,16,128]{3,2,1,0:T(8,128)(2,1)S(1)}, u32[]{:S(2)}, u32[]{:S(2)}) collective-permute-start(bf16[4,64,16,128]{3,2,1,0:T(8,128)(2,1)S(1)} %get-tuple-element.62), channel_id=1, source_target_pairs={{0,8},{8,0},{1,9},{9,1},{2,10},{10,2},{3,11},{11,3},{4,12},{12,4},... | collective-permute-start | bytes 3145736 | tf_op jit(solution)/shard_map/ppermute | solution.py:366
  64.7 11.7 %copy-start.7 = (s32[1,128]{1,0:T(1,128)S(1)}, s32[1,128]{1,0:T(1,128)}, u32[]{:S(2)}) copy-start(s32[1,128]{1,0:T(1,128)} %param.11) | copy-start | bytes 1540
  64.7 8.9 %collective-permute-start.15 = (bf16[64,16,128]{2,1,0:T(8,128)(2,1)S(1)}, bf16[64,16,128]{2,1,0:T(8,128)(2,1)S(1)}, u32[]{:S(2)}, u32[]{:S(2)}) collective-permute-start(bf16[64,16,128]{2,1,0:T(8,128)(2,1)S(1)} %get-tuple-element.58), channel_id=1, source_target_pairs={{0,128},{64,192},{128,0},{192,64},{1,129},{65,193},{129,1},{193,65... | collective-permute-start | bytes 786440 | tf_op jit(solution)/shard_map/ppermute | solution.py:369
  67.6 13.2 %collective-permute-start.16 = (bf16[64,16,128]{2,1,0:T(8,128)(2,1)}, bf16[64,16,128]{2,1,0:T(8,128)(2,1)S(1)}, u32[]{:S(2)}, u32[]{:S(2)}) collective-permute-start(bf16[64,16,128]{2,1,0:T(8,128)(2,1)} %get-tuple-element.59), channel_id=1, source_target_pairs={{0,64},{64,128},{128,192},{192,0},{1,65},{65,129},{129,193},{193,1... | collective-permute-start | bytes 786440 | tf_op jit(solution)/shard_map/ppermute | solution.py:369
  68.0 12.8 %collective-permute-start.17 = (bf16[64,16,128]{2,1,0:T(8,128)(2,1)}, bf16[64,16,128]{2,1,0:T(8,128)(2,1)S(1)}, u32[]{:S(2)}, u32[]{:S(2)}) collective-permute-start(bf16[64,16,128]{2,1,0:T(8,128)(2,1)} %get-tuple-element.60), channel_id=1, source_target_pairs={{0,192},{64,0},{128,64},{192,128},{1,193},{65,1},{129,65},{193,129... | collective-permute-start | bytes 786440 | tf_op jit(solution)/shard_map/ppermute | solution.py:369
  71.8 13.2 %collective-permute-start.20 = (bf16[64,16,128]{2,1,0:T(8,128)(2,1)}, bf16[64,16,128]{2,1,0:T(8,128)(2,1)}, u32[]{:S(2)}, u32[]{:S(2)}) collective-permute-start(bf16[64,16,128]{2,1,0:T(8,128)(2,1)} %get-tuple-element.66), channel_id=1, source_target_pairs={{0,128},{64,192},{128,0},{192,64},{1,129},{65,193},{129,1},{193,65... | collective-permute-start | bytes 786440 | tf_op jit(solution)/shard_map/ppermute | solution.py:369
  71.8 19.5 %collective-permute-start.21 = (bf16[64,16,128]{2,1,0:T(8,128)(2,1)}, bf16[64,16,128]{2,1,0:T(8,128)(2,1)}, u32[]{:S(2)}, u32[]{:S(2)}) collective-permute-start(bf16[64,16,128]{2,1,0:T(8,128)(2,1)} %get-tuple-element.67), channel_id=1, source_target_pairs={{0,64},{64,128},{128,192},{192,0},{1,65},{65,129},{129,193},{193,1... | collective-permute-start | bytes 786440 | tf_op jit(solution)/shard_map/ppermute | solution.py:369
  73.6 17.8 %collective-permute-start.22 = (bf16[64,16,128]{2,1,0:T(8,128)(2,1)}, bf16[64,16,128]{2,1,0:T(8,128)(2,1)}, u32[]{:S(2)}, u32[]{:S(2)}) collective-permute-start(bf16[64,16,128]{2,1,0:T(8,128)(2,1)} %get-tuple-element.68), channel_id=1, source_target_pairs={{0,192},{64,0},{128,64},{192,128},{1,193},{65,1},{129,65},{193,129... | collective-permute-start | bytes 786440 | tf_op jit(solution)/shard_map/ppermute | solution.py:369
  93.8 21.8 %all-to-all-start = ((bf16[32,5,16,128]{3,2,1,0:T(8,128)(2,1)}), bf16[32,5,16,128]{3,2,1,0:T(8,128)(2,1)S(1)}, u32[]{:S(2)}, u32[]{:S(2)}) async-start(bf16[32,5,16,128]{3,2,1,0:T(8,128)(2,1)} %bitcast.6), calls=%async_computation | async-start | bytes 1310720 | tf_op jit(solution)/shard_map/all_to_all | solution.py:330
  115.6 0.8 copy-start.6
  122.0 22.9 %copy-start.1 = (f32[1,5,256,256]{3,2,1,0:T(8,128)S(1)}, f32[1,5,256,256]{3,2,1,0:T(8,128)}, u32[]{:S(2)}) copy-start(f32[1,5,256,256]{3,2,1,0:T(8,128)} %right.1) | copy-start | bytes 3932164
  139.3 5.7 %copy-start = (f32[1,5,256,256]{3,2,1,0:T(8,128)S(1)}, f32[1,5,256,256]{3,2,1,0:T(8,128)}, u32[]{:S(2)}) copy-start(f32[1,5,256,256]{3,2,1,0:T(8,128)} %left.1) | copy-start | bytes 3932164
  139.3 5.7 %copy-start.4 = (s32[5]{0:T(128)S(1)}, s32[5]{0:T(128)}, u32[]{:S(2)}) copy-start(s32[5]{0:T(128)} %compare_convert_fusion.live) | copy-start | bytes 64
  140.8 15.8 %all-to-all-start.2 = ((bf16[32,4,16,128]{3,2,1,0:T(8,128)(2,1)}), bf16[32,4,16,128]{3,2,1,0:T(8,128)(2,1)S(1)}, u32[]{:S(2)}, u32[]{:S(2)}) async-start(bf16[32,4,16,128]{3,2,1,0:T(8,128)(2,1)} %bitcast.8), calls=%async_computation.2 | async-start | bytes 1048576 | tf_op jit(solution)/shard_map/all_to_all | solution.py:330
  145.0 1.1 copy-start.2

commit v6 on v5

--- a/solution.py
+++ b/solution.py
@@ -184,31 +184,55 @@
     )(*parts[1:], other)
 
 
-def to_slots_kernel(slot, *refs):
-    out = refs[-1]
+def sum_kernel(mine, other, one, two, three, out):
+    total = mine[...].astype(jnp.float32) + other[0].astype(jnp.float32)
+    for part in (one, two, three):
+        total = total + part[...].astype(jnp.float32)
+    out[...] = total.astype(jnp.bfloat16)
+
+
+def sum_chunk(parts):
+    blocks = CHUNK_K // 4
+    part = pl.BlockSpec((blocks, TILE_ROWS, TILE_COLS), lambda c: (c, 0, 0))
+    first = pl.BlockSpec((1, blocks, TILE_ROWS, TILE_COLS), lambda c: (0, c, 0, 0))
+    return pl.pallas_call(
+        sum_kernel,
+        grid=(4,),
+        in_specs=[part, first, part, part, part],
+        out_specs=part,
+        out_shape=jax.ShapeDtypeStruct((CHUNK_K, TILE_ROWS, TILE_COLS), jnp.bfloat16),
+        compiler_params=params(16),
+        cost_estimate=pl.CostEstimate(flops=MIB, bytes_accessed=2 * MIB, transcendentals=0),
+        name="sum_chunk",
+    )(*parts)
+
+
+def to_slots_kernel(slot, summed, mine, other, one, two, three, out):
     out[...] = jnp.zeros_like(out)
-    for chunk in range(2):
-        mine, other, *rest = refs[5 * chunk : 5 * chunk + 5]
-
-        def body(k, carry):
-            total = mine[k].astype(jnp.float32) + other[0, k].astype(jnp.float32)
-            for part in rest:
-                total = total + part[k].astype(jnp.float32)
-            out[slot[chunk * CHUNK_K + k]] = total.astype(jnp.bfloat16)
-            return carry
-
-        lax.fori_loop(0, CHUNK_K, body, 0, unroll=8)
+
+    def early(k, carry):
+        out[slot[k]] = summed[k]
+        return carry
+
+    def late(k, carry):
+        total = mine[k].astype(jnp.float32) + other[0, k].astype(jnp.float32)
+        for part in (one, two, three):
+            total = total + part[k].astype(jnp.float32)
+        out[slot[CHUNK_K + k]] = total.astype(jnp.bfloat16)
+        return carry
+
+    lax.fori_loop(0, CHUNK_K, early, 0, unroll=8)
+    lax.fori_loop(0, CHUNK_K, late, 0, unroll=8)
 
 
 def to_slots(slot, chunks):
-    flat = [a for chunk in chunks for a in chunk]
     return pl.pallas_call(
         to_slots_kernel,
-        in_specs=[SMEM] + [VMEM] * len(flat),
+        in_specs=[SMEM] + [VMEM] * 6,
         out_shape=jax.ShapeDtypeStruct((N_DP * SLOTS, TILE_ROWS, TILE_COLS), jnp.bfloat16),
         compiler_params=params(16),
         name="to_slots",
-    )(slot, *flat)
+    )(slot, sum_chunk(chunks[0]), *chunks[1])
 
 
 def from_slots_kernel(slot, tiles, out):
@@ -289,7 +313,7 @@
             like(first),
             like(second),
         ],
-        compiler_params=params(63),
+        compiler_params=params(52),
         name="update",
     )(live, tiles, basis_left, basis_right, first, second)
 
@@ -347,14 +371,14 @@
     whole = [mine, below, above]
     below, above = lax.ppermute(below, "z", up), lax.ppermute(above, "z", down)
     whole += [below, above]
+    below, above = lax.ppermute(below, "z", up), lax.ppermute(above, "z", down)
+    whole += [below, above]
     behind, before, below, above = lax.optimization_barrier((behind, before, below, above))
     half = grads.shape[-1] // 2
     far = [
         lax.ppermute(behind[..., :half], "x", ahead),
         lax.ppermute(before[..., half:], "x", back),
     ]
-    below, above = lax.ppermute(below, "z", up), lax.ppermute(above, "z", down)
-    whole += [below, above]
     halves = [
         lax.ppermute(below[:LOCAL_ROWS], "z", up),
         lax.ppermute(above[LOCAL_ROWS:], "z", down),
@@ -366,7 +390,7 @@
     mine, other = parts[:Y], lax.ppermute(parts[Y], "core", ring(CORE, 1))
     one, two, three = add_cores(mine, other)
     moved = [
-        lax.ppermute(a, "y", ring(Y, step)) for a, step in ((two, 2), (one, 1), (three, 3))
+        lax.ppermute(a, "y", ring(Y, step)) for a, step in ((one, 1), (two, 2), (three, 3))
     ]
     return [mine[0], other] + moved
 

time: 158 us -> 151 us (0.956)
  starting transfers between devices: 50.4 us -> 45.6 us
  waiting for transfers between devices: 57.7 us -> 55.8 us
    ppermute x1, waiting for transfers between devices: 4.49 us -> 0.01 us  [gather_row(): lax.ppermute(grads, 'x', ahead)]
    all_to_all x2, starting transfers between devices: 13 us -> 9.62 us  [spread(): return lax.all_to_all(array, axes, split_axis=0, concat_axis=0, tiled=True)]
    ppermute x1, starting transfers between devices: 3.19 us -> 0.08 us  [gather_row(): lax.ppermute(below[:LOCAL_ROWS], 'z', up)]
    ppermute x2, waiting for transfers between devices: 3.92 us -> 6.96 us  [gather_row(): lax.ppermute(below, 'z', up)]
    ppermute x1, waiting for transfers between devices: 3.54 us -> 1.5 us  [gather_row(): lax.ppermute(above[LOCAL_ROWS:], 'z', down)]
    pallas_call x1 -> x2, Pallas kernels: 2.45 us -> 4.14 us  [the longest x1 2.28 us: to_slots(): pl.pallas_call(to_slots_kernel, in_specs=[SMEM] + [VMEM] * 6, out_shape=j...]
  transfers between devices with their start and end apart: 25 -> 25, of which waited for: 16 -> 15; matrix products, arithmetic and copies ran while one was open for 1% -> 1% of each run, Pallas kernels for 10% -> 11%
where the time goes in v6:
time: 151 us; the launch traced here: 150 us
  waiting for transfers between devices  55.8 us (37%)
  starting transfers between devices  45.6 us (30%)
  Pallas kernels  27.7 us (18%)
  blocking collectives  16.6 us (11%)
  local copies, waits for them, and re-layouts  2.15 us (1%)
  other arithmetic  1.58 us (1%)
    all_to_all x2, waiting for transfers between devices, spread(): return lax.all_to_all(array, axes, split_axis=0, concat_axis=0, tiled=True)  19.1 us
    all_to_all x1, blocking collectives, spread(): return lax.all_to_all(array, axes, split_axis=0, concat_axis=0, tiled=True)  16.6 us
    ppermute x6, waiting for transfers between devices, sum_parts(): lax.ppermute(a, 'y', ring(Y, step))  15 us
    all_to_all x2, starting transfers between devices, spread(): return lax.all_to_all(array, axes, split_axis=0, concat_axis=0, tiled=True)  9.62 us
    pallas_call x2, Pallas kernels, gradient_tiles(): pl.pallas_call(gradient_kernel, grid_spec=pltpu.PrefetchScalarGridSpec(nu...  8.24 us
    ppermute x6, starting transfers between devices, sum_parts(): lax.ppermute(a, 'y', ring(Y, step))  7.57 us
    ppermute x2, starting transfers between devices, sum_parts(): mine, other = (parts[:Y], lax.ppermute(parts[Y], 'core', ring(CORE, 1)))  7.08 us
    ppermute x2, waiting for transfers between devices, gather_row(): lax.ppermute(below, 'z', up)  6.96 us
  transfers between devices with their start and end apart: 25, of which 15 were waited for; matrix products, arithmetic and copies ran while one was open for 1% of the time, Pallas kernels for 11%

profile of v6, /device:TPU:97, one launch (start us, length us, event | category | flops | bytes accessed | tf_op | source)
XLA Modules:
  0.0 150.2 jit_solution(5100502545345616842)
XLA Ops:
  0.6 0.1 pad_add_fusion.spot
  0.7 0.9 copy-done.4
  1.7 0.9 cut_tokens.1
  2.5 1.3 collective-permute-start
  3.8 1.5 collective-permute-start.1
  5.3 1.5 %collective-permute-start.2 = (bf16[32,1024]{1,0:T(8,128)(2,1)S(1)}, bf16[32,1024]{1,0:T(8,128)(2,1)S(1)}, u32[]{:S(2)}, u32[]{:S(2)}) collective-permute-start(bf16[32,1024]{1,0:T(8,128)(2,1)S(1)} %get-tuple-element.43), channel_id=1, source_target_pairs={{0,32},{16,48},{32,0},{48,16},{1,33},{17,49},{33,1},{49,17},{2,34}... | collective-permute-start | bytes 196616 | tf_op jit(solution)/shard_map/ppermute | solution.py:366
  6.8 0.1 collective-permute-done.refs_1_
  6.9 0.0 collective-permute-done.1.refs_2_
  6.9 3.0 %collective-permute-done.2.refs_3_ = bf16[32,1024]{1,0:T(8,128)(2,1)S(1)} collective-permute-done((bf16[32,1024]{1,0:T(8,128)(2,1)S(1)}, bf16[32,1024]{1,0:T(8,128)(2,1)S(1)}, u32[]{:S(2)}, u32[]{:S(2)}) %collective-permute-start.2) | collective-permute-done | bytes 65568 | tf_op jit(solution)/shard_map/ppermute | solution.py:366
  9.9 0.4 collective-permute-start.9
  10.3 2.3 %collective-permute-start.10 = (bf16[8,32,2048]{2,1,0:T(8,128)(2,1)}, bf16[8,32,2048]{2,1,0:T(8,128)(2,1)S(1)}, u32[]{:S(2)}, u32[]{:S(2)}) collective-permute-start(bf16[8,32,2048]{2,1,0:T(8,128)(2,1)} %bitcast.13), channel_id=1, source_target_pairs={{0,48},{16,0},{32,16},{48,32},{1,49},{17,1},{33,17},{49,33},{2,50}... | collective-permute-start | bytes 3145736 | tf_op jit(solution)/shard_map/ppermute | solution.py:368
  12.6 0.1 turn.1.refs_0_
  12.7 0.0 copy-start.5
  12.7 2.9 %collective-permute-start.3 = (bf16[1024,128]{1,0:T(8,128)(2,1)S(1)}, bf16[1024,128]{1,0:T(8,128)(2,1)S(1)}, u32[]{:S(2)}, u32[]{:S(2)}) collective-permute-start(bf16[1024,128]{1,0:T(8,128)(2,1)S(1)} %turn.1.refs_0_), channel_id=1, source_target_pairs={{0,1},{1,2},{2,3},{3,4},{4,5},{5,6},{6,7},{7,0},{8,9},{9,10},{10,1... | collective-permute-start | bytes 786440 | tf_op jit(solution)/shard_map/ppermute | solution.py:370
  15.7 0.0 collective-permute-start.4
  15.7 3.3 %collective-permute-done.3.refs_1_ = bf16[1024,128]{1,0:T(8,128)(2,1)S(1)} collective-permute-done((bf16[1024,128]{1,0:T(8,128)(2,1)S(1)}, bf16[1024,128]{1,0:T(8,128)(2,1)S(1)}, u32[]{:S(2)}, u32[]{:S(2)}) %collective-permute-start.3) | collective-permute-done | bytes 262176 | tf_op jit(solution)/shard_map/ppermute | solution.py:370
  19.0 3.4 %collective-permute-start.5 = (bf16[1024,128]{1,0:T(8,128)(2,1)S(1)}, bf16[1024,128]{1,0:T(8,128)(2,1)S(1)}, u32[]{:S(2)}, u32[]{:S(2)}) collective-permute-start(bf16[1024,128]{1,0:T(8,128)(2,1)S(1)} %collective-permute-done.3.refs_1_), channel_id=1, source_target_pairs={{0,1},{1,2},{2,3},{3,4},{4,5},{5,6},{6,7},{7,0},{8,9},{9,10},{10,1... | collective-permute-start | bytes 786440 | tf_op jit(solution)/shard_map/ppermute | solution.py:372
  22.4 0.0 collective-permute-done.4.refs_2_
  22.4 0.0 collective-permute-start.6
  22.4 3.3 %collective-permute-done.5.refs_3_ = bf16[1024,128]{1,0:T(8,128)(2,1)S(1)} collective-permute-done((bf16[1024,128]{1,0:T(8,128)(2,1)S(1)}, bf16[1024,128]{1,0:T(8,128)(2,1)S(1)}, u32[]{:S(2)}, u32[]{:S(2)}) %collective-permute-start.5) | collective-permute-done | bytes 262176 | tf_op jit(solution)/shard_map/ppermute | solution.py:372
  25.7 3.4 %collective-permute-start.7 = (bf16[1024,128]{1,0:T(8,128)(2,1)S(1)}, bf16[1024,128]{1,0:T(8,128)(2,1)S(1)}, u32[]{:S(2)}, u32[]{:S(2)}) collective-permute-start(bf16[1024,128]{1,0:T(8,128)(2,1)S(1)} %collective-permute-done.5.refs_3_), channel_id=1, source_target_pairs={{0,1},{1,2},{2,3},{3,4},{4,5},{5,6},{6,7},{7,0},{8,9},{9,10},{10,1... | collective-permute-start | bytes 786440 | tf_op jit(solution)/shard_map/ppermute | solution.py:374
  29.1 0.0 collective-permute-done.6.refs_4_
  29.1 3.6 %collective-permute-done.7.refs_5_ = bf16[1024,128]{1,0:T(8,128)(2,1)S(1)} collective-permute-done((bf16[1024,128]{1,0:T(8,128)(2,1)S(1)}, bf16[1024,128]{1,0:T(8,128)(2,1)S(1)}, u32[]{:S(2)}, u32[]{:S(2)}) %collective-permute-start.7) | collective-permute-done | bytes 262176 | tf_op jit(solution)/shard_map/ppermute | solution.py:374
  32.8 3.7 %collective-permute-done.8.refs_6_ = bf16[1024,128]{1,0:T(8,128)(2,1)S(1)} collective-permute-done((bf16[1024,128]{1,0:T(8,128)(2,1)S(1)}, bf16[1024,128]{1,0:T(8,128)(2,1)S(1)}, u32[]{:S(2)}, u32[]{:S(2)}) %collective-permute-start.8) | collective-permute-done | bytes 262176 | tf_op jit(solution)/shard_map/ppermute | solution.py:374
  36.5 0.0 collective-permute-done.10.refs_11_
  36.5 0.1 collective-permute-start.13
  36.7 2.7 %collective-permute-start.18 = (bf16[8,32,1024]{2,1,0:T(8,128)(2,1)S(1)}, bf16[8,32,1024]{2,1,0:T(8,128)(2,1)S(1)}, u32[]{:S(2)}, u32[]{:S(2)}) collective-permute-start(bf16[8,32,1024]{2,1,0:T(8,128)(2,1)S(1)} %slice.15), channel_id=1, source_target_pairs={{0,48},{16,0},{32,16},{48,32},{1,49},{17,1},{33,17},{49,33},{2,50}... | collective-permute-start | bytes 1572872 | tf_op jit(solution)/shard_map/ppermute | solution.py:380
  39.4 0.1 collective-permute-start.11
  39.5 1.7 %collective-permute-start.12 = (bf16[512,128]{1,0:T(8,128)(2,1)S(1)}, bf16[512,128]{1,0:T(8,128)(2,1)S(1)}, u32[]{:S(2)}, u32[]{:S(2)}) collective-permute-start(bf16[512,128]{1,0:T(8,128)(2,1)S(1)} %slice.13), channel_id=1, source_target_pairs={{0,7},{1,0},{2,1},{3,2},{4,3},{5,4},{6,5},{7,6},{8,15},{9,8},{10,9... | collective-permute-start | bytes 393224 | tf_op jit(solution)/shard_map/ppermute | solution.py:384
  41.2 2.1 %collective-permute-done.11.refs_7_ = bf16[512,128]{1,0:T(8,128)(2,1)S(1)} collective-permute-done((bf16[512,128]{1,0:T(8,128)(2,1)S(1)}, bf16[512,128]{1,0:T(8,128)(2,1)S(1)}, u32[]{:S(2)}, u32[]{:S(2)}) %collective-permute-start.11) | collective-permute-done | bytes 131104 | tf_op jit(solution)/shard_map/ppermute | solution.py:383
  43.3 1.5 collective-permute-done.12.refs_8_
  44.8 1.0 collective-permute-done.13.refs_12_
  45.8 4.1 %gradient_tiles.2 = (bf16[64,16,128]{2,1,0:T(8,128)(2,1)S(1)}, bf16[64,16,128]{2,1,0:T(8,128)(2,1)S(1)}, bf16[64,16,128]{2,1,0:T(8,128)(2,1)S(1)}, bf16[64,16,12...) custom-call(s32[4]{0:T(128)S(1)} %pad_add_fusion.spot, bf16[1024,128]{1,0:T(8,128)(2,1)S(1)} %turn.1.refs_0_, ...), custom_call_target="tpu_custom_call" | custom-call | flops 2147483648 | bytes 8388608 | tf_op jit(solution)/shard_map/gradient_tiles/pallas_call | solution.py:140
  50.0 7.0 %collective-permute-start.14 = (bf16[4,64,16,128]{3,2,1,0:T(8,128)(2,1)S(1)}, bf16[4,64,16,128]{3,2,1,0:T(8,128)(2,1)S(1)}, u32[]{:S(2)}, u32[]{:S(2)}) collective-permute-start(bf16[4,64,16,128]{3,2,1,0:T(8,128)(2,1)S(1)} %get-tuple-element.54), channel_id=1, source_target_pairs={{0,8},{8,0},{1,9},{9,1},{2,10},{10,2},{3,11},{11,3},{4,12},{12,4},... | collective-permute-start | bytes 3145736 | tf_op jit(solution)/shard_map/ppermute | solution.py:390
  56.9 4.1 %gradient_tiles.3 = (bf16[64,16,128]{2,1,0:T(8,128)(2,1)S(1)}, bf16[64,16,128]{2,1,0:T(8,128)(2,1)S(1)}, bf16[64,16,128]{2,1,0:T(8,128)(2,1)S(1)}, bf16[64,16,12...) custom-call(s32[4]{0:T(128)S(1)} %pad_add_fusion.spot, bf16[1024,128]{1,0:T(8,128)(2,1)S(1)} %turn.1.refs_0_, ...), custom_call_target="tpu_custom_call" | custom-call | flops 2147483648 | bytes 8388608 | tf_op jit(solution)/shard_map/gradient_tiles/pallas_call | solution.py:140
  61.1 0.1 collective-permute-start.19
  61.2 1.5 add_cores.2
  62.7 1.3 collective-permute-start.15
  63.9 2.6 %collective-permute-start.16 = (bf16[64,16,128]{2,1,0:T(8,128)(2,1)}, bf16[64,16,128]{2,1,0:T(8,128)(2,1)S(1)}, u32[]{:S(2)}, u32[]{:S(2)}) collective-permute-start(bf16[64,16,128]{2,1,0:T(8,128)(2,1)} %get-tuple-element.59), channel_id=1, source_target_pairs={{0,128},{64,192},{128,0},{192,64},{1,129},{65,193},{129,1},{193,65... | collective-permute-start | bytes 786440 | tf_op jit(solution)/shard_map/ppermute | solution.py:393
  66.6 1.1 collective-permute-start.17
  67.7 1.5 %add_cores.3 = (bf16[64,16,128]{2,1,0:T(8,128)(2,1)}, bf16[64,16,128]{2,1,0:T(8,128)(2,1)}, bf16[64,16,128]{2,1,0:T(8,128)(2,1)}) custom-call(bf16[64,16,128]{2,1,0:T(8,128)(2,1)S(1)} %get-tuple-element.63.one, bf16[64,16,128]{2,1,0:T(8,128)(2,1)S(1)} %get-tuple-element.64.two, bf16[64,16,128]{2,1,0:T(8,128)(2,1)S(1)} %get-tuple-element.65.three, ...), custom_call_target="tpu_custom_call" | custom-call | tf_op jit(solution)/shard_map/add_cores/pallas_call | solution.py:175
  69.2 0.4 collective-permute-start.20
  69.6 0.8 collective-permute-start.21
  70.4 1.0 collective-permute-done.15.one
  71.4 1.4 collective-permute-start.22
  72.8 0.2 convert_reduce_fusion
  73.0 0.7 fusion.1
  73.7 4.5 %collective-permute-done.16.two = bf16[64,16,128]{2,1,0:T(8,128)(2,1)S(1)} collective-permute-done((bf16[64,16,128]{2,1,0:T(8,128)(2,1)}, bf16[64,16,128]{2,1,0:T(8,128)(2,1)S(1)}, u32[]{:S(2)}, u32[]{:S(2)}) %collective-permute-start.16) | collective-permute-done | bytes 262176 | tf_op jit(solution)/shard_map/ppermute | solution.py:393
  78.2 1.9 %sum_chunk.1.summed = bf16[64,16,128]{2,1,0:T(8,128)(2,1)S(1)} custom-call(bf16[64,16,128]{2,1,0:T(8,128)(2,1)S(1)} %get-tuple-element.53.mine, bf16[4,64,16,128]{3,2,1,0:T(8,128)(2,1)S(1)} %collective-permute-done.14.other, bf16[64,16,128]{2,1,0:T(8,128)(2,1)S(1)} %collective-permute-done.15.one, bf16[64,16,128]{2,1,0:T(8,128)(2,1)S(1)} %collective-permute-done.16.two, ...), custom_call_target="tpu_custom_call" | custom-call | flops 1048576 | bytes 2097152 | tf_op jit(solution)/shard_map/sum_chunk/pallas_call | solution.py:198
  80.1 3.4 %collective-permute-done.20.one = bf16[64,16,128]{2,1,0:T(8,128)(2,1)S(1)} collective-permute-done((bf16[64,16,128]{2,1,0:T(8,128)(2,1)}, bf16[64,16,128]{2,1,0:T(8,128)(2,1)S(1)}, u32[]{:S(2)}, u32[]{:S(2)}) %collective-permute-start.20) | collective-permute-done | bytes 262176 | tf_op jit(solution)/shard_map/ppermute | solution.py:393
  83.5 6.1 %collective-permute-done.21.two = bf16[64,16,128]{2,1,0:T(8,128)(2,1)} collective-permute-done((bf16[64,16,128]{2,1,0:T(8,128)(2,1)}, bf16[64,16,128]{2,1,0:T(8,128)(2,1)}, u32[]{:S(2)}, u32[]{:S(2)}) %collective-permute-start.21) | collective-permute-done | bytes 262176 | tf_op jit(solution)/shard_map/ppermute | solution.py:393
  89.5 2.3 %to_slots.1 = bf16[160,16,128]{2,1,0:T(8,128)(2,1)} custom-call(s32[128]{0:T(128)S(1)} %get-tuple-element.76.slot, bf16[64,16,128]{2,1,0:T(8,128)(2,1)S(1)} %sum_chunk.1.summed, bf16[64,16,128]{2,1,0:T(8,128)(2,1)S(1)} %get-tuple-element.61.mine, bf16[4,64,16,128]{3,2,1,0:T(8,128)(2,1)S(1)} %collective-permute-done.19.other, ...), custom_call_target="tpu_custom_call" | custom-call | tf_op jit(solution)/shard_map/to_slots/pallas_call | solution.py:229
  91.8 5.5 %all-to-all-start = ((bf16[32,5,16,128]{3,2,1,0:T(8,128)(2,1)}), bf16[32,5,16,128]{3,2,1,0:T(8,128)(2,1)S(1)}, u32[]{:S(2)}, u32[]{:S(2)}) async-start(bf16[32,5,16,128]{3,2,1,0:T(8,128)(2,1)} %bitcast.6), calls=%async_computation | async-start | bytes 1310720 | tf_op jit(solution)/shard_map/all_to_all | solution.py:354
  97.3 0.6 compare_convert_fusion.live
  98.0 12.3 %all-to-all-done.tiles = bf16[32,5,16,128]{3,2,1,0:T(8,128)(2,1)S(1)} async-done(((bf16[32,5,16,128]{3,2,1,0:T(8,128)(2,1)}), bf16[32,5,16,128]{3,2,1,0:T(8,128)(2,1)S(1)}, u32[]{:S(2)}, u32[]{:S(2)}) %all-to-all-start) | async-done | bytes 655392 | tf_op jit(solution)/shard_map/all_to_all | solution.py:354
  110.3 5.2 %update.1 = (bf16[32,5,16,128]{3,2,1,0:T(8,128)(2,1)S(1)}, bf16[5,256,256]{2,1,0:T(8,128)(2,1)S(1)}, bf16[1,5,256,256]{3,2,1,0:T(8,128)(2,1)}, bf16[1,5,256,256]{3,2,1,0:T(8,128)(2,1)}) custom-call(s32[5]{0:T(128)S(1)} %compare_convert_fusion.live, bf16[32,5,16,128]{3,2,1,0:T(8,128)(2,1)S(1)} %all-to-all-done.tiles, bf16[1,5,256,256]{3,2,1,0:T(8,128)(2,1)} %basis_left.1, ...), custom_call_target="tpu_custom_call" | custom-call | tf_op jit(solution)/shard_map/update/pallas_call | solution.py:307
  115.4 16.6 %all_to_all.15 = bf16[32,5,16,128]{3,2,1,0:T(8,128)(2,1)S(1)} all-to-all(bf16[32,5,16,128]{3,2,1,0:T(8,128)(2,1)S(1)} %get-tuple-element.69), channel_id=1, replica_groups=mesh['y'=4,'x'=4,'core'=2,'z'=8] {'y','x','core'}, dimensions={0} | all-to-all | bytes 1310720 | tf_op jit(solution)/shard_map/all_to_all | solution.py:354
  132.0 1.6 %from_slots.1 = bf16[128,16,128]{2,1,0:T(8,128)(2,1)} custom-call(s32[128]{0:T(128)S(1)} %get-tuple-element.76.slot, bf16[160,16,128]{2,1,0:T(8,128)(2,1)S(1)} %bitcast.11), custom_call_target="tpu_custom_call" | custom-call | tf_op jit(solution)/shard_map/from_slots/pallas_call | solution.py:247
  133.6 4.1 %all-to-all-start.2 = ((bf16[32,4,16,128]{3,2,1,0:T(8,128)(2,1)}), bf16[32,4,16,128]{3,2,1,0:T(8,128)(2,1)S(1)}, u32[]{:S(2)}, u32[]{:S(2)}) async-start(bf16[32,4,16,128]{3,2,1,0:T(8,128)(2,1)} %bitcast.8), calls=%async_computation.2 | async-start | bytes 1048576 | tf_op jit(solution)/shard_map/all_to_all | solution.py:354
  137.7 0.0 copy-start.3
  137.7 1.1 copy-done.3
  138.8 3.7 %factors.1 = (f32[1,5,256,256]{3,2,1,0:T(8,128)}, f32[1,5,256,256]{3,2,1,0:T(8,128)}) custom-call(s32[5]{0:T(128)S(1)} %compare_convert_fusion.live, bf16[5,256,256]{2,1,0:T(8,128)(2,1)S(1)} %copy-done.3, f32[1,5,256,256]{3,2,1,0:T(8,128)S(1)} %copy-done, f32[1,5,256,256]{3,2,1,0:T(8,128)S(1)} %copy-done.1), custom_call_target="tpu_custom_call" | custom-call | flops 335544320 | bytes 6291456 | tf_op jit(solution)/shard_map/factors/pallas_call | solution.py:336
  142.5 6.8 %all-to-all-done.2.tiles = bf16[32,4,16,128]{3,2,1,0:T(8,128)(2,1)S(1)} async-done(((bf16[32,4,16,128]{3,2,1,0:T(8,128)(2,1)}), bf16[32,4,16,128]{3,2,1,0:T(8,128)(2,1)S(1)}, u32[]{:S(2)}, u32[]{:S(2)}) %all-to-all-start.2) | async-done | bytes 524320 | tf_op jit(solution)/shard_map/all_to_all | solution.py:354
  149.3 0.9 assemble.1
  (21 shorter events, 0.1 us)
Async XLA Ops:
  0.7 1.0 copy-start.4
  2.5 4.4 %collective-permute-start = (bf16[32,1024]{1,0:T(8,128)(2,1)S(1)}, bf16[32,1024]{1,0:T(8,128)(2,1)S(1)}, u32[]{:S(2)}, u32[]{:S(2)}) collective-permute-start(bf16[32,1024]{1,0:T(8,128)(2,1)S(1)} %get-tuple-element.41), channel_id=1, source_target_pairs={{0,16},{16,32},{32,48},{48,0},{1,17},{17,33},{33,49},{49,1},{2,18}... | collective-permute-start | bytes 196616 | tf_op jit(solution)/shard_map/ppermute | solution.py:366
  3.8 3.1 %collective-permute-start.1 = (bf16[32,1024]{1,0:T(8,128)(2,1)S(1)}, bf16[32,1024]{1,0:T(8,128)(2,1)S(1)}, u32[]{:S(2)}, u32[]{:S(2)}) collective-permute-start(bf16[32,1024]{1,0:T(8,128)(2,1)S(1)} %get-tuple-element.42), channel_id=1, source_target_pairs={{0,48},{16,0},{32,16},{48,32},{1,49},{17,1},{33,17},{49,33},{2,50}... | collective-permute-start | bytes 196616 | tf_op jit(solution)/shard_map/ppermute | solution.py:366
  5.3 4.6 %collective-permute-start.2 = (bf16[32,1024]{1,0:T(8,128)(2,1)S(1)}, bf16[32,1024]{1,0:T(8,128)(2,1)S(1)}, u32[]{:S(2)}, u32[]{:S(2)}) collective-permute-start(bf16[32,1024]{1,0:T(8,128)(2,1)S(1)} %get-tuple-element.43), channel_id=1, source_target_pairs={{0,32},{16,48},{32,0},{48,16},{1,33},{17,49},{33,1},{49,17},{2,34}... | collective-permute-start | bytes 196616 | tf_op jit(solution)/shard_map/ppermute | solution.py:366
  9.9 26.6 %collective-permute-start.9 = (bf16[8,32,2048]{2,1,0:T(8,128)(2,1)}, bf16[8,32,2048]{2,1,0:T(8,128)(2,1)S(1)}, u32[]{:S(2)}, u32[]{:S(2)}) collective-permute-start(bf16[8,32,2048]{2,1,0:T(8,128)(2,1)} %bitcast.12), channel_id=1, source_target_pairs={{0,16},{16,32},{32,48},{48,0},{1,17},{17,33},{33,49},{49,1},{2,18}... | collective-permute-start | bytes 3145736 | tf_op jit(solution)/shard_map/ppermute | solution.py:368
  10.3 26.1 %collective-permute-start.10 = (bf16[8,32,2048]{2,1,0:T(8,128)(2,1)}, bf16[8,32,2048]{2,1,0:T(8,128)(2,1)S(1)}, u32[]{:S(2)}, u32[]{:S(2)}) collective-permute-start(bf16[8,32,2048]{2,1,0:T(8,128)(2,1)} %bitcast.13), channel_id=1, source_target_pairs={{0,48},{16,0},{32,16},{48,32},{1,49},{17,1},{33,17},{49,33},{2,50}... | collective-permute-start | bytes 3145736 | tf_op jit(solution)/shard_map/ppermute | solution.py:368
  12.7 33.1 %copy-start.5 = (bf16[256,2048]{1,0:T(8,128)(2,1)S(1)}, bf16[256,2048]{1,0:T(8,128)(2,1)}, u32[]{:S(2)}) copy-start(bf16[256,2048]{1,0:T(8,128)(2,1)} %param.10) | copy-start | bytes 3145732
  12.7 6.2 %collective-permute-start.3 = (bf16[1024,128]{1,0:T(8,128)(2,1)S(1)}, bf16[1024,128]{1,0:T(8,128)(2,1)S(1)}, u32[]{:S(2)}, u32[]{:S(2)}) collective-permute-start(bf16[1024,128]{1,0:T(8,128)(2,1)S(1)} %turn.1.refs_0_), channel_id=1, source_target_pairs={{0,1},{1,2},{2,3},{3,4},{4,5},{5,6},{6,7},{7,0},{8,9},{9,10},{10,1... | collective-permute-start | bytes 786440 | tf_op jit(solution)/shard_map/ppermute | solution.py:370
  15.7 6.7 %collective-permute-start.4 = (bf16[1024,128]{1,0:T(8,128)(2,1)S(1)}, bf16[1024,128]{1,0:T(8,128)(2,1)S(1)}, u32[]{:S(2)}, u32[]{:S(2)}) collective-permute-start(bf16[1024,128]{1,0:T(8,128)(2,1)S(1)} %turn.1.refs_0_), channel_id=1, source_target_pairs={{0,7},{1,0},{2,1},{3,2},{4,3},{5,4},{6,5},{7,6},{8,15},{9,8},{10,9... | collective-permute-start | bytes 786440 | tf_op jit(solution)/shard_map/ppermute | solution.py:370
  19.0 6.7 %collective-permute-start.5 = (bf16[1024,128]{1,0:T(8,128)(2,1)S(1)}, bf16[1024,128]{1,0:T(8,128)(2,1)S(1)}, u32[]{:S(2)}, u32[]{:S(2)}) collective-permute-start(bf16[1024,128]{1,0:T(8,128)(2,1)S(1)} %collective-permute-done.3.refs_1_), channel_id=1, source_target_pairs={{0,1},{1,2},{2,3},{3,4},{4,5},{5,6},{6,7},{7,0},{8,9},{9,10},{10,1... | collective-permute-start | bytes 786440 | tf_op jit(solution)/shard_map/ppermute | solution.py:372
  22.4 6.7 %collective-permute-start.6 = (bf16[1024,128]{1,0:T(8,128)(2,1)S(1)}, bf16[1024,128]{1,0:T(8,128)(2,1)S(1)}, u32[]{:S(2)}, u32[]{:S(2)}) collective-permute-start(bf16[1024,128]{1,0:T(8,128)(2,1)S(1)} %collective-permute-done.4.refs_2_), channel_id=1, source_target_pairs={{0,7},{1,0},{2,1},{3,2},{4,3},{5,4},{6,5},{7,6},{8,15},{9,8},{10,9... | collective-permute-start | bytes 786440 | tf_op jit(solution)/shard_map/ppermute | solution.py:372
  25.7 7.1 %collective-permute-start.7 = (bf16[1024,128]{1,0:T(8,128)(2,1)S(1)}, bf16[1024,128]{1,0:T(8,128)(2,1)S(1)}, u32[]{:S(2)}, u32[]{:S(2)}) collective-permute-start(bf16[1024,128]{1,0:T(8,128)(2,1)S(1)} %collective-permute-done.5.refs_3_), channel_id=1, source_target_pairs={{0,1},{1,2},{2,3},{3,4},{4,5},{5,6},{6,7},{7,0},{8,9},{9,10},{10,1... | collective-permute-start | bytes 786440 | tf_op jit(solution)/shard_map/ppermute | solution.py:374
  29.1 7.3 %collective-permute-start.8 = (bf16[1024,128]{1,0:T(8,128)(2,1)S(1)}, bf16[1024,128]{1,0:T(8,128)(2,1)S(1)}, u32[]{:S(2)}, u32[]{:S(2)}) collective-permute-start(bf16[1024,128]{1,0:T(8,128)(2,1)S(1)} %collective-permute-done.6.refs_4_), channel_id=1, source_target_pairs={{0,7},{1,0},{2,1},{3,2},{4,3},{5,4},{6,5},{7,6},{8,15},{9,8},{10,9... | collective-permute-start | bytes 786440 | tf_op jit(solution)/shard_map/ppermute | solution.py:374
  36.5 9.3 %collective-permute-start.13 = (bf16[8,32,1024]{2,1,0:T(8,128)(2,1)S(1)}, bf16[8,32,1024]{2,1,0:T(8,128)(2,1)S(1)}, u32[]{:S(2)}, u32[]{:S(2)}) collective-permute-start(bf16[8,32,1024]{2,1,0:T(8,128)(2,1)S(1)} %slice.14), channel_id=1, source_target_pairs={{0,16},{16,32},{32,48},{48,0},{1,17},{17,33},{33,49},{49,1},{2,18}... | collective-permute-start | bytes 1572872 | tf_op jit(solution)/shard_map/ppermute | solution.py:379
  36.7 20.3 %collective-permute-start.18 = (bf16[8,32,1024]{2,1,0:T(8,128)(2,1)S(1)}, bf16[8,32,1024]{2,1,0:T(8,128)(2,1)S(1)}, u32[]{:S(2)}, u32[]{:S(2)}) collective-permute-start(bf16[8,32,1024]{2,1,0:T(8,128)(2,1)S(1)} %slice.15), channel_id=1, source_target_pairs={{0,48},{16,0},{32,16},{48,32},{1,49},{17,1},{33,17},{49,33},{2,50}... | collective-permute-start | bytes 1572872 | tf_op jit(solution)/shard_map/ppermute | solution.py:380
  39.4 3.9 %collective-permute-start.11 = (bf16[512,128]{1,0:T(8,128)(2,1)S(1)}, bf16[512,128]{1,0:T(8,128)(2,1)S(1)}, u32[]{:S(2)}, u32[]{:S(2)}) collective-permute-start(bf16[512,128]{1,0:T(8,128)(2,1)S(1)} %slice.12), channel_id=1, source_target_pairs={{0,1},{1,2},{2,3},{3,4},{4,5},{5,6},{6,7},{7,0},{8,9},{9,10},{10,1... | collective-permute-start | bytes 393224 | tf_op jit(solution)/shard_map/ppermute | solution.py:383
  39.5 5.3 %collective-permute-start.12 = (bf16[512,128]{1,0:T(8,128)(2,1)S(1)}, bf16[512,128]{1,0:T(8,128)(2,1)S(1)}, u32[]{:S(2)}, u32[]{:S(2)}) collective-permute-start(bf16[512,128]{1,0:T(8,128)(2,1)S(1)} %slice.13), channel_id=1, source_target_pairs={{0,7},{1,0},{2,1},{3,2},{4,3},{5,4},{6,5},{7,6},{8,15},{9,8},{10,9... | collective-permute-start | bytes 393224 | tf_op jit(solution)/shard_map/ppermute | solution.py:384
  50.0 11.2 %collective-permute-start.14 = (bf16[4,64,16,128]{3,2,1,0:T(8,128)(2,1)S(1)}, bf16[4,64,16,128]{3,2,1,0:T(8,128)(2,1)S(1)}, u32[]{:S(2)}, u32[]{:S(2)}) collective-permute-start(bf16[4,64,16,128]{3,2,1,0:T(8,128)(2,1)S(1)} %get-tuple-element.54), channel_id=1, source_target_pairs={{0,8},{8,0},{1,9},{9,1},{2,10},{10,2},{3,11},{11,3},{4,12},{12,4},... | collective-permute-start | bytes 3145736 | tf_op jit(solution)/shard_map/ppermute | solution.py:390
  61.1 6.6 %collective-permute-start.19 = (bf16[4,64,16,128]{3,2,1,0:T(8,128)(2,1)S(1)}, bf16[4,64,16,128]{3,2,1,0:T(8,128)(2,1)S(1)}, u32[]{:S(2)}, u32[]{:S(2)}) collective-permute-start(bf16[4,64,16,128]{3,2,1,0:T(8,128)(2,1)S(1)} %get-tuple-element.62), channel_id=1, source_target_pairs={{0,8},{8,0},{1,9},{9,1},{2,10},{10,2},{3,11},{11,3},{4,12},{12,4},... | collective-permute-start | bytes 3145736 | tf_op jit(solution)/shard_map/ppermute | solution.py:390
  62.7 10.1 %copy-start.6 = (s32[1,128]{1,0:T(1,128)S(1)}, s32[1,128]{1,0:T(1,128)}, u32[]{:S(2)}) copy-start(s32[1,128]{1,0:T(1,128)} %param.11) | copy-start | bytes 1540
  62.7 8.7 %collective-permute-start.15 = (bf16[64,16,128]{2,1,0:T(8,128)(2,1)S(1)}, bf16[64,16,128]{2,1,0:T(8,128)(2,1)S(1)}, u32[]{:S(2)}, u32[]{:S(2)}) collective-permute-start(bf16[64,16,128]{2,1,0:T(8,128)(2,1)S(1)} %get-tuple-element.58), channel_id=1, source_target_pairs={{0,64},{64,128},{128,192},{192,0},{1,65},{65,129},{129,193},{193,1... | collective-permute-start | bytes 786440 | tf_op jit(solution)/shard_map/ppermute | solution.py:393
  63.9 14.2 %collective-permute-start.16 = (bf16[64,16,128]{2,1,0:T(8,128)(2,1)}, bf16[64,16,128]{2,1,0:T(8,128)(2,1)S(1)}, u32[]{:S(2)}, u32[]{:S(2)}) collective-permute-start(bf16[64,16,128]{2,1,0:T(8,128)(2,1)} %get-tuple-element.59), channel_id=1, source_target_pairs={{0,128},{64,192},{128,0},{192,64},{1,129},{65,193},{129,1},{193,65... | collective-permute-start | bytes 786440 | tf_op jit(solution)/shard_map/ppermute | solution.py:393
  66.6 11.6 %collective-permute-start.17 = (bf16[64,16,128]{2,1,0:T(8,128)(2,1)}, bf16[64,16,128]{2,1,0:T(8,128)(2,1)}, u32[]{:S(2)}, u32[]{:S(2)}) collective-permute-start(bf16[64,16,128]{2,1,0:T(8,128)(2,1)} %get-tuple-element.60), channel_id=1, source_target_pairs={{0,192},{64,0},{128,64},{192,128},{1,193},{65,1},{129,65},{193,129... | collective-permute-start | bytes 786440 | tf_op jit(solution)/shard_map/ppermute | solution.py:393
  69.2 14.3 %collective-permute-start.20 = (bf16[64,16,128]{2,1,0:T(8,128)(2,1)}, bf16[64,16,128]{2,1,0:T(8,128)(2,1)S(1)}, u32[]{:S(2)}, u32[]{:S(2)}) collective-permute-start(bf16[64,16,128]{2,1,0:T(8,128)(2,1)} %get-tuple-element.66), channel_id=1, source_target_pairs={{0,64},{64,128},{128,192},{192,0},{1,65},{65,129},{129,193},{193,1... | collective-permute-start | bytes 786440 | tf_op jit(solution)/shard_map/ppermute | solution.py:393
  69.6 19.9 %collective-permute-start.21 = (bf16[64,16,128]{2,1,0:T(8,128)(2,1)}, bf16[64,16,128]{2,1,0:T(8,128)(2,1)}, u32[]{:S(2)}, u32[]{:S(2)}) collective-permute-start(bf16[64,16,128]{2,1,0:T(8,128)(2,1)} %get-tuple-element.67), channel_id=1, source_target_pairs={{0,128},{64,192},{128,0},{192,64},{1,129},{65,193},{129,1},{193,65... | collective-permute-start | bytes 786440 | tf_op jit(solution)/shard_map/ppermute | solution.py:393
  71.4 18.1 %collective-permute-start.22 = (bf16[64,16,128]{2,1,0:T(8,128)(2,1)}, bf16[64,16,128]{2,1,0:T(8,128)(2,1)}, u32[]{:S(2)}, u32[]{:S(2)}) collective-permute-start(bf16[64,16,128]{2,1,0:T(8,128)(2,1)} %get-tuple-element.68), channel_id=1, source_target_pairs={{0,192},{64,0},{128,64},{192,128},{1,193},{65,1},{129,65},{193,129... | collective-permute-start | bytes 786440 | tf_op jit(solution)/shard_map/ppermute | solution.py:393
  91.8 18.4 %all-to-all-start = ((bf16[32,5,16,128]{3,2,1,0:T(8,128)(2,1)}), bf16[32,5,16,128]{3,2,1,0:T(8,128)(2,1)S(1)}, u32[]{:S(2)}, u32[]{:S(2)}) async-start(bf16[32,5,16,128]{3,2,1,0:T(8,128)(2,1)} %bitcast.6), calls=%async_computation | async-start | bytes 1310720 | tf_op jit(solution)/shard_map/all_to_all | solution.py:354
  115.4 18.2 %copy-start.2 = (bf16[5,256,256]{2,1,0:T(8,128)(2,1)}, bf16[5,256,256]{2,1,0:T(8,128)(2,1)S(1)}, u32[]{:S(2)}) copy-start(bf16[5,256,256]{2,1,0:T(8,128)(2,1)S(1)} %get-tuple-element.70.grads) | copy-start | bytes 1966084
  115.4 22.3 %copy-start.1 = (f32[1,5,256,256]{3,2,1,0:T(8,128)S(1)}, f32[1,5,256,256]{3,2,1,0:T(8,128)}, u32[]{:S(2)}) copy-start(f32[1,5,256,256]{3,2,1,0:T(8,128)} %right.1) | copy-start | bytes 3932164
  132.0 5.7 %copy-start = (f32[1,5,256,256]{3,2,1,0:T(8,128)S(1)}, f32[1,5,256,256]{3,2,1,0:T(8,128)}, u32[]{:S(2)}) copy-start(f32[1,5,256,256]{3,2,1,0:T(8,128)} %left.1) | copy-start | bytes 3932164
  133.6 15.8 %all-to-all-start.2 = ((bf16[32,4,16,128]{3,2,1,0:T(8,128)(2,1)}), bf16[32,4,16,128]{3,2,1,0:T(8,128)(2,1)S(1)}, u32[]{:S(2)}, u32[]{:S(2)}) async-start(bf16[32,4,16,128]{3,2,1,0:T(8,128)(2,1)} %bitcast.8), calls=%async_computation.2 | async-start | bytes 1048576 | tf_op jit(solution)/shard_map/all_to_all | solution.py:354
  137.7 1.1 copy-start.3

commit v7 on v6

--- a/solution.py
+++ b/solution.py
@@ -170,14 +170,8 @@
 
 
 def add_cores(parts, other):
-    blocks = CHUNK_K // 4
-    part = pl.BlockSpec((blocks, TILE_ROWS, TILE_COLS), lambda c: (c, 0, 0))
     return pl.pallas_call(
         add_cores_kernel,
-        grid=(4,),
-        in_specs=[part] * 3
-        + [pl.BlockSpec((Y, blocks, TILE_ROWS, TILE_COLS), lambda c: (0, c, 0, 0))],
-        out_specs=[part] * 3,
         out_shape=[jax.ShapeDtypeStruct(a.shape, a.dtype) for a in parts[1:]],
         compiler_params=params(16),
         name="add_cores",
@@ -192,14 +186,8 @@
 
 
 def sum_chunk(parts):
-    blocks = CHUNK_K // 4
-    part = pl.BlockSpec((blocks, TILE_ROWS, TILE_COLS), lambda c: (c, 0, 0))
-    first = pl.BlockSpec((1, blocks, TILE_ROWS, TILE_COLS), lambda c: (0, c, 0, 0))
     return pl.pallas_call(
         sum_kernel,
-        grid=(4,),
-        in_specs=[part, first, part, part, part],
-        out_specs=part,
         out_shape=jax.ShapeDtypeStruct((CHUNK_K, TILE_ROWS, TILE_COLS), jnp.bfloat16),
         compiler_params=params(16),
         cost_estimate=pl.CostEstimate(flops=MIB, bytes_accessed=2 * MIB, transcendentals=0),
@@ -221,8 +209,8 @@
         out[slot[CHUNK_K + k]] = total.astype(jnp.bfloat16)
         return carry
 
-    lax.fori_loop(0, CHUNK_K, early, 0, unroll=8)
-    lax.fori_loop(0, CHUNK_K, late, 0, unroll=8)
+    lax.fori_loop(0, CHUNK_K, early, 0, unroll=16)
+    lax.fori_loop(0, CHUNK_K, late, 0, unroll=16)
 
 
 def to_slots(slot, chunks):
@@ -240,7 +228,7 @@
         out[k] = tiles[slot[k]]
         return carry
 
-    lax.fori_loop(0, NBLK, body, 0, unroll=8)
+    lax.fori_loop(0, NBLK, body, 0, unroll=32)
 
 
 def from_slots(slot, tiles):

time: 151 us -> 150 us (level)
  Pallas kernels: 27.7 us -> 25.7 us
    pallas_call x3, Pallas kernels: 4.86 us -> 2.99 us  [the longest x2 1.88 us: add_cores(): pl.pallas_call(add_cores_kernel, out_shape=[jax.ShapeDtypeStruct(a.shape,...]
  transfers between devices with their start and end apart: 25 -> 25, of which waited for: 15 -> 15; matrix products, arithmetic and copies ran while one was open for 1% -> 1% of each run, Pallas kernels for 11% -> 10%
where the time goes in v7:
time: 150 us
  waiting for transfers between devices  57.1 us (38%)
  starting transfers between devices  45.6 us (30%)
  Pallas kernels  25.7 us (17%)
  blocking collectives  16.6 us (11%)
  local copies, waits for them, and re-layouts  2.15 us (1%)
  other arithmetic  1.58 us (1%)
    all_to_all x2, waiting for transfers between devices, spread(): return lax.all_to_all(array, axes, split_axis=0, concat_axis=0, tiled=True)  19.1 us
    all_to_all x1, blocking collectives, spread(): return lax.all_to_all(array, axes, split_axis=0, concat_axis=0, tiled=True)  16.6 us
    ppermute x6, waiting for transfers between devices, sum_parts(): lax.ppermute(a, 'y', ring(Y, step))  16.3 us
    all_to_all x2, starting transfers between devices, spread(): return lax.all_to_all(array, axes, split_axis=0, concat_axis=0, tiled=True)  9.62 us
    pallas_call x2, Pallas kernels, gradient_tiles(): pl.pallas_call(gradient_kernel, grid_spec=pltpu.PrefetchScalarGridSpec(nu...  8.24 us
    ppermute x6, starting transfers between devices, sum_parts(): lax.ppermute(a, 'y', ring(Y, step))  7.57 us
    ppermute x2, starting transfers between devices, sum_parts(): mine, other = (parts[:Y], lax.ppermute(parts[Y], 'core', ring(CORE, 1)))  7.08 us
    ppermute x2, waiting for transfers between devices, gather_row(): lax.ppermute(below, 'z', up)  6.96 us
  transfers between devices with their start and end apart: 25, of which 15 were waited for; matrix products, arithmetic and copies ran while one was open for 1% of the time, Pallas kernels for 10%

profile of v7, /device:TPU:97, one launch (start us, length us, event | category | flops | bytes accessed | tf_op | source)
XLA Modules:
  0.0 149.5 jit_solution(1632958417681626960)
XLA Ops:
  0.6 0.1 pad_add_fusion.spot
  0.7 0.9 copy-done.4
  1.7 0.9 cut_tokens.1
  2.5 1.3 collective-permute-start
  3.8 1.5 collective-permute-start.1
  5.3 1.5 %collective-permute-start.2 = (bf16[32,1024]{1,0:T(8,128)(2,1)S(1)}, bf16[32,1024]{1,0:T(8,128)(2,1)S(1)}, u32[]{:S(2)}, u32[]{:S(2)}) collective-permute-start(bf16[32,1024]{1,0:T(8,128)(2,1)S(1)} %get-tuple-element.43), channel_id=1, source_target_pairs={{0,32},{16,48},{32,0},{48,16},{1,33},{17,49},{33,1},{49,17},{2,34}... | collective-permute-start | bytes 196616 | tf_op jit(solution)/shard_map/ppermute | solution.py:354
  6.8 0.1 collective-permute-done.refs_1_
  6.9 0.0 collective-permute-done.1.refs_2_
  6.9 3.0 %collective-permute-done.2.refs_3_ = bf16[32,1024]{1,0:T(8,128)(2,1)S(1)} collective-permute-done((bf16[32,1024]{1,0:T(8,128)(2,1)S(1)}, bf16[32,1024]{1,0:T(8,128)(2,1)S(1)}, u32[]{:S(2)}, u32[]{:S(2)}) %collective-permute-start.2) | collective-permute-done | bytes 65568 | tf_op jit(solution)/shard_map/ppermute | solution.py:354
  9.9 0.4 collective-permute-start.9
  10.3 2.3 %collective-permute-start.10 = (bf16[8,32,2048]{2,1,0:T(8,128)(2,1)}, bf16[8,32,2048]{2,1,0:T(8,128)(2,1)S(1)}, u32[]{:S(2)}, u32[]{:S(2)}) collective-permute-start(bf16[8,32,2048]{2,1,0:T(8,128)(2,1)} %bitcast.13), channel_id=1, source_target_pairs={{0,48},{16,0},{32,16},{48,32},{1,49},{17,1},{33,17},{49,33},{2,50}... | collective-permute-start | bytes 3145736 | tf_op jit(solution)/shard_map/ppermute | solution.py:356
  12.6 0.1 turn.1.refs_0_
  12.7 0.0 copy-start.5
  12.7 2.9 %collective-permute-start.3 = (bf16[1024,128]{1,0:T(8,128)(2,1)S(1)}, bf16[1024,128]{1,0:T(8,128)(2,1)S(1)}, u32[]{:S(2)}, u32[]{:S(2)}) collective-permute-start(bf16[1024,128]{1,0:T(8,128)(2,1)S(1)} %turn.1.refs_0_), channel_id=1, source_target_pairs={{0,1},{1,2},{2,3},{3,4},{4,5},{5,6},{6,7},{7,0},{8,9},{9,10},{10,1... | collective-permute-start | bytes 786440 | tf_op jit(solution)/shard_map/ppermute | solution.py:358
  15.7 0.0 collective-permute-start.4
  15.7 3.3 %collective-permute-done.3.refs_1_ = bf16[1024,128]{1,0:T(8,128)(2,1)S(1)} collective-permute-done((bf16[1024,128]{1,0:T(8,128)(2,1)S(1)}, bf16[1024,128]{1,0:T(8,128)(2,1)S(1)}, u32[]{:S(2)}, u32[]{:S(2)}) %collective-permute-start.3) | collective-permute-done | bytes 262176 | tf_op jit(solution)/shard_map/ppermute | solution.py:358
  19.0 3.4 %collective-permute-start.5 = (bf16[1024,128]{1,0:T(8,128)(2,1)S(1)}, bf16[1024,128]{1,0:T(8,128)(2,1)S(1)}, u32[]{:S(2)}, u32[]{:S(2)}) collective-permute-start(bf16[1024,128]{1,0:T(8,128)(2,1)S(1)} %collective-permute-done.3.refs_1_), channel_id=1, source_target_pairs={{0,1},{1,2},{2,3},{3,4},{4,5},{5,6},{6,7},{7,0},{8,9},{9,10},{10,1... | collective-permute-start | bytes 786440 | tf_op jit(solution)/shard_map/ppermute | solution.py:360
  22.4 0.0 collective-permute-done.4.refs_2_
  22.4 0.0 collective-permute-start.6
  22.4 3.3 %collective-permute-done.5.refs_3_ = bf16[1024,128]{1,0:T(8,128)(2,1)S(1)} collective-permute-done((bf16[1024,128]{1,0:T(8,128)(2,1)S(1)}, bf16[1024,128]{1,0:T(8,128)(2,1)S(1)}, u32[]{:S(2)}, u32[]{:S(2)}) %collective-permute-start.5) | collective-permute-done | bytes 262176 | tf_op jit(solution)/shard_map/ppermute | solution.py:360
  25.7 3.4 %collective-permute-start.7 = (bf16[1024,128]{1,0:T(8,128)(2,1)S(1)}, bf16[1024,128]{1,0:T(8,128)(2,1)S(1)}, u32[]{:S(2)}, u32[]{:S(2)}) collective-permute-start(bf16[1024,128]{1,0:T(8,128)(2,1)S(1)} %collective-permute-done.5.refs_3_), channel_id=1, source_target_pairs={{0,1},{1,2},{2,3},{3,4},{4,5},{5,6},{6,7},{7,0},{8,9},{9,10},{10,1... | collective-permute-start | bytes 786440 | tf_op jit(solution)/shard_map/ppermute | solution.py:362
  29.1 0.0 collective-permute-done.6.refs_4_
  29.1 3.6 %collective-permute-done.7.refs_5_ = bf16[1024,128]{1,0:T(8,128)(2,1)S(1)} collective-permute-done((bf16[1024,128]{1,0:T(8,128)(2,1)S(1)}, bf16[1024,128]{1,0:T(8,128)(2,1)S(1)}, u32[]{:S(2)}, u32[]{:S(2)}) %collective-permute-start.7) | collective-permute-done | bytes 262176 | tf_op jit(solution)/shard_map/ppermute | solution.py:362
  32.8 3.7 %collective-permute-done.8.refs_6_ = bf16[1024,128]{1,0:T(8,128)(2,1)S(1)} collective-permute-done((bf16[1024,128]{1,0:T(8,128)(2,1)S(1)}, bf16[1024,128]{1,0:T(8,128)(2,1)S(1)}, u32[]{:S(2)}, u32[]{:S(2)}) %collective-permute-start.8) | collective-permute-done | bytes 262176 | tf_op jit(solution)/shard_map/ppermute | solution.py:362
  36.5 0.1 collective-permute-start.13
  36.7 2.7 %collective-permute-start.18 = (bf16[8,32,1024]{2,1,0:T(8,128)(2,1)S(1)}, bf16[8,32,1024]{2,1,0:T(8,128)(2,1)S(1)}, u32[]{:S(2)}, u32[]{:S(2)}) collective-permute-start(bf16[8,32,1024]{2,1,0:T(8,128)(2,1)S(1)} %slice.15), channel_id=1, source_target_pairs={{0,48},{16,0},{32,16},{48,32},{1,49},{17,1},{33,17},{49,33},{2,50}... | collective-permute-start | bytes 1572872 | tf_op jit(solution)/shard_map/ppermute | solution.py:368
  39.4 0.1 collective-permute-start.11
  39.5 1.7 %collective-permute-start.12 = (bf16[512,128]{1,0:T(8,128)(2,1)S(1)}, bf16[512,128]{1,0:T(8,128)(2,1)S(1)}, u32[]{:S(2)}, u32[]{:S(2)}) collective-permute-start(bf16[512,128]{1,0:T(8,128)(2,1)S(1)} %slice.13), channel_id=1, source_target_pairs={{0,7},{1,0},{2,1},{3,2},{4,3},{5,4},{6,5},{7,6},{8,15},{9,8},{10,9... | collective-permute-start | bytes 393224 | tf_op jit(solution)/shard_map/ppermute | solution.py:372
  41.2 2.1 %collective-permute-done.11.refs_7_ = bf16[512,128]{1,0:T(8,128)(2,1)S(1)} collective-permute-done((bf16[512,128]{1,0:T(8,128)(2,1)S(1)}, bf16[512,128]{1,0:T(8,128)(2,1)S(1)}, u32[]{:S(2)}, u32[]{:S(2)}) %collective-permute-start.11) | collective-permute-done | bytes 131104 | tf_op jit(solution)/shard_map/ppermute | solution.py:371
  43.3 1.5 %collective-permute-done.12.refs_8_ = bf16[512,128]{1,0:T(8,128)(2,1)S(1)} collective-permute-done((bf16[512,128]{1,0:T(8,128)(2,1)S(1)}, bf16[512,128]{1,0:T(8,128)(2,1)S(1)}, u32[]{:S(2)}, u32[]{:S(2)}) %collective-permute-start.12) | collective-permute-done | bytes 131104 | tf_op jit(solution)/shard_map/ppermute | solution.py:372
  44.8 1.0 collective-permute-done.13.refs_12_
  45.8 4.1 %gradient_tiles.2 = (bf16[64,16,128]{2,1,0:T(8,128)(2,1)S(1)}, bf16[64,16,128]{2,1,0:T(8,128)(2,1)S(1)}, bf16[64,16,128]{2,1,0:T(8,128)(2,1)S(1)}, bf16[64,16,12...) custom-call(s32[4]{0:T(128)S(1)} %pad_add_fusion.spot, bf16[1024,128]{1,0:T(8,128)(2,1)S(1)} %turn.1.refs_0_, ...), custom_call_target="tpu_custom_call" | custom-call | flops 2147483648 | bytes 8388608 | tf_op jit(solution)/shard_map/gradient_tiles/pallas_call | solution.py:140
  50.0 7.0 %collective-permute-start.14 = (bf16[4,64,16,128]{3,2,1,0:T(8,128)(2,1)S(1)}, bf16[4,64,16,128]{3,2,1,0:T(8,128)(2,1)S(1)}, u32[]{:S(2)}, u32[]{:S(2)}) collective-permute-start(bf16[4,64,16,128]{3,2,1,0:T(8,128)(2,1)S(1)} %get-tuple-element.54), channel_id=1, source_target_pairs={{0,8},{8,0},{1,9},{9,1},{2,10},{10,2},{3,11},{11,3},{4,12},{12,4},... | collective-permute-start | bytes 3145736 | tf_op jit(solution)/shard_map/ppermute | solution.py:378
  56.9 4.1 %gradient_tiles.3 = (bf16[64,16,128]{2,1,0:T(8,128)(2,1)S(1)}, bf16[64,16,128]{2,1,0:T(8,128)(2,1)S(1)}, bf16[64,16,128]{2,1,0:T(8,128)(2,1)S(1)}, bf16[64,16,12...) custom-call(s32[4]{0:T(128)S(1)} %pad_add_fusion.spot, bf16[1024,128]{1,0:T(8,128)(2,1)S(1)} %turn.1.refs_0_, ...), custom_call_target="tpu_custom_call" | custom-call | flops 2147483648 | bytes 8388608 | tf_op jit(solution)/shard_map/gradient_tiles/pallas_call | solution.py:140
  61.1 0.1 collective-permute-start.19
  61.2 0.9 add_cores.2
  62.1 1.3 collective-permute-start.15
  63.4 2.6 %collective-permute-start.16 = (bf16[64,16,128]{2,1,0:T(8,128)(2,1)}, bf16[64,16,128]{2,1,0:T(8,128)(2,1)S(1)}, u32[]{:S(2)}, u32[]{:S(2)}) collective-permute-start(bf16[64,16,128]{2,1,0:T(8,128)(2,1)} %get-tuple-element.59), channel_id=1, source_target_pairs={{0,128},{64,192},{128,0},{192,64},{1,129},{65,193},{129,1},{193,65... | collective-permute-start | bytes 786440 | tf_op jit(solution)/shard_map/ppermute | solution.py:381
  66.0 1.1 collective-permute-start.17
  67.1 1.0 add_cores.3
  68.1 0.4 collective-permute-start.20
  68.5 0.8 collective-permute-start.21
  69.2 1.6 %collective-permute-done.15.one = bf16[64,16,128]{2,1,0:T(8,128)(2,1)S(1)} collective-permute-done((bf16[64,16,128]{2,1,0:T(8,128)(2,1)S(1)}, bf16[64,16,128]{2,1,0:T(8,128)(2,1)S(1)}, u32[]{:S(2)}, u32[]{:S(2)}) %collective-permute-start.15) | collective-permute-done | bytes 262176 | tf_op jit(solution)/shard_map/ppermute | solution.py:381
  70.8 1.4 collective-permute-start.22
  72.2 0.2 convert_reduce_fusion
  72.4 0.7 fusion.1
  73.1 4.5 %collective-permute-done.16.two = bf16[64,16,128]{2,1,0:T(8,128)(2,1)S(1)} collective-permute-done((bf16[64,16,128]{2,1,0:T(8,128)(2,1)}, bf16[64,16,128]{2,1,0:T(8,128)(2,1)S(1)}, u32[]{:S(2)}, u32[]{:S(2)}) %collective-permute-start.16) | collective-permute-done | bytes 262176 | tf_op jit(solution)/shard_map/ppermute | solution.py:381
  77.6 0.0 collective-permute-done.17.three
  77.6 1.1 sum_chunk.1.summed
  78.7 3.6 %collective-permute-done.20.one = bf16[64,16,128]{2,1,0:T(8,128)(2,1)S(1)} collective-permute-done((bf16[64,16,128]{2,1,0:T(8,128)(2,1)}, bf16[64,16,128]{2,1,0:T(8,128)(2,1)S(1)}, u32[]{:S(2)}, u32[]{:S(2)}) %collective-permute-start.20) | collective-permute-done | bytes 262176 | tf_op jit(solution)/shard_map/ppermute | solution.py:381
  82.3 6.6 %collective-permute-done.21.two = bf16[64,16,128]{2,1,0:T(8,128)(2,1)} collective-permute-done((bf16[64,16,128]{2,1,0:T(8,128)(2,1)}, bf16[64,16,128]{2,1,0:T(8,128)(2,1)}, u32[]{:S(2)}, u32[]{:S(2)}) %collective-permute-start.21) | collective-permute-done | bytes 262176 | tf_op jit(solution)/shard_map/ppermute | solution.py:381
  88.9 2.2 %to_slots.1 = bf16[160,16,128]{2,1,0:T(8,128)(2,1)} custom-call(s32[128]{0:T(128)S(1)} %get-tuple-element.76.slot, bf16[64,16,128]{2,1,0:T(8,128)(2,1)S(1)} %sum_chunk.1.summed, bf16[64,16,128]{2,1,0:T(8,128)(2,1)S(1)} %get-tuple-element.61.mine, bf16[4,64,16,128]{3,2,1,0:T(8,128)(2,1)S(1)} %collective-permute-done.19.other, ...), custom_call_target="tpu_custom_call" | custom-call | tf_op jit(solution)/shard_map/to_slots/pallas_call | solution.py:217
  91.2 5.5 %all-to-all-start = ((bf16[32,5,16,128]{3,2,1,0:T(8,128)(2,1)}), bf16[32,5,16,128]{3,2,1,0:T(8,128)(2,1)S(1)}, u32[]{:S(2)}, u32[]{:S(2)}) async-start(bf16[32,5,16,128]{3,2,1,0:T(8,128)(2,1)} %bitcast.6), calls=%async_computation | async-start | bytes 1310720 | tf_op jit(solution)/shard_map/all_to_all | solution.py:342
  96.7 0.6 compare_convert_fusion.live
  97.4 12.3 %all-to-all-done.tiles = bf16[32,5,16,128]{3,2,1,0:T(8,128)(2,1)S(1)} async-done(((bf16[32,5,16,128]{3,2,1,0:T(8,128)(2,1)}), bf16[32,5,16,128]{3,2,1,0:T(8,128)(2,1)S(1)}, u32[]{:S(2)}, u32[]{:S(2)}) %all-to-all-start) | async-done | bytes 655392 | tf_op jit(solution)/shard_map/all_to_all | solution.py:342
  109.6 5.2 %update.1 = (bf16[32,5,16,128]{3,2,1,0:T(8,128)(2,1)S(1)}, bf16[5,256,256]{2,1,0:T(8,128)(2,1)S(1)}, bf16[1,5,256,256]{3,2,1,0:T(8,128)(2,1)}, bf16[1,5,256,256]{3,2,1,0:T(8,128)(2,1)}) custom-call(s32[5]{0:T(128)S(1)} %compare_convert_fusion.live, bf16[32,5,16,128]{3,2,1,0:T(8,128)(2,1)S(1)} %all-to-all-done.tiles, bf16[1,5,256,256]{3,2,1,0:T(8,128)(2,1)} %basis_left.1, ...), custom_call_target="tpu_custom_call" | custom-call | tf_op jit(solution)/shard_map/update/pallas_call | solution.py:295
  114.8 16.6 %all_to_all.15 = bf16[32,5,16,128]{3,2,1,0:T(8,128)(2,1)S(1)} all-to-all(bf16[32,5,16,128]{3,2,1,0:T(8,128)(2,1)S(1)} %get-tuple-element.69), channel_id=1, replica_groups=mesh['y'=4,'x'=4,'core'=2,'z'=8] {'y','x','core'}, dimensions={0} | all-to-all | bytes 1310720 | tf_op jit(solution)/shard_map/all_to_all | solution.py:342
  131.4 1.5 from_slots.1
  132.9 4.1 %all-to-all-start.2 = ((bf16[32,4,16,128]{3,2,1,0:T(8,128)(2,1)}), bf16[32,4,16,128]{3,2,1,0:T(8,128)(2,1)S(1)}, u32[]{:S(2)}, u32[]{:S(2)}) async-start(bf16[32,4,16,128]{3,2,1,0:T(8,128)(2,1)} %bitcast.8), calls=%async_computation.2 | async-start | bytes 1048576 | tf_op jit(solution)/shard_map/all_to_all | solution.py:342
  137.0 0.0 copy-start.3
  137.0 1.1 copy-done.3
  138.1 3.7 %factors.1 = (f32[1,5,256,256]{3,2,1,0:T(8,128)}, f32[1,5,256,256]{3,2,1,0:T(8,128)}) custom-call(s32[5]{0:T(128)S(1)} %compare_convert_fusion.live, bf16[5,256,256]{2,1,0:T(8,128)(2,1)S(1)} %copy-done.3, f32[1,5,256,256]{3,2,1,0:T(8,128)S(1)} %copy-done, f32[1,5,256,256]{3,2,1,0:T(8,128)S(1)} %copy-done.1), custom_call_target="tpu_custom_call" | custom-call | flops 335544320 | bytes 6291456 | tf_op jit(solution)/shard_map/factors/pallas_call | solution.py:324
  141.8 6.8 %all-to-all-done.2.tiles = bf16[32,4,16,128]{3,2,1,0:T(8,128)(2,1)S(1)} async-done(((bf16[32,4,16,128]{3,2,1,0:T(8,128)(2,1)}), bf16[32,4,16,128]{3,2,1,0:T(8,128)(2,1)S(1)}, u32[]{:S(2)}, u32[]{:S(2)}) %all-to-all-start.2) | async-done | bytes 524320 | tf_op jit(solution)/shard_map/all_to_all | solution.py:342
  148.7 0.9 assemble.1
  (21 shorter events, 0.1 us)
Async XLA Ops:
  0.7 1.0 copy-start.4
  2.5 4.4 %collective-permute-start = (bf16[32,1024]{1,0:T(8,128)(2,1)S(1)}, bf16[32,1024]{1,0:T(8,128)(2,1)S(1)}, u32[]{:S(2)}, u32[]{:S(2)}) collective-permute-start(bf16[32,1024]{1,0:T(8,128)(2,1)S(1)} %get-tuple-element.41), channel_id=1, source_target_pairs={{0,16},{16,32},{32,48},{48,0},{1,17},{17,33},{33,49},{49,1},{2,18}... | collective-permute-start | bytes 196616 | tf_op jit(solution)/shard_map/ppermute | solution.py:354
  3.8 3.1 %collective-permute-start.1 = (bf16[32,1024]{1,0:T(8,128)(2,1)S(1)}, bf16[32,1024]{1,0:T(8,128)(2,1)S(1)}, u32[]{:S(2)}, u32[]{:S(2)}) collective-permute-start(bf16[32,1024]{1,0:T(8,128)(2,1)S(1)} %get-tuple-element.42), channel_id=1, source_target_pairs={{0,48},{16,0},{32,16},{48,32},{1,49},{17,1},{33,17},{49,33},{2,50}... | collective-permute-start | bytes 196616 | tf_op jit(solution)/shard_map/ppermute | solution.py:354
  5.3 4.6 %collective-permute-start.2 = (bf16[32,1024]{1,0:T(8,128)(2,1)S(1)}, bf16[32,1024]{1,0:T(8,128)(2,1)S(1)}, u32[]{:S(2)}, u32[]{:S(2)}) collective-permute-start(bf16[32,1024]{1,0:T(8,128)(2,1)S(1)} %get-tuple-element.43), channel_id=1, source_target_pairs={{0,32},{16,48},{32,0},{48,16},{1,33},{17,49},{33,1},{49,17},{2,34}... | collective-permute-start | bytes 196616 | tf_op jit(solution)/shard_map/ppermute | solution.py:354
  9.9 26.6 %collective-permute-start.9 = (bf16[8,32,2048]{2,1,0:T(8,128)(2,1)}, bf16[8,32,2048]{2,1,0:T(8,128)(2,1)S(1)}, u32[]{:S(2)}, u32[]{:S(2)}) collective-permute-start(bf16[8,32,2048]{2,1,0:T(8,128)(2,1)} %bitcast.12), channel_id=1, source_target_pairs={{0,16},{16,32},{32,48},{48,0},{1,17},{17,33},{33,49},{49,1},{2,18}... | collective-permute-start | bytes 3145736 | tf_op jit(solution)/shard_map/ppermute | solution.py:356
  10.3 26.1 %collective-permute-start.10 = (bf16[8,32,2048]{2,1,0:T(8,128)(2,1)}, bf16[8,32,2048]{2,1,0:T(8,128)(2,1)S(1)}, u32[]{:S(2)}, u32[]{:S(2)}) collective-permute-start(bf16[8,32,2048]{2,1,0:T(8,128)(2,1)} %bitcast.13), channel_id=1, source_target_pairs={{0,48},{16,0},{32,16},{48,32},{1,49},{17,1},{33,17},{49,33},{2,50}... | collective-permute-start | bytes 3145736 | tf_op jit(solution)/shard_map/ppermute | solution.py:356
  12.7 33.1 %copy-start.5 = (bf16[256,2048]{1,0:T(8,128)(2,1)S(1)}, bf16[256,2048]{1,0:T(8,128)(2,1)}, u32[]{:S(2)}) copy-start(bf16[256,2048]{1,0:T(8,128)(2,1)} %param.10) | copy-start | bytes 3145732
  12.7 6.2 %collective-permute-start.3 = (bf16[1024,128]{1,0:T(8,128)(2,1)S(1)}, bf16[1024,128]{1,0:T(8,128)(2,1)S(1)}, u32[]{:S(2)}, u32[]{:S(2)}) collective-permute-start(bf16[1024,128]{1,0:T(8,128)(2,1)S(1)} %turn.1.refs_0_), channel_id=1, source_target_pairs={{0,1},{1,2},{2,3},{3,4},{4,5},{5,6},{6,7},{7,0},{8,9},{9,10},{10,1... | collective-permute-start | bytes 786440 | tf_op jit(solution)/shard_map/ppermute | solution.py:358
  15.7 6.7 %collective-permute-start.4 = (bf16[1024,128]{1,0:T(8,128)(2,1)S(1)}, bf16[1024,128]{1,0:T(8,128)(2,1)S(1)}, u32[]{:S(2)}, u32[]{:S(2)}) collective-permute-start(bf16[1024,128]{1,0:T(8,128)(2,1)S(1)} %turn.1.refs_0_), channel_id=1, source_target_pairs={{0,7},{1,0},{2,1},{3,2},{4,3},{5,4},{6,5},{7,6},{8,15},{9,8},{10,9... | collective-permute-start | bytes 786440 | tf_op jit(solution)/shard_map/ppermute | solution.py:358
  19.0 6.7 %collective-permute-start.5 = (bf16[1024,128]{1,0:T(8,128)(2,1)S(1)}, bf16[1024,128]{1,0:T(8,128)(2,1)S(1)}, u32[]{:S(2)}, u32[]{:S(2)}) collective-permute-start(bf16[1024,128]{1,0:T(8,128)(2,1)S(1)} %collective-permute-done.3.refs_1_), channel_id=1, source_target_pairs={{0,1},{1,2},{2,3},{3,4},{4,5},{5,6},{6,7},{7,0},{8,9},{9,10},{10,1... | collective-permute-start | bytes 786440 | tf_op jit(solution)/shard_map/ppermute | solution.py:360
  22.4 6.7 %collective-permute-start.6 = (bf16[1024,128]{1,0:T(8,128)(2,1)S(1)}, bf16[1024,128]{1,0:T(8,128)(2,1)S(1)}, u32[]{:S(2)}, u32[]{:S(2)}) collective-permute-start(bf16[1024,128]{1,0:T(8,128)(2,1)S(1)} %collective-permute-done.4.refs_2_), channel_id=1, source_target_pairs={{0,7},{1,0},{2,1},{3,2},{4,3},{5,4},{6,5},{7,6},{8,15},{9,8},{10,9... | collective-permute-start | bytes 786440 | tf_op jit(solution)/shard_map/ppermute | solution.py:360
  25.7 7.1 %collective-permute-start.7 = (bf16[1024,128]{1,0:T(8,128)(2,1)S(1)}, bf16[1024,128]{1,0:T(8,128)(2,1)S(1)}, u32[]{:S(2)}, u32[]{:S(2)}) collective-permute-start(bf16[1024,128]{1,0:T(8,128)(2,1)S(1)} %collective-permute-done.5.refs_3_), channel_id=1, source_target_pairs={{0,1},{1,2},{2,3},{3,4},{4,5},{5,6},{6,7},{7,0},{8,9},{9,10},{10,1... | collective-permute-start | bytes 786440 | tf_op jit(solution)/shard_map/ppermute | solution.py:362
  29.1 7.3 %collective-permute-start.8 = (bf16[1024,128]{1,0:T(8,128)(2,1)S(1)}, bf16[1024,128]{1,0:T(8,128)(2,1)S(1)}, u32[]{:S(2)}, u32[]{:S(2)}) collective-permute-start(bf16[1024,128]{1,0:T(8,128)(2,1)S(1)} %collective-permute-done.6.refs_4_), channel_id=1, source_target_pairs={{0,7},{1,0},{2,1},{3,2},{4,3},{5,4},{6,5},{7,6},{8,15},{9,8},{10,9... | collective-permute-start | bytes 786440 | tf_op jit(solution)/shard_map/ppermute | solution.py:362
  36.5 9.3 %collective-permute-start.13 = (bf16[8,32,1024]{2,1,0:T(8,128)(2,1)S(1)}, bf16[8,32,1024]{2,1,0:T(8,128)(2,1)S(1)}, u32[]{:S(2)}, u32[]{:S(2)}) collective-permute-start(bf16[8,32,1024]{2,1,0:T(8,128)(2,1)S(1)} %slice.14), channel_id=1, source_target_pairs={{0,16},{16,32},{32,48},{48,0},{1,17},{17,33},{33,49},{49,1},{2,18}... | collective-permute-start | bytes 1572872 | tf_op jit(solution)/shard_map/ppermute | solution.py:367
  36.7 20.3 %collective-permute-start.18 = (bf16[8,32,1024]{2,1,0:T(8,128)(2,1)S(1)}, bf16[8,32,1024]{2,1,0:T(8,128)(2,1)S(1)}, u32[]{:S(2)}, u32[]{:S(2)}) collective-permute-start(bf16[8,32,1024]{2,1,0:T(8,128)(2,1)S(1)} %slice.15), channel_id=1, source_target_pairs={{0,48},{16,0},{32,16},{48,32},{1,49},{17,1},{33,17},{49,33},{2,50}... | collective-permute-start | bytes 1572872 | tf_op jit(solution)/shard_map/ppermute | solution.py:368
  39.4 3.9 %collective-permute-start.11 = (bf16[512,128]{1,0:T(8,128)(2,1)S(1)}, bf16[512,128]{1,0:T(8,128)(2,1)S(1)}, u32[]{:S(2)}, u32[]{:S(2)}) collective-permute-start(bf16[512,128]{1,0:T(8,128)(2,1)S(1)} %slice.12), channel_id=1, source_target_pairs={{0,1},{1,2},{2,3},{3,4},{4,5},{5,6},{6,7},{7,0},{8,9},{9,10},{10,1... | collective-permute-start | bytes 393224 | tf_op jit(solution)/shard_map/ppermute | solution.py:371
  39.5 5.3 %collective-permute-start.12 = (bf16[512,128]{1,0:T(8,128)(2,1)S(1)}, bf16[512,128]{1,0:T(8,128)(2,1)S(1)}, u32[]{:S(2)}, u32[]{:S(2)}) collective-permute-start(bf16[512,128]{1,0:T(8,128)(2,1)S(1)} %slice.13), channel_id=1, source_target_pairs={{0,7},{1,0},{2,1},{3,2},{4,3},{5,4},{6,5},{7,6},{8,15},{9,8},{10,9... | collective-permute-start | bytes 393224 | tf_op jit(solution)/shard_map/ppermute | solution.py:372
  50.0 11.2 %collective-permute-start.14 = (bf16[4,64,16,128]{3,2,1,0:T(8,128)(2,1)S(1)}, bf16[4,64,16,128]{3,2,1,0:T(8,128)(2,1)S(1)}, u32[]{:S(2)}, u32[]{:S(2)}) collective-permute-start(bf16[4,64,16,128]{3,2,1,0:T(8,128)(2,1)S(1)} %get-tuple-element.54), channel_id=1, source_target_pairs={{0,8},{8,0},{1,9},{9,1},{2,10},{10,2},{3,11},{11,3},{4,12},{12,4},... | collective-permute-start | bytes 3145736 | tf_op jit(solution)/shard_map/ppermute | solution.py:378
  61.1 6.0 %collective-permute-start.19 = (bf16[4,64,16,128]{3,2,1,0:T(8,128)(2,1)S(1)}, bf16[4,64,16,128]{3,2,1,0:T(8,128)(2,1)S(1)}, u32[]{:S(2)}, u32[]{:S(2)}) collective-permute-start(bf16[4,64,16,128]{3,2,1,0:T(8,128)(2,1)S(1)} %get-tuple-element.62), channel_id=1, source_target_pairs={{0,8},{8,0},{1,9},{9,1},{2,10},{10,2},{3,11},{11,3},{4,12},{12,4},... | collective-permute-start | bytes 3145736 | tf_op jit(solution)/shard_map/ppermute | solution.py:378
  62.1 10.1 %copy-start.6 = (s32[1,128]{1,0:T(1,128)S(1)}, s32[1,128]{1,0:T(1,128)}, u32[]{:S(2)}) copy-start(s32[1,128]{1,0:T(1,128)} %param.11) | copy-start | bytes 1540
  62.1 8.7 %collective-permute-start.15 = (bf16[64,16,128]{2,1,0:T(8,128)(2,1)S(1)}, bf16[64,16,128]{2,1,0:T(8,128)(2,1)S(1)}, u32[]{:S(2)}, u32[]{:S(2)}) collective-permute-start(bf16[64,16,128]{2,1,0:T(8,128)(2,1)S(1)} %get-tuple-element.58), channel_id=1, source_target_pairs={{0,64},{64,128},{128,192},{192,0},{1,65},{65,129},{129,193},{193,1... | collective-permute-start | bytes 786440 | tf_op jit(solution)/shard_map/ppermute | solution.py:381
  63.4 14.2 %collective-permute-start.16 = (bf16[64,16,128]{2,1,0:T(8,128)(2,1)}, bf16[64,16,128]{2,1,0:T(8,128)(2,1)S(1)}, u32[]{:S(2)}, u32[]{:S(2)}) collective-permute-start(bf16[64,16,128]{2,1,0:T(8,128)(2,1)} %get-tuple-element.59), channel_id=1, source_target_pairs={{0,128},{64,192},{128,0},{192,64},{1,129},{65,193},{129,1},{193,65... | collective-permute-start | bytes 786440 | tf_op jit(solution)/shard_map/ppermute | solution.py:381
  66.0 11.6 %collective-permute-start.17 = (bf16[64,16,128]{2,1,0:T(8,128)(2,1)}, bf16[64,16,128]{2,1,0:T(8,128)(2,1)}, u32[]{:S(2)}, u32[]{:S(2)}) collective-permute-start(bf16[64,16,128]{2,1,0:T(8,128)(2,1)} %get-tuple-element.60), channel_id=1, source_target_pairs={{0,192},{64,0},{128,64},{192,128},{1,193},{65,1},{129,65},{193,129... | collective-permute-start | bytes 786440 | tf_op jit(solution)/shard_map/ppermute | solution.py:381
  68.1 14.3 %collective-permute-start.20 = (bf16[64,16,128]{2,1,0:T(8,128)(2,1)}, bf16[64,16,128]{2,1,0:T(8,128)(2,1)S(1)}, u32[]{:S(2)}, u32[]{:S(2)}) collective-permute-start(bf16[64,16,128]{2,1,0:T(8,128)(2,1)} %get-tuple-element.66), channel_id=1, source_target_pairs={{0,64},{64,128},{128,192},{192,0},{1,65},{65,129},{129,193},{193,1... | collective-permute-start | bytes 786440 | tf_op jit(solution)/shard_map/ppermute | solution.py:381
  68.5 20.5 %collective-permute-start.21 = (bf16[64,16,128]{2,1,0:T(8,128)(2,1)}, bf16[64,16,128]{2,1,0:T(8,128)(2,1)}, u32[]{:S(2)}, u32[]{:S(2)}) collective-permute-start(bf16[64,16,128]{2,1,0:T(8,128)(2,1)} %get-tuple-element.67), channel_id=1, source_target_pairs={{0,128},{64,192},{128,0},{192,64},{1,129},{65,193},{129,1},{193,65... | collective-permute-start | bytes 786440 | tf_op jit(solution)/shard_map/ppermute | solution.py:381
  70.8 18.1 %collective-permute-start.22 = (bf16[64,16,128]{2,1,0:T(8,128)(2,1)}, bf16[64,16,128]{2,1,0:T(8,128)(2,1)}, u32[]{:S(2)}, u32[]{:S(2)}) collective-permute-start(bf16[64,16,128]{2,1,0:T(8,128)(2,1)} %get-tuple-element.68), channel_id=1, source_target_pairs={{0,192},{64,0},{128,64},{192,128},{1,193},{65,1},{129,65},{193,129... | collective-permute-start | bytes 786440 | tf_op jit(solution)/shard_map/ppermute | solution.py:381
  91.2 18.5 %all-to-all-start = ((bf16[32,5,16,128]{3,2,1,0:T(8,128)(2,1)}), bf16[32,5,16,128]{3,2,1,0:T(8,128)(2,1)S(1)}, u32[]{:S(2)}, u32[]{:S(2)}) async-start(bf16[32,5,16,128]{3,2,1,0:T(8,128)(2,1)} %bitcast.6), calls=%async_computation | async-start | bytes 1310720 | tf_op jit(solution)/shard_map/all_to_all | solution.py:342
  114.8 18.1 %copy-start.2 = (bf16[5,256,256]{2,1,0:T(8,128)(2,1)}, bf16[5,256,256]{2,1,0:T(8,128)(2,1)S(1)}, u32[]{:S(2)}) copy-start(bf16[5,256,256]{2,1,0:T(8,128)(2,1)S(1)} %get-tuple-element.70.grads) | copy-start | bytes 1966084
  114.8 22.2 %copy-start.1 = (f32[1,5,256,256]{3,2,1,0:T(8,128)S(1)}, f32[1,5,256,256]{3,2,1,0:T(8,128)}, u32[]{:S(2)}) copy-start(f32[1,5,256,256]{3,2,1,0:T(8,128)} %right.1) | copy-start | bytes 3932164
  131.4 5.6 %copy-start = (f32[1,5,256,256]{3,2,1,0:T(8,128)S(1)}, f32[1,5,256,256]{3,2,1,0:T(8,128)}, u32[]{:S(2)}) copy-start(f32[1,5,256,256]{3,2,1,0:T(8,128)} %left.1) | copy-start | bytes 3932164
  132.9 15.8 %all-to-all-start.2 = ((bf16[32,4,16,128]{3,2,1,0:T(8,128)(2,1)}), bf16[32,4,16,128]{3,2,1,0:T(8,128)(2,1)S(1)}, u32[]{:S(2)}, u32[]{:S(2)}) async-start(bf16[32,4,16,128]{3,2,1,0:T(8,128)(2,1)} %bitcast.8), calls=%async_computation.2 | async-start | bytes 1048576 | tf_op jit(solution)/shard_map/all_to_all | solution.py:342
  137.0 1.1 copy-start.3

commit v8 on v7

--- a/solution.py
+++ b/solution.py
@@ -301,7 +301,7 @@
             like(first),
             like(second),
         ],
-        compiler_params=params(52),
+        compiler_params=params(48),
         name="update",
     )(live, tiles, basis_left, basis_right, first, second)
 
@@ -395,6 +395,7 @@
     slot = owner_row * SLOTS + rank
     held = jnp.sum((owner_row == lax.axis_index(DP)).astype(jnp.int32))
     live = (jnp.arange(SLOTS, dtype=jnp.int32) < held).astype(jnp.int32)
+    slot, live = lax.optimization_barrier((slot, live))
 
     spot = jnp.stack([lax.axis_index(axis) for axis in (*DP, "z")]).astype(jnp.int32)
     grads = grad_out.reshape(N_TENSOR, TOK_SUB, grad_out.shape[1])

time: 150 us -> 150 us (level)
  blocking collectives: 16.6 us -> 35 us
  waiting for transfers between devices: 57.1 us -> 45 us
  starting transfers between devices: 45.6 us -> 40.1 us
  Pallas kernels: 25.7 us -> 22.1 us
  local copies, waits for them, and re-layouts: 2.15 us -> 4.53 us
    all_to_all x1 -> x2, blocking collectives: 16.6 us -> 35 us  [spread(): return lax.all_to_all(array, axes, split_axis=0, concat_axis=0, tiled=True)]
    all_to_all x2 -> x1, waiting for transfers between devices: 19.1 us -> 6.84 us  [spread(): return lax.all_to_all(array, axes, split_axis=0, concat_axis=0, tiled=True)]
    all_to_all x2 -> x1, starting transfers between devices: 9.62 us -> 4.09 us  [spread(): return lax.all_to_all(array, axes, split_axis=0, concat_axis=0, tiled=True)]
    unnamed x14 -> x30, local copies, waits for them, and re-layouts: 2.06 us -> 4.43 us
  transfers between devices with their start and end apart: 25 -> 24, of which waited for: 15 -> 15; matrix products, arithmetic and copies ran while one was open for 1% -> 1% of each run, Pallas kernels for 10% -> 9%
where the time goes in v8:
time: 150 us; the launch traced here: 149 us
  waiting for transfers between devices  45 us (30%)
  starting transfers between devices  40.1 us (27%)
  blocking collectives  35 us (23%)
  Pallas kernels  22.1 us (15%)
  local copies, waits for them, and re-layouts  4.53 us (3%)
  other arithmetic  1.52 us (1%)
    all_to_all x2, blocking collectives, spread(): return lax.all_to_all(array, axes, split_axis=0, concat_axis=0, tiled=True)  35 us
    ppermute x6, waiting for transfers between devices, sum_parts(): lax.ppermute(a, 'y', ring(Y, step))  16.5 us
    pallas_call x2, Pallas kernels, gradient_tiles(): pl.pallas_call(gradient_kernel, grid_spec=pltpu.PrefetchScalarGridSpec(nu...  8.94 us
    ppermute x6, starting transfers between devices, sum_parts(): lax.ppermute(a, 'y', ring(Y, step))  7.73 us
    ppermute x2, starting transfers between devices, sum_parts(): mine, other = (parts[:Y], lax.ppermute(parts[Y], 'core', ring(CORE, 1)))  6.99 us
    ppermute x2, waiting for transfers between devices, gather_row(): lax.ppermute(below, 'z', up)  6.96 us
    all_to_all x1, waiting for transfers between devices, spread(): return lax.all_to_all(array, axes, split_axis=0, concat_axis=0, tiled=True)  6.84 us
    ppermute x2, starting transfers between devices, gather_row(): lax.ppermute(below, 'z', up)  6.82 us
  transfers between devices with their start and end apart: 24, of which 15 were waited for; matrix products, arithmetic and copies ran while one was open for 1% of the time, Pallas kernels for 9%

profile of v8, /device:TPU:97, one launch (start us, length us, event | category | flops | bytes accessed | tf_op | source)
XLA Modules:
  0.0 149.1 jit_solution(9627481620142162640)
XLA Ops:
  0.6 0.1 pad_add_fusion.spot
  0.7 0.9 copy-done.10
  1.7 0.9 cut_tokens.1
  2.5 1.3 collective-permute-start
  3.8 1.5 collective-permute-start.1
  5.3 1.5 %collective-permute-start.2 = (bf16[32,1024]{1,0:T(8,128)(2,1)S(1)}, bf16[32,1024]{1,0:T(8,128)(2,1)S(1)}, u32[]{:S(2)}, u32[]{:S(2)}) collective-permute-start(bf16[32,1024]{1,0:T(8,128)(2,1)S(1)} %get-tuple-element.47), channel_id=1, source_target_pairs={{0,32},{16,48},{32,0},{48,16},{1,33},{17,49},{33,1},{49,17},{2,34}... | collective-permute-start | bytes 196616 | tf_op jit(solution)/shard_map/ppermute | solution.py:354
  6.8 0.1 collective-permute-done.refs_1_
  6.9 3.0 %collective-permute-done.2.refs_3_ = bf16[32,1024]{1,0:T(8,128)(2,1)S(1)} collective-permute-done((bf16[32,1024]{1,0:T(8,128)(2,1)S(1)}, bf16[32,1024]{1,0:T(8,128)(2,1)S(1)}, u32[]{:S(2)}, u32[]{:S(2)}) %collective-permute-start.2) | collective-permute-done | bytes 65568 | tf_op jit(solution)/shard_map/ppermute | solution.py:354
  9.9 0.4 collective-permute-start.9
  10.3 2.3 %collective-permute-start.10 = (bf16[8,32,2048]{2,1,0:T(8,128)(2,1)}, bf16[8,32,2048]{2,1,0:T(8,128)(2,1)S(1)}, u32[]{:S(2)}, u32[]{:S(2)}) collective-permute-start(bf16[8,32,2048]{2,1,0:T(8,128)(2,1)} %bitcast.14), channel_id=1, source_target_pairs={{0,48},{16,0},{32,16},{48,32},{1,49},{17,1},{33,17},{49,33},{2,50}... | collective-permute-start | bytes 3145736 | tf_op jit(solution)/shard_map/ppermute | solution.py:356
  12.6 0.1 turn.1.refs_0_
  12.7 0.0 copy-start.11
  12.7 2.9 %collective-permute-start.3 = (bf16[1024,128]{1,0:T(8,128)(2,1)S(1)}, bf16[1024,128]{1,0:T(8,128)(2,1)S(1)}, u32[]{:S(2)}, u32[]{:S(2)}) collective-permute-start(bf16[1024,128]{1,0:T(8,128)(2,1)S(1)} %turn.1.refs_0_), channel_id=1, source_target_pairs={{0,1},{1,2},{2,3},{3,4},{4,5},{5,6},{6,7},{7,0},{8,9},{9,10},{10,1... | collective-permute-start | bytes 786440 | tf_op jit(solution)/shard_map/ppermute | solution.py:358
  15.7 3.3 %collective-permute-done.3.refs_1_ = bf16[1024,128]{1,0:T(8,128)(2,1)S(1)} collective-permute-done((bf16[1024,128]{1,0:T(8,128)(2,1)S(1)}, bf16[1024,128]{1,0:T(8,128)(2,1)S(1)}, u32[]{:S(2)}, u32[]{:S(2)}) %collective-permute-start.3) | collective-permute-done | bytes 262176 | tf_op jit(solution)/shard_map/ppermute | solution.py:358
  19.0 3.4 %collective-permute-start.5 = (bf16[1024,128]{1,0:T(8,128)(2,1)S(1)}, bf16[1024,128]{1,0:T(8,128)(2,1)S(1)}, u32[]{:S(2)}, u32[]{:S(2)}) collective-permute-start(bf16[1024,128]{1,0:T(8,128)(2,1)S(1)} %collective-permute-done.3.refs_1_), channel_id=1, source_target_pairs={{0,1},{1,2},{2,3},{3,4},{4,5},{5,6},{6,7},{7,0},{8,9},{9,10},{10,1... | collective-permute-start | bytes 786440 | tf_op jit(solution)/shard_map/ppermute | solution.py:360
  22.4 3.3 %collective-permute-done.5.refs_3_ = bf16[1024,128]{1,0:T(8,128)(2,1)S(1)} collective-permute-done((bf16[1024,128]{1,0:T(8,128)(2,1)S(1)}, bf16[1024,128]{1,0:T(8,128)(2,1)S(1)}, u32[]{:S(2)}, u32[]{:S(2)}) %collective-permute-start.5) | collective-permute-done | bytes 262176 | tf_op jit(solution)/shard_map/ppermute | solution.py:360
  25.7 3.4 %collective-permute-start.7 = (bf16[1024,128]{1,0:T(8,128)(2,1)S(1)}, bf16[1024,128]{1,0:T(8,128)(2,1)S(1)}, u32[]{:S(2)}, u32[]{:S(2)}) collective-permute-start(bf16[1024,128]{1,0:T(8,128)(2,1)S(1)} %collective-permute-done.5.refs_3_), channel_id=1, source_target_pairs={{0,1},{1,2},{2,3},{3,4},{4,5},{5,6},{6,7},{7,0},{8,9},{9,10},{10,1... | collective-permute-start | bytes 786440 | tf_op jit(solution)/shard_map/ppermute | solution.py:362
  29.1 0.0 collective-permute-done.6.refs_4_
  29.1 3.6 %collective-permute-done.7.refs_5_ = bf16[1024,128]{1,0:T(8,128)(2,1)S(1)} collective-permute-done((bf16[1024,128]{1,0:T(8,128)(2,1)S(1)}, bf16[1024,128]{1,0:T(8,128)(2,1)S(1)}, u32[]{:S(2)}, u32[]{:S(2)}) %collective-permute-start.7) | collective-permute-done | bytes 262176 | tf_op jit(solution)/shard_map/ppermute | solution.py:362
  32.8 3.7 %collective-permute-done.8.refs_6_ = bf16[1024,128]{1,0:T(8,128)(2,1)S(1)} collective-permute-done((bf16[1024,128]{1,0:T(8,128)(2,1)S(1)}, bf16[1024,128]{1,0:T(8,128)(2,1)S(1)}, u32[]{:S(2)}, u32[]{:S(2)}) %collective-permute-start.8) | collective-permute-done | bytes 262176 | tf_op jit(solution)/shard_map/ppermute | solution.py:362
  36.5 0.1 collective-permute-start.13
  36.6 2.7 %collective-permute-start.18 = (bf16[8,32,1024]{2,1,0:T(8,128)(2,1)S(1)}, bf16[8,32,1024]{2,1,0:T(8,128)(2,1)S(1)}, u32[]{:S(2)}, u32[]{:S(2)}) collective-permute-start(bf16[8,32,1024]{2,1,0:T(8,128)(2,1)S(1)} %slice.15), channel_id=1, source_target_pairs={{0,48},{16,0},{32,16},{48,32},{1,49},{17,1},{33,17},{49,33},{2,50}... | collective-permute-start | bytes 1572872 | tf_op jit(solution)/shard_map/ppermute | solution.py:368
  39.4 0.1 collective-permute-start.11
  39.5 1.7 %collective-permute-start.12 = (bf16[512,128]{1,0:T(8,128)(2,1)S(1)}, bf16[512,128]{1,0:T(8,128)(2,1)S(1)}, u32[]{:S(2)}, u32[]{:S(2)}) collective-permute-start(bf16[512,128]{1,0:T(8,128)(2,1)S(1)} %slice.13), channel_id=1, source_target_pairs={{0,7},{1,0},{2,1},{3,2},{4,3},{5,4},{6,5},{7,6},{8,15},{9,8},{10,9... | collective-permute-start | bytes 393224 | tf_op jit(solution)/shard_map/ppermute | solution.py:372
  41.2 2.1 %collective-permute-done.11.refs_7_ = bf16[512,128]{1,0:T(8,128)(2,1)S(1)} collective-permute-done((bf16[512,128]{1,0:T(8,128)(2,1)S(1)}, bf16[512,128]{1,0:T(8,128)(2,1)S(1)}, u32[]{:S(2)}, u32[]{:S(2)}) %collective-permute-start.11) | collective-permute-done | bytes 131104 | tf_op jit(solution)/shard_map/ppermute | solution.py:371
  43.3 1.5 %collective-permute-done.12.refs_8_ = bf16[512,128]{1,0:T(8,128)(2,1)S(1)} collective-permute-done((bf16[512,128]{1,0:T(8,128)(2,1)S(1)}, bf16[512,128]{1,0:T(8,128)(2,1)S(1)}, u32[]{:S(2)}, u32[]{:S(2)}) %collective-permute-start.12) | collective-permute-done | bytes 131104 | tf_op jit(solution)/shard_map/ppermute | solution.py:372
  44.8 1.0 collective-permute-done.13.refs_12_
  45.8 4.1 %gradient_tiles.2 = (bf16[64,16,128]{2,1,0:T(8,128)(2,1)S(1)}, bf16[64,16,128]{2,1,0:T(8,128)(2,1)S(1)}, bf16[64,16,128]{2,1,0:T(8,128)(2,1)S(1)}, bf16[64,16,12...) custom-call(s32[4]{0:T(128)S(1)} %pad_add_fusion.spot, bf16[1024,128]{1,0:T(8,128)(2,1)S(1)} %turn.1.refs_0_, ...), custom_call_target="tpu_custom_call" | custom-call | flops 2147483648 | bytes 8388608 | tf_op jit(solution)/shard_map/gradient_tiles/pallas_call | solution.py:140
  50.0 7.0 %collective-permute-start.14 = (bf16[4,64,16,128]{3,2,1,0:T(8,128)(2,1)S(1)}, bf16[4,64,16,128]{3,2,1,0:T(8,128)(2,1)S(1)}, u32[]{:S(2)}, u32[]{:S(2)}) collective-permute-start(bf16[4,64,16,128]{3,2,1,0:T(8,128)(2,1)S(1)} %get-tuple-element.58), channel_id=1, source_target_pairs={{0,8},{8,0},{1,9},{9,1},{2,10},{10,2},{3,11},{11,3},{4,12},{12,4},... | collective-permute-start | bytes 3145736 | tf_op jit(solution)/shard_map/ppermute | solution.py:378
  56.9 4.8 %gradient_tiles.3 = (bf16[64,16,128]{2,1,0:T(8,128)(2,1)S(1)}, bf16[64,16,128]{2,1,0:T(8,128)(2,1)S(1)}, bf16[64,16,128]{2,1,0:T(8,128)(2,1)S(1)}, bf16[64,16,12...) custom-call(s32[4]{0:T(128)S(1)} %pad_add_fusion.spot, bf16[1024,128]{1,0:T(8,128)(2,1)S(1)} %turn.1.refs_0_, ...), custom_call_target="tpu_custom_call" | custom-call | flops 2147483648 | bytes 8388608 | tf_op jit(solution)/shard_map/gradient_tiles/pallas_call | solution.py:140
  61.7 0.0 collective-permute-start.19
  61.8 0.8 add_cores.2
  62.6 0.7 copy-done.12
  63.3 0.7 copy-done.13
  64.0 1.3 collective-permute-start.15
  65.3 0.2 convert_reduce_fusion
  65.5 2.7 %collective-permute-start.16 = (bf16[64,16,128]{2,1,0:T(8,128)(2,1)}, bf16[64,16,128]{2,1,0:T(8,128)(2,1)S(1)}, u32[]{:S(2)}, u32[]{:S(2)}) collective-permute-start(bf16[64,16,128]{2,1,0:T(8,128)(2,1)} %copy-done.13), channel_id=1, source_target_pairs={{0,128},{64,192},{128,0},{192,64},{1,129},{65,193},{129,1},{193,65... | collective-permute-start | bytes 786440 | tf_op jit(solution)/shard_map/ppermute | solution.py:381
  68.2 1.1 collective-permute-start.17
  69.3 0.9 copy-done.9
  70.2 0.2 add_cores.3
  70.4 0.5 collective-permute-start.20
  70.9 0.8 collective-permute-start.21
  71.7 1.3 collective-permute-done.15.one
  73.0 1.4 collective-permute-start.22
  74.4 0.6 fusion.1
  75.0 0.6 compare_convert_fusion.live
  75.6 4.1 %collective-permute-done.16.two = bf16[64,16,128]{2,1,0:T(8,128)(2,1)S(1)} collective-permute-done((bf16[64,16,128]{2,1,0:T(8,128)(2,1)}, bf16[64,16,128]{2,1,0:T(8,128)(2,1)S(1)}, u32[]{:S(2)}, u32[]{:S(2)}) %collective-permute-start.16) | collective-permute-done | bytes 262176 | tf_op jit(solution)/shard_map/ppermute | solution.py:381
  79.7 0.1 collective-permute-done.17.three
  79.8 0.2 sum_chunk.1.summed
  80.0 4.6 %collective-permute-done.20.one = bf16[64,16,128]{2,1,0:T(8,128)(2,1)S(1)} collective-permute-done((bf16[64,16,128]{2,1,0:T(8,128)(2,1)S(1)}, bf16[64,16,128]{2,1,0:T(8,128)(2,1)S(1)}, u32[]{:S(2)}, u32[]{:S(2)}) %collective-permute-start.20) | collective-permute-done | bytes 262176 | tf_op jit(solution)/shard_map/ppermute | solution.py:381
  84.5 6.4 %collective-permute-done.21.two = bf16[64,16,128]{2,1,0:T(8,128)(2,1)S(1)} collective-permute-done((bf16[64,16,128]{2,1,0:T(8,128)(2,1)S(1)}, bf16[64,16,128]{2,1,0:T(8,128)(2,1)S(1)}, u32[]{:S(2)}, u32[]{:S(2)}) %collective-permute-start.21) | collective-permute-done | bytes 262176 | tf_op jit(solution)/shard_map/ppermute | solution.py:381
  91.0 0.9 to_slots.1
  91.9 0.0 copy-start.2
  91.9 0.0 copy-start.3
  91.9 18.4 %all_to_all.15.tiles = bf16[32,5,16,128]{3,2,1,0:T(8,128)(2,1)S(1)} all-to-all(bf16[32,5,16,128]{3,2,1,0:T(8,128)(2,1)S(1)} %bitcast.12), channel_id=1, replica_groups=mesh['y'=4,'x'=4,'core'=2,'z'=8] {'y','x','core'}, dimensions={0} | all-to-all | bytes 1310720 | tf_op jit(solution)/shard_map/all_to_all | solution.py:342
  110.4 4.0 %update.1 = (bf16[32,5,16,128]{3,2,1,0:T(8,128)(2,1)S(1)}, bf16[5,256,256]{2,1,0:T(8,128)(2,1)S(1)}, bf16[1,5,256,256]{3,2,1,0:T(8,128)(2,1)}, bf16[1,5,256,256]{3,2,1,0:T(8,128)(2,1)}) custom-call(s32[5]{0:T(128)S(1)} %compare_convert_fusion.live, bf16[32,5,16,128]{3,2,1,0:T(8,128)(2,1)S(1)} %all_to_all.15.tiles, bf16[1,5,256,256]{3,2,1,0:T(8,128)(2,1)S(1)} %copy-done.2, ...), custom_call_target="tpu_custom_call" | custom-call | tf_op jit(solution)/shard_map/update/pallas_call | solution.py:295
  114.4 16.6 %all_to_all.16 = bf16[32,5,16,128]{3,2,1,0:T(8,128)(2,1)S(1)} all-to-all(bf16[32,5,16,128]{3,2,1,0:T(8,128)(2,1)S(1)} %get-tuple-element.73), channel_id=1, replica_groups=mesh['y'=4,'x'=4,'core'=2,'z'=8] {'y','x','core'}, dimensions={0} | all-to-all | bytes 1310720 | tf_op jit(solution)/shard_map/all_to_all | solution.py:342
  131.0 1.5 from_slots.1
  132.5 4.1 %all-to-all-start.2 = ((bf16[32,4,16,128]{3,2,1,0:T(8,128)(2,1)}), bf16[32,4,16,128]{3,2,1,0:T(8,128)(2,1)S(1)}, u32[]{:S(2)}, u32[]{:S(2)}) async-start(bf16[32,4,16,128]{3,2,1,0:T(8,128)(2,1)} %bitcast.8), calls=%async_computation.2 | async-start | bytes 1048576 | tf_op jit(solution)/shard_map/all_to_all | solution.py:342
  136.6 0.0 copy-start.7
  136.6 1.1 copy-done.7
  137.7 3.7 %factors.1 = (f32[1,5,256,256]{3,2,1,0:T(8,128)}, f32[1,5,256,256]{3,2,1,0:T(8,128)}) custom-call(s32[5]{0:T(128)S(1)} %compare_convert_fusion.live, bf16[5,256,256]{2,1,0:T(8,128)(2,1)S(1)} %copy-done.7, f32[1,5,256,256]{3,2,1,0:T(8,128)S(1)} %copy-done, f32[1,5,256,256]{3,2,1,0:T(8,128)S(1)} %copy-done.1), custom_call_target="tpu_custom_call" | custom-call | flops 335544320 | bytes 6291456 | tf_op jit(solution)/shard_map/factors/pallas_call | solution.py:324
  141.4 6.8 %all-to-all-done.2.tiles = bf16[32,4,16,128]{3,2,1,0:T(8,128)(2,1)S(1)} async-done(((bf16[32,4,16,128]{3,2,1,0:T(8,128)(2,1)}), bf16[32,4,16,128]{3,2,1,0:T(8,128)(2,1)S(1)}, u32[]{:S(2)}, u32[]{:S(2)}) %all-to-all-start.2) | async-done | bytes 524320 | tf_op jit(solution)/shard_map/all_to_all | solution.py:342
  148.2 0.9 assemble.1
  (36 shorter events, 0.2 us)
Async XLA Ops:
  0.7 1.0 copy-start.10
  2.5 4.4 %collective-permute-start = (bf16[32,1024]{1,0:T(8,128)(2,1)S(1)}, bf16[32,1024]{1,0:T(8,128)(2,1)S(1)}, u32[]{:S(2)}, u32[]{:S(2)}) collective-permute-start(bf16[32,1024]{1,0:T(8,128)(2,1)S(1)} %get-tuple-element.45), channel_id=1, source_target_pairs={{0,16},{16,32},{32,48},{48,0},{1,17},{17,33},{33,49},{49,1},{2,18}... | collective-permute-start | bytes 196616 | tf_op jit(solution)/shard_map/ppermute | solution.py:354
  3.8 3.1 %collective-permute-start.1 = (bf16[32,1024]{1,0:T(8,128)(2,1)S(1)}, bf16[32,1024]{1,0:T(8,128)(2,1)S(1)}, u32[]{:S(2)}, u32[]{:S(2)}) collective-permute-start(bf16[32,1024]{1,0:T(8,128)(2,1)S(1)} %get-tuple-element.46), channel_id=1, source_target_pairs={{0,48},{16,0},{32,16},{48,32},{1,49},{17,1},{33,17},{49,33},{2,50}... | collective-permute-start | bytes 196616 | tf_op jit(solution)/shard_map/ppermute | solution.py:354
  5.3 4.6 %collective-permute-start.2 = (bf16[32,1024]{1,0:T(8,128)(2,1)S(1)}, bf16[32,1024]{1,0:T(8,128)(2,1)S(1)}, u32[]{:S(2)}, u32[]{:S(2)}) collective-permute-start(bf16[32,1024]{1,0:T(8,128)(2,1)S(1)} %get-tuple-element.47), channel_id=1, source_target_pairs={{0,32},{16,48},{32,0},{48,16},{1,33},{17,49},{33,1},{49,17},{2,34}... | collective-permute-start | bytes 196616 | tf_op jit(solution)/shard_map/ppermute | solution.py:354
  9.9 26.6 %collective-permute-start.9 = (bf16[8,32,2048]{2,1,0:T(8,128)(2,1)}, bf16[8,32,2048]{2,1,0:T(8,128)(2,1)S(1)}, u32[]{:S(2)}, u32[]{:S(2)}) collective-permute-start(bf16[8,32,2048]{2,1,0:T(8,128)(2,1)} %bitcast.13), channel_id=1, source_target_pairs={{0,16},{16,32},{32,48},{48,0},{1,17},{17,33},{33,49},{49,1},{2,18}... | collective-permute-start | bytes 3145736 | tf_op jit(solution)/shard_map/ppermute | solution.py:356
  10.3 26.1 %collective-permute-start.10 = (bf16[8,32,2048]{2,1,0:T(8,128)(2,1)}, bf16[8,32,2048]{2,1,0:T(8,128)(2,1)S(1)}, u32[]{:S(2)}, u32[]{:S(2)}) collective-permute-start(bf16[8,32,2048]{2,1,0:T(8,128)(2,1)} %bitcast.14), channel_id=1, source_target_pairs={{0,48},{16,0},{32,16},{48,32},{1,49},{17,1},{33,17},{49,33},{2,50}... | collective-permute-start | bytes 3145736 | tf_op jit(solution)/shard_map/ppermute | solution.py:356
  12.7 33.1 %copy-start.11 = (bf16[256,2048]{1,0:T(8,128)(2,1)S(1)}, bf16[256,2048]{1,0:T(8,128)(2,1)}, u32[]{:S(2)}) copy-start(bf16[256,2048]{1,0:T(8,128)(2,1)} %param.10) | copy-start | bytes 3145732
  12.7 6.2 %collective-permute-start.3 = (bf16[1024,128]{1,0:T(8,128)(2,1)S(1)}, bf16[1024,128]{1,0:T(8,128)(2,1)S(1)}, u32[]{:S(2)}, u32[]{:S(2)}) collective-permute-start(bf16[1024,128]{1,0:T(8,128)(2,1)S(1)} %turn.1.refs_0_), channel_id=1, source_target_pairs={{0,1},{1,2},{2,3},{3,4},{4,5},{5,6},{6,7},{7,0},{8,9},{9,10},{10,1... | collective-permute-start | bytes 786440 | tf_op jit(solution)/shard_map/ppermute | solution.py:358
  15.7 6.7 %collective-permute-start.4 = (bf16[1024,128]{1,0:T(8,128)(2,1)S(1)}, bf16[1024,128]{1,0:T(8,128)(2,1)S(1)}, u32[]{:S(2)}, u32[]{:S(2)}) collective-permute-start(bf16[1024,128]{1,0:T(8,128)(2,1)S(1)} %turn.1.refs_0_), channel_id=1, source_target_pairs={{0,7},{1,0},{2,1},{3,2},{4,3},{5,4},{6,5},{7,6},{8,15},{9,8},{10,9... | collective-permute-start | bytes 786440 | tf_op jit(solution)/shard_map/ppermute | solution.py:358
  19.0 6.7 %collective-permute-start.5 = (bf16[1024,128]{1,0:T(8,128)(2,1)S(1)}, bf16[1024,128]{1,0:T(8,128)(2,1)S(1)}, u32[]{:S(2)}, u32[]{:S(2)}) collective-permute-start(bf16[1024,128]{1,0:T(8,128)(2,1)S(1)} %collective-permute-done.3.refs_1_), channel_id=1, source_target_pairs={{0,1},{1,2},{2,3},{3,4},{4,5},{5,6},{6,7},{7,0},{8,9},{9,10},{10,1... | collective-permute-start | bytes 786440 | tf_op jit(solution)/shard_map/ppermute | solution.py:360
  22.4 6.7 %collective-permute-start.6 = (bf16[1024,128]{1,0:T(8,128)(2,1)S(1)}, bf16[1024,128]{1,0:T(8,128)(2,1)S(1)}, u32[]{:S(2)}, u32[]{:S(2)}) collective-permute-start(bf16[1024,128]{1,0:T(8,128)(2,1)S(1)} %collective-permute-done.4.refs_2_), channel_id=1, source_target_pairs={{0,7},{1,0},{2,1},{3,2},{4,3},{5,4},{6,5},{7,6},{8,15},{9,8},{10,9... | collective-permute-start | bytes 786440 | tf_op jit(solution)/shard_map/ppermute | solution.py:360
  25.7 7.1 %collective-permute-start.7 = (bf16[1024,128]{1,0:T(8,128)(2,1)S(1)}, bf16[1024,128]{1,0:T(8,128)(2,1)S(1)}, u32[]{:S(2)}, u32[]{:S(2)}) collective-permute-start(bf16[1024,128]{1,0:T(8,128)(2,1)S(1)} %collective-permute-done.5.refs_3_), channel_id=1, source_target_pairs={{0,1},{1,2},{2,3},{3,4},{4,5},{5,6},{6,7},{7,0},{8,9},{9,10},{10,1... | collective-permute-start | bytes 786440 | tf_op jit(solution)/shard_map/ppermute | solution.py:362
  29.1 7.3 %collective-permute-start.8 = (bf16[1024,128]{1,0:T(8,128)(2,1)S(1)}, bf16[1024,128]{1,0:T(8,128)(2,1)S(1)}, u32[]{:S(2)}, u32[]{:S(2)}) collective-permute-start(bf16[1024,128]{1,0:T(8,128)(2,1)S(1)} %collective-permute-done.6.refs_4_), channel_id=1, source_target_pairs={{0,7},{1,0},{2,1},{3,2},{4,3},{5,4},{6,5},{7,6},{8,15},{9,8},{10,9... | collective-permute-start | bytes 786440 | tf_op jit(solution)/shard_map/ppermute | solution.py:362
  36.5 9.3 %collective-permute-start.13 = (bf16[8,32,1024]{2,1,0:T(8,128)(2,1)S(1)}, bf16[8,32,1024]{2,1,0:T(8,128)(2,1)S(1)}, u32[]{:S(2)}, u32[]{:S(2)}) collective-permute-start(bf16[8,32,1024]{2,1,0:T(8,128)(2,1)S(1)} %slice.14), channel_id=1, source_target_pairs={{0,16},{16,32},{32,48},{48,0},{1,17},{17,33},{33,49},{49,1},{2,18}... | collective-permute-start | bytes 1572872 | tf_op jit(solution)/shard_map/ppermute | solution.py:367
  36.6 20.3 %collective-permute-start.18 = (bf16[8,32,1024]{2,1,0:T(8,128)(2,1)S(1)}, bf16[8,32,1024]{2,1,0:T(8,128)(2,1)S(1)}, u32[]{:S(2)}, u32[]{:S(2)}) collective-permute-start(bf16[8,32,1024]{2,1,0:T(8,128)(2,1)S(1)} %slice.15), channel_id=1, source_target_pairs={{0,48},{16,0},{32,16},{48,32},{1,49},{17,1},{33,17},{49,33},{2,50}... | collective-permute-start | bytes 1572872 | tf_op jit(solution)/shard_map/ppermute | solution.py:368
  39.4 3.9 %collective-permute-start.11 = (bf16[512,128]{1,0:T(8,128)(2,1)S(1)}, bf16[512,128]{1,0:T(8,128)(2,1)S(1)}, u32[]{:S(2)}, u32[]{:S(2)}) collective-permute-start(bf16[512,128]{1,0:T(8,128)(2,1)S(1)} %slice.12), channel_id=1, source_target_pairs={{0,1},{1,2},{2,3},{3,4},{4,5},{5,6},{6,7},{7,0},{8,9},{9,10},{10,1... | collective-permute-start | bytes 393224 | tf_op jit(solution)/shard_map/ppermute | solution.py:371
  39.5 5.3 %collective-permute-start.12 = (bf16[512,128]{1,0:T(8,128)(2,1)S(1)}, bf16[512,128]{1,0:T(8,128)(2,1)S(1)}, u32[]{:S(2)}, u32[]{:S(2)}) collective-permute-start(bf16[512,128]{1,0:T(8,128)(2,1)S(1)} %slice.13), channel_id=1, source_target_pairs={{0,7},{1,0},{2,1},{3,2},{4,3},{5,4},{6,5},{7,6},{8,15},{9,8},{10,9... | collective-permute-start | bytes 393224 | tf_op jit(solution)/shard_map/ppermute | solution.py:372
  50.0 11.8 %collective-permute-start.14 = (bf16[4,64,16,128]{3,2,1,0:T(8,128)(2,1)S(1)}, bf16[4,64,16,128]{3,2,1,0:T(8,128)(2,1)S(1)}, u32[]{:S(2)}, u32[]{:S(2)}) collective-permute-start(bf16[4,64,16,128]{3,2,1,0:T(8,128)(2,1)S(1)} %get-tuple-element.58), channel_id=1, source_target_pairs={{0,8},{8,0},{1,9},{9,1},{2,10},{10,2},{3,11},{11,3},{4,12},{12,4},... | collective-permute-start | bytes 3145736 | tf_op jit(solution)/shard_map/ppermute | solution.py:378
  61.7 0.9 copy-start.8
  61.7 3.6 %copy-start.14 = (s32[1,128]{1,0:T(1,128)S(1)}, s32[1,128]{1,0:T(1,128)}, u32[]{:S(2)}) copy-start(s32[1,128]{1,0:T(1,128)} %param.11) | copy-start | bytes 1540
  61.7 7.5 %collective-permute-start.19 = (bf16[4,64,16,128]{3,2,1,0:T(8,128)(2,1)}, bf16[4,64,16,128]{3,2,1,0:T(8,128)(2,1)S(1)}, u32[]{:S(2)}, u32[]{:S(2)}) collective-permute-start(bf16[4,64,16,128]{3,2,1,0:T(8,128)(2,1)} %get-tuple-element.66), channel_id=1, source_target_pairs={{0,8},{8,0},{1,9},{9,1},{2,10},{10,2},{3,11},{11,3},{4,12},{12,4},... | collective-permute-start | bytes 3145736 | tf_op jit(solution)/shard_map/ppermute | solution.py:378
  62.6 0.7 copy-start.12
  63.3 0.7 copy-start.13
  64.0 8.9 %collective-permute-start.15 = (bf16[64,16,128]{2,1,0:T(8,128)(2,1)}, bf16[64,16,128]{2,1,0:T(8,128)(2,1)S(1)}, u32[]{:S(2)}, u32[]{:S(2)}) collective-permute-start(bf16[64,16,128]{2,1,0:T(8,128)(2,1)} %get-tuple-element.62), channel_id=1, source_target_pairs={{0,64},{64,128},{128,192},{192,0},{1,65},{65,129},{129,193},{193,1... | collective-permute-start | bytes 786440 | tf_op jit(solution)/shard_map/ppermute | solution.py:381
  65.5 14.3 %collective-permute-start.16 = (bf16[64,16,128]{2,1,0:T(8,128)(2,1)}, bf16[64,16,128]{2,1,0:T(8,128)(2,1)S(1)}, u32[]{:S(2)}, u32[]{:S(2)}) collective-permute-start(bf16[64,16,128]{2,1,0:T(8,128)(2,1)} %copy-done.13), channel_id=1, source_target_pairs={{0,128},{64,192},{128,0},{192,64},{1,129},{65,193},{129,1},{193,65... | collective-permute-start | bytes 786440 | tf_op jit(solution)/shard_map/ppermute | solution.py:381
  68.2 11.6 %collective-permute-start.17 = (bf16[64,16,128]{2,1,0:T(8,128)(2,1)}, bf16[64,16,128]{2,1,0:T(8,128)(2,1)S(1)}, u32[]{:S(2)}, u32[]{:S(2)}) collective-permute-start(bf16[64,16,128]{2,1,0:T(8,128)(2,1)} %copy-done.12), channel_id=1, source_target_pairs={{0,192},{64,0},{128,64},{192,128},{1,193},{65,1},{129,65},{193,129... | collective-permute-start | bytes 786440 | tf_op jit(solution)/shard_map/ppermute | solution.py:381
  69.3 1.0 copy-start.9
  70.4 14.1 %collective-permute-start.20 = (bf16[64,16,128]{2,1,0:T(8,128)(2,1)S(1)}, bf16[64,16,128]{2,1,0:T(8,128)(2,1)S(1)}, u32[]{:S(2)}, u32[]{:S(2)}) collective-permute-start(bf16[64,16,128]{2,1,0:T(8,128)(2,1)S(1)} %get-tuple-element.70), channel_id=1, source_target_pairs={{0,64},{64,128},{128,192},{192,0},{1,65},{65,129},{129,193},{193,1... | collective-permute-start | bytes 786440 | tf_op jit(solution)/shard_map/ppermute | solution.py:381
  70.9 20.1 %collective-permute-start.21 = (bf16[64,16,128]{2,1,0:T(8,128)(2,1)S(1)}, bf16[64,16,128]{2,1,0:T(8,128)(2,1)S(1)}, u32[]{:S(2)}, u32[]{:S(2)}) collective-permute-start(bf16[64,16,128]{2,1,0:T(8,128)(2,1)S(1)} %get-tuple-element.71), channel_id=1, source_target_pairs={{0,128},{64,192},{128,0},{192,64},{1,129},{65,193},{129,1},{193,65... | collective-permute-start | bytes 786440 | tf_op jit(solution)/shard_map/ppermute | solution.py:381
  73.0 18.0 %collective-permute-start.22 = (bf16[64,16,128]{2,1,0:T(8,128)(2,1)S(1)}, bf16[64,16,128]{2,1,0:T(8,128)(2,1)S(1)}, u32[]{:S(2)}, u32[]{:S(2)}) collective-permute-start(bf16[64,16,128]{2,1,0:T(8,128)(2,1)S(1)} %get-tuple-element.72), channel_id=1, source_target_pairs={{0,192},{64,0},{128,64},{192,128},{1,193},{65,1},{129,65},{193,129... | collective-permute-start | bytes 786440 | tf_op jit(solution)/shard_map/ppermute | solution.py:381
  91.0 19.4 %copy-start.4 = (bf16[1,5,256,256]{3,2,1,0:T(8,128)(2,1)S(1)}, bf16[1,5,256,256]{3,2,1,0:T(8,128)(2,1)}, u32[]{:S(2)}) copy-start(bf16[1,5,256,256]{3,2,1,0:T(8,128)(2,1)} %first.1) | copy-start | bytes 1966084
  91.0 19.4 %copy-start.5 = (bf16[1,5,256,256]{3,2,1,0:T(8,128)(2,1)S(1)}, bf16[1,5,256,256]{3,2,1,0:T(8,128)(2,1)}, u32[]{:S(2)}) copy-start(bf16[1,5,256,256]{3,2,1,0:T(8,128)(2,1)} %second.1) | copy-start | bytes 1966084
  91.9 18.5 %copy-start.2 = (bf16[1,5,256,256]{3,2,1,0:T(8,128)(2,1)S(1)}, bf16[1,5,256,256]{3,2,1,0:T(8,128)(2,1)}, u32[]{:S(2)}) copy-start(bf16[1,5,256,256]{3,2,1,0:T(8,128)(2,1)} %basis_left.1) | copy-start | bytes 1966084
  91.9 18.4 %copy-start.3 = (bf16[1,5,256,256]{3,2,1,0:T(8,128)(2,1)S(1)}, bf16[1,5,256,256]{3,2,1,0:T(8,128)(2,1)}, u32[]{:S(2)}) copy-start(bf16[1,5,256,256]{3,2,1,0:T(8,128)(2,1)} %basis_right.1) | copy-start | bytes 1966084
  114.4 18.1 %copy-start.6 = (bf16[5,256,256]{2,1,0:T(8,128)(2,1)}, bf16[5,256,256]{2,1,0:T(8,128)(2,1)S(1)}, u32[]{:S(2)}) copy-start(bf16[5,256,256]{2,1,0:T(8,128)(2,1)S(1)} %get-tuple-element.74.grads) | copy-start | bytes 1966084
  114.4 22.2 %copy-start.1 = (f32[1,5,256,256]{3,2,1,0:T(8,128)S(1)}, f32[1,5,256,256]{3,2,1,0:T(8,128)}, u32[]{:S(2)}) copy-start(f32[1,5,256,256]{3,2,1,0:T(8,128)} %right.1) | copy-start | bytes 3932164
  131.0 5.6 %copy-start = (f32[1,5,256,256]{3,2,1,0:T(8,128)S(1)}, f32[1,5,256,256]{3,2,1,0:T(8,128)}, u32[]{:S(2)}) copy-start(f32[1,5,256,256]{3,2,1,0:T(8,128)} %left.1) | copy-start | bytes 3932164
  132.5 15.8 %all-to-all-start.2 = ((bf16[32,4,16,128]{3,2,1,0:T(8,128)(2,1)}), bf16[32,4,16,128]{3,2,1,0:T(8,128)(2,1)S(1)}, u32[]{:S(2)}, u32[]{:S(2)}) async-start(bf16[32,4,16,128]{3,2,1,0:T(8,128)(2,1)} %bitcast.8), calls=%async_computation.2 | async-start | bytes 1048576 | tf_op jit(solution)/shard_map/all_to_all | solution.py:342
  136.6 1.1 copy-start.7
